TPU v7x, 32 devices: a whole 2x2x4 slice. The times are simulated.
32 devices in a mesh: wide: 8 (over z, x), narrow: 4 (over y, core).
Axes of the slice: x: 2, y: 2, z: 4, core: 2. Of those that a mesh axis runs over, the one named last changes fastest.
Arguments:
- inputs: bfloat16 [2, 32, 512, 768], P(None, ('wide', 'narrow')), may hold values from -6 to 6
- cotangent: bfloat16 [2, 32, 512, 768], P(None, ('wide', 'narrow')), may hold values from -6 to 6
- doc_ids: int32 [2, 32, 512], P(None, ('wide', 'narrow')), may hold values from 0 to 7, never falling along the last dimension, each value on 1 to 128 neighbouring positions
- attention_weights: float32 [4, 768, 768], P(None, ('wide', 'narrow'))
- attention_momentum: float32 [4, 768, 768], P(None, ('wide', 'narrow')), may hold values from -1024 to 1024
- attention_average: float32 [4, 768, 768], P(None, ('wide', 'narrow'))
- feedforward_weights: float32 [2, 768, 3072], P(None, ('wide', 'narrow'))
- feedforward_momentum: float32 [2, 768, 3072], P(None, ('wide', 'narrow')), may hold values from -1024 to 1024
- feedforward_average: float32 [2, 768, 3072], P(None, ('wide', 'narrow'))
- vector_weights: float32 [12, 768], P(None, ('wide', 'narrow'))
- vector_momentum: float32 [12, 768], P(None, ('wide', 'narrow')), may hold values from -1024 to 1024
- vector_average: float32 [12, 768], P(None, ('wide', 'narrow'))
Outputs:
- layer_out: bfloat16 [2, 32, 512, 768], P(None, ('wide', 'narrow'))
- input_grad: bfloat16 [2, 32, 512, 768], P(None, ('wide', 'narrow'))
- attention_next: float32 [4, 768, 768], P(None, ('wide', 'narrow'))
- attention_buffer: float32 [4, 768, 768], P(None, ('wide', 'narrow'))
- attention_trailing: float32 [4, 768, 768], P(None, ('wide', 'narrow'))
- attention_copy: bfloat16 [4, 768, 768], P(None, ('wide', 'narrow'))
- feedforward_next: float32 [2, 768, 3072], P(None, ('wide', 'narrow'))
- feedforward_buffer: float32 [2, 768, 3072], P(None, ('wide', 'narrow'))
- feedforward_trailing: float32 [2, 768, 3072], P(None, ('wide', 'narrow'))
- feedforward_copy: bfloat16 [2, 768, 3072], P(None, ('wide', 'narrow'))
- vector_next: float32 [12, 768], P(None, ('wide', 'narrow'))
- vector_buffer: float32 [12, 768], P(None, ('wide', 'narrow'))
- vector_trailing: float32 [12, 768], P(None, ('wide', 'narrow'))
- vector_copy: bfloat16 [12, 768], P(None, ('wide', 'narrow'))
Inputs may be any that keep to these rules, and one draw needn't show every extreme that they name: `doc_ids`: in each packed row the example number starts at 0, never falls, rises by at most one from a token to the next and ends at 7; an example has at most 128 tokens.
All inputs are finite; a program needn't handle non-finite values.
Results may differ from a plain program's by a relative error of at most 0.012.
The roundings to bfloat16 on the way count: a program that leaves them out, or rounds other values in their place, can miss the bound.
Values may be sent and summed in bfloat16 or wider, within the bound.
No kernel may reach another device: no remote copies, remote signals or barrier semaphores. Data moves between devices by JAX's collectives and lax.ppermute only.
A program may use at most 512 MiB of HBM per device.

v0:
```python
from functools import partial
import math

import jax
import jax.numpy as jnp
from jax import lax
from jax.sharding import PartitionSpec as P

D = 768
HEADS = 12
HEAD_DIM = 64
FF = 3072


EPSILON = 1e-12
SCALING = 0.125
MASKED = -1000000000.0
MOMENTUM = 0.5
DECAY = 0.5


def dot_last(left, right):
    return lax.dot_general(
        left, right, (((1,), (1,)), ((), ())), preferred_element_type=jnp.float32
    )


def dot_first(left, right):
    return lax.dot_general(
        left, right, (((0,), (0,)), ((), ())), preferred_element_type=jnp.float32
    )


def norm_forward(summed, gain_row, shift_row):
    average = jnp.mean(summed, axis=-1, keepdims=True)
    centered = summed - average
    inverse = lax.rsqrt(jnp.mean(centered * centered, axis=-1, keepdims=True) + EPSILON)
    normed = centered * inverse
    return (normed * gain_row + shift_row, normed, inverse)


def norm_backward(upstream, normed, inverse, gain_row):
    scaled = upstream * gain_row
    centered = scaled - jnp.mean(scaled, axis=-1, keepdims=True)
    grad_in = inverse * (centered - normed * jnp.mean(scaled * normed, axis=-1, keepdims=True))
    return (grad_in, jnp.sum(upstream * normed, axis=0), jnp.sum(upstream, axis=0))


def fetch_prefix(attention_weights, feedforward_weights, vector_weights, head_width, hidden_used):
    return (
        lax.all_gather(
            attention_weights[:, :, :head_width].astype(jnp.bfloat16),
            ("wide", "narrow"),
            axis=1,
            tiled=True,
        ),
        lax.all_gather(
            feedforward_weights[:, :, :hidden_used].astype(jnp.bfloat16),
            ("wide", "narrow"),
            axis=1,
            tiled=True,
        ),
        lax.all_gather(vector_weights.astype(jnp.bfloat16), ("wide", "narrow"), axis=1, tiled=True),
    )


def fetch_again(attention_weights, feedforward_weights, vector_weights, head_width, hidden_used):
    return (
        lax.all_gather(
            attention_weights[:, :, :head_width].astype(jnp.bfloat16),
            ("wide", "narrow"),
            axis=1,
            tiled=True,
        ),
        lax.all_gather(
            feedforward_weights[:, :, :hidden_used].astype(jnp.bfloat16),
            ("wide", "narrow"),
            axis=1,
            tiled=True,
        ),
        lax.all_gather(vector_weights.astype(jnp.bfloat16), ("wide", "narrow"), axis=1, tiled=True),
    )


def attention_scores(query_heads, key_heads, document_row):
    scores = (
        jnp.einsum("qhd,khd->hqk", query_heads, key_heads, preferred_element_type=jnp.float32)
        * SCALING
    )
    same_document = document_row[:, None] == document_row[None, :]
    return jnp.where(same_document[None], scores, MASKED)


def forward_pass(inputs_row, document_row, slabs, heads_used):
    attention_slab, feedforward_slab, vector_slab = slabs
    vector_float = vector_slab.astype(jnp.float32)
    blocks = FF // D
    length = inputs_row.shape[0]
    head_width = attention_slab.shape[2]
    hidden_used = feedforward_slab.shape[2]
    queries = (
        jnp.dot(inputs_row, attention_slab[0], preferred_element_type=jnp.float32)
        + vector_float[0, :head_width]
    ).astype(jnp.bfloat16)
    keys_all = jnp.dot(inputs_row, attention_slab[1], preferred_element_type=jnp.float32).astype(
        jnp.bfloat16
    )
    values_all = (
        jnp.dot(inputs_row, attention_slab[2], preferred_element_type=jnp.float32)
        + vector_float[1, :head_width]
    ).astype(jnp.bfloat16)
    query_heads = queries.reshape(length, heads_used, HEAD_DIM)
    key_heads = keys_all.reshape(length, heads_used, HEAD_DIM)
    value_heads = values_all.reshape(length, heads_used, HEAD_DIM)
    scores = attention_scores(query_heads, key_heads, document_row)
    row_peak = jnp.max(scores, axis=-1, keepdims=True)
    exponent = jnp.exp(scores - row_peak)
    exp_total = jnp.sum(exponent, axis=-1, keepdims=True)
    probability = exponent / exp_total
    log_total = row_peak + jnp.log(exp_total)
    attended = jnp.einsum(
        "hqk,khd->qhd",
        probability.astype(jnp.bfloat16),
        value_heads,
        preferred_element_type=jnp.float32,
    )
    attended = attended.reshape(length, head_width).astype(jnp.bfloat16)
    branch = dot_last(attended, attention_slab[3]) + vector_float[2]
    first_norm, normed_one, inverse_one = norm_forward(
        inputs_row.astype(jnp.float32) + branch, vector_float[blocks + 4], vector_float[blocks + 5]
    )
    first_low = first_norm.astype(jnp.bfloat16)
    hidden_bias = vector_float[3 : 3 + blocks].reshape(blocks * D)[:hidden_used]
    hidden_pre = (
        jnp.dot(first_low, feedforward_slab[0], preferred_element_type=jnp.float32) + hidden_bias
    )
    hidden = jax.nn.gelu(hidden_pre, approximate=False).astype(jnp.bfloat16)
    second = dot_last(hidden, feedforward_slab[1]) + vector_float[3 + blocks]
    output, normed_two, inverse_two = norm_forward(
        first_norm + second, vector_float[blocks + 6], vector_float[blocks + 7]
    )
    kept_state = (
        query_heads,
        key_heads,
        value_heads,
        log_total,
        attended,
        normed_one,
        inverse_one,
        first_low,
        hidden_pre,
        hidden,
        normed_two,
        inverse_two,
    )
    return (output, kept_state)


def backward_pass(inputs_row, document_row, cotangent_row, slabs, heads_used, kept_state):
    attention_slab, feedforward_slab, vector_slab = slabs
    (
        query_heads,
        key_heads,
        value_heads,
        log_total,
        attended,
        normed_one,
        inverse_one,
        first_low,
        hidden_pre,
        hidden,
        normed_two,
        inverse_two,
    ) = kept_state
    vector_float = vector_slab.astype(jnp.float32)
    blocks = FF // D
    length = inputs_row.shape[0]
    head_width = attention_slab.shape[2]
    hidden_used = feedforward_slab.shape[2]
    upstream = cotangent_row.astype(jnp.float32)
    grad_sum_two, grad_gain_two, grad_shift_two = norm_backward(
        upstream, normed_two, inverse_two, vector_float[blocks + 6]
    )
    grad_second = grad_sum_two.astype(jnp.bfloat16)
    grad_bias_two = jnp.sum(grad_second.astype(jnp.float32), axis=0)
    grad_down = dot_first(grad_second, hidden)
    grad_hidden = jnp.dot(grad_second, feedforward_slab[1], preferred_element_type=jnp.float32)
    ignored, gelu_back = jax.vjp(partial(jax.nn.gelu, approximate=False), hidden_pre)
    grad_pre = gelu_back(grad_hidden)[0].astype(jnp.bfloat16)
    grad_bias_one = jnp.sum(grad_pre.astype(jnp.float32), axis=0)
    grad_up = dot_first(first_low, grad_pre)
    grad_first = dot_last(grad_pre, feedforward_slab[0]) + grad_sum_two
    grad_sum_one, grad_gain_one, grad_shift_one = norm_backward(
        grad_first, normed_one, inverse_one, vector_float[blocks + 4]
    )
    grad_branch = grad_sum_one.astype(jnp.bfloat16)
    grad_bias_out = jnp.sum(grad_branch.astype(jnp.float32), axis=0)
    grad_out_proj = dot_first(grad_branch, attended)
    grad_attended = jnp.dot(
        grad_branch, attention_slab[3], preferred_element_type=jnp.float32
    ).astype(jnp.bfloat16)
    grad_heads = grad_attended.reshape(length, heads_used, HEAD_DIM)
    scores = attention_scores(query_heads, key_heads, document_row)
    probability = jnp.exp(scores - log_total)
    grad_values = jnp.einsum(
        "hqk,qhd->khd",
        probability.astype(jnp.bfloat16),
        grad_heads,
        preferred_element_type=jnp.float32,
    )
    grad_probability = jnp.einsum(
        "qhd,khd->hqk", grad_heads, value_heads, preferred_element_type=jnp.float32
    )
    row_inner = jnp.sum(probability * grad_probability, axis=-1, keepdims=True)
    grad_scores = (probability * (grad_probability - row_inner)).astype(jnp.bfloat16)
    grad_queries = (
        jnp.einsum("hqk,khd->qhd", grad_scores, key_heads, preferred_element_type=jnp.float32)
        * SCALING
    )
    grad_keys = (
        jnp.einsum("hqk,qhd->khd", grad_scores, query_heads, preferred_element_type=jnp.float32)
        * SCALING
    )
    grad_queries = grad_queries.reshape(length, head_width).astype(jnp.bfloat16)
    grad_keys = grad_keys.reshape(length, head_width).astype(jnp.bfloat16)
    grad_values = grad_values.reshape(length, head_width).astype(jnp.bfloat16)
    grad_input = (
        grad_sum_one
        + dot_last(grad_queries, attention_slab[0])
        + dot_last(grad_keys, attention_slab[1])
        + dot_last(grad_values, attention_slab[2])
    )
    grad_attention = jnp.stack(
        [
            dot_first(inputs_row, grad_queries),
            dot_first(inputs_row, grad_keys),
            dot_first(inputs_row, grad_values),
            grad_out_proj,
        ]
    )
    grad_feedforward = jnp.stack([grad_up, grad_down])
    pad_width = D - head_width
    bias_query = jnp.pad(jnp.sum(grad_queries.astype(jnp.float32), axis=0), (0, pad_width))
    bias_value = jnp.pad(jnp.sum(grad_values.astype(jnp.float32), axis=0), (0, pad_width))
    bias_hidden = jnp.pad(grad_bias_one, (0, blocks * D - hidden_used)).reshape(blocks, D)
    grad_vector = jnp.concatenate(
        [
            jnp.stack([bias_query, bias_value, grad_bias_out]),
            bias_hidden,
            jnp.stack(
                [grad_bias_two, grad_gain_one, grad_shift_one, grad_gain_two, grad_shift_two]
            ),
        ],
        axis=0,
    )
    return (grad_input, grad_attention, grad_feedforward, grad_vector)


def update(weights_now, momentum_now, average_now, gradient, rate):
    momentum_next = MOMENTUM * momentum_now + gradient
    weights_next = weights_now - rate * (gradient + MOMENTUM * momentum_next)
    average_next = DECAY * average_now + (1.0 - DECAY) * weights_next
    return (weights_next, momentum_next, average_next, weights_next.astype(jnp.bfloat16))


def body(
    inputs,
    cotangent,
    doc_ids,
    attention_weights,
    attention_momentum,
    attention_average,
    feedforward_weights,
    feedforward_momentum,
    feedforward_average,
    vector_weights,
    vector_momentum,
    vector_average,
):
    micro_count = inputs.shape[0]
    length = inputs.shape[2]
    vector_rows = vector_weights.shape[0]
    attention_total = jnp.zeros((4, D, D), jnp.float32)
    feedforward_total = jnp.zeros((2, D, FF), jnp.float32)
    vector_total = jnp.zeros((vector_rows, D), jnp.float32)
    outputs_list = []
    gradients_list = []
    for micro_index in range(micro_count):
        inputs_row = inputs[micro_index, 0]
        cotangent_row = cotangent[micro_index, 0]
        document_row = doc_ids[micro_index, 0]
        input_total = jnp.zeros((length, D), jnp.float32)
        for quarter in (4, 3, 2, 1):
            heads_used = HEADS * quarter // 4
            head_width = heads_used * HEAD_DIM
            hidden_used = FF * quarter // 4
            slabs = fetch_prefix(
                attention_weights, feedforward_weights, vector_weights, head_width, hidden_used
            )
            output, kept_state = forward_pass(inputs_row, document_row, slabs, heads_used)
            if quarter == 4:
                outputs_list.append(output.astype(jnp.bfloat16))
            back_slabs = fetch_again(
                attention_weights, feedforward_weights, vector_weights, head_width, hidden_used
            )
            grad_input, grad_attention, grad_feedforward, grad_vector = backward_pass(
                inputs_row, document_row, cotangent_row, back_slabs, heads_used, kept_state
            )
            input_total = input_total + grad_input
            attention_total = attention_total.at[:, :, :head_width].add(grad_attention)
            feedforward_total = feedforward_total.at[:, :, :hidden_used].add(grad_feedforward)
            vector_total = vector_total + grad_vector
        gradients_list.append(input_total.astype(jnp.bfloat16))
    reduced = (
        lax.psum_scatter(attention_total, ("wide", "narrow"), scatter_dimension=1, tiled=True),
        lax.psum_scatter(feedforward_total, ("wide", "narrow"), scatter_dimension=1, tiled=True),
        lax.psum_scatter(vector_total, ("wide", "narrow"), scatter_dimension=1, tiled=True),
    )
    layer_out = jnp.stack(outputs_list)[:, None]
    input_grad = jnp.stack(gradients_list)[:, None]
    token_count = micro_count * length * lax.axis_size("wide") * lax.axis_size("narrow")
    rate = 0.05 / math.sqrt(token_count)
    attention_out = update(
        attention_weights, attention_momentum, attention_average, reduced[0], rate
    )
    feedforward_out = update(
        feedforward_weights, feedforward_momentum, feedforward_average, reduced[1], rate
    )
    vector_out = update(vector_weights, vector_momentum, vector_average, reduced[2], rate)
    return (
        layer_out,
        input_grad,
        attention_out[0],
        attention_out[1],
        attention_out[2],
        attention_out[3],
        feedforward_out[0],
        feedforward_out[1],
        feedforward_out[2],
        feedforward_out[3],
        vector_out[0],
        vector_out[1],
        vector_out[2],
        vector_out[3],
    )


def solution(mesh):
    in_specs = (
        P(None, ("wide", "narrow"), None, None),
        P(None, ("wide", "narrow"), None, None),
        P(None, ("wide", "narrow"), None),
        P(None, ("wide", "narrow"), None),
        P(None, ("wide", "narrow"), None),
        P(None, ("wide", "narrow"), None),
        P(None, ("wide", "narrow"), None),
        P(None, ("wide", "narrow"), None),
        P(None, ("wide", "narrow"), None),
        P(None, ("wide", "narrow")),
        P(None, ("wide", "narrow")),
        P(None, ("wide", "narrow")),
    )
    out_specs = (
        P(None, ("wide", "narrow"), None, None),
        P(None, ("wide", "narrow"), None, None),
        P(None, ("wide", "narrow"), None),
        P(None, ("wide", "narrow"), None),
        P(None, ("wide", "narrow"), None),
        P(None, ("wide", "narrow"), None),
        P(None, ("wide", "narrow"), None),
        P(None, ("wide", "narrow"), None),
        P(None, ("wide", "narrow"), None),
        P(None, ("wide", "narrow"), None),
        P(None, ("wide", "narrow")),
        P(None, ("wide", "narrow")),
        P(None, ("wide", "narrow")),
        P(None, ("wide", "narrow")),
    )
    return jax.shard_map(body, mesh=mesh, in_specs=in_specs, out_specs=out_specs, check_vma=False)
```

profile of v0, /device:TPU:0, one launch (start us, length us, event | category | flops | bytes accessed | tf_op | source)
XLA Modules:
  0.0 1462.7 jit_solution(1390979345267800499)
XLA Ops:
  15.3 43.9 %all-gather = bf16[32,24,12]{1,2,0:T(8,128)(2,1)S(1)} all-gather(bf16[1,24,12]{1,2,0:T(8,128)(2,1)S(1)} %convert_bitcast_fusion.2), channel_id=1, replica_groups=mesh['wide'=8,'narrow'=4] {'wide','narrow'}, dimensions={0}, use_global_device_ids=true | all-gather | bytes 19008 | tf_op jit(solution)/shard_map/all_gather | solution.py:63
  81.9 45.5 %all-gather.24.cloned.1.call-done = bf16[2,768,768]{2,1,0:T(8,128)(2,1)} async-done(((bf16[2,24,768]{2,1,0:T(8,128)(2,1)}), bf16[2,768,768]{2,1,0:T(8,128)(2,1)}) %all-gather.24.cloned.1.call-update) | async-done | bytes 2359312 | tf_op jit(solution)/shard_map/all_gather | solution.py:57
  127.4 7.1 multiply_convert_fusion.14
  137.5 6.5 multiply_convert_fusion.17
  147.5 39.6 %all-gather.18.cloned.1.call-done = bf16[4,768,384]{2,1,0:T(8,128)(2,1)} async-done(((bf16[4,24,384]{2,1,0:T(8,128)(2,1)}), bf16[4,768,384]{2,1,0:T(8,128)(2,1)}) %all-gather.18.cloned.1.call-update) | async-done | bytes 2359312 | tf_op jit(solution)/shard_map/all_gather | solution.py:51
  206.4 44.5 %all-gather.14.cloned.1.call-done = bf16[4,768,576]{2,1,0:T(8,128)(2,1)} async-done(((bf16[4,24,576]{2,1,0:T(8,128)(2,1)}), bf16[4,768,576]{2,1,0:T(8,128)(2,1)}) %all-gather.14.cloned.1.call-update) | async-done | bytes 3538960 | tf_op jit(solution)/shard_map/all_gather | solution.py:51
  277.7 38.5 %all-gather.10.cloned.1.call-done = bf16[4,768,768]{2,1,0:T(8,128)(2,1)} async-done(((bf16[4,24,768]{2,1,0:T(8,128)(2,1)}), bf16[4,768,768]{2,1,0:T(8,128)(2,1)}) %all-gather.10.cloned.1.call-update) | async-done | bytes 4718608 | tf_op jit(solution)/shard_map/all_gather | solution.py:51
  372.0 9.9 all-gather.20.cloned.1.call-done
  381.9 11.4 multiply_convert_fusion.13
  396.2 10.5 multiply_convert_fusion.11
  416.2 40.7 %all-gather.16.cloned.1.call-done = bf16[2,768,2304]{2,1,0:T(8,128)(2,1)} async-done(((bf16[2,24,2304]{2,1,0:T(8,128)(2,1)}), bf16[2,768,2304]{2,1,0:T(8,128)(2,1)}) %all-gather.16.cloned.1.call-update) | async-done | bytes 7077904 | tf_op jit(solution)/shard_map/all_gather | solution.py:57
  456.9 15.6 %multiply_convert_fusion.9 = (bf16[512,2304]{1,0:T(8,128)(2,1)S(1)}, f32[512,2304]{1,0:T(8,128)}, f32[512,2304]{1,0:T(8,128)}) fusion(f32[2304]{0:T(1024)S(1)} %copy-done.376, bf16[2,768,2304]{2,1,0:T(8,128)(2,1)} %all-gather.16.cloned.1.call-done, f32[512,768]{1,0:T(8,128)S(1)} %copy-done.103, f32[512]{0:T(512)S(1)} %add_rsqrt_fusion.11, ...), kind=kOutput, calls=%fused_computation.148 | convolution fusion | flops 1891762176 | bytes 16929792 | tf_op jit(solution)/shard_map/dot_general | solution.py:135
  477.1 15.0 %multiply_convert_fusion.8 = (bf16[512,2304]{1,0:T(8,128)(2,1)S(1)}, f32[512,2304]{1,0:T(8,128)}, f32[512,2304]{1,0:T(8,128)}) fusion(f32[2304]{0:T(1024)S(1)} %copy-done.376, bf16[2,768,2304]{2,1,0:T(8,128)(2,1)S(1)} %copy-done.410, f32[512,768]{1,0:T(8,128)S(1)} %copy-done.209, f32[512]{0:T(512)S(1)} %copy-done.404, f32[512]{0:T(512)S(1)} %copy-done.378, ...), kind=kOutput, calls=%fused_computation.133 | convolution fusion | flops 1891762176 | bytes 16930816 | tf_op jit(solution)/shard_map/dot_general | solution.py:135
  495.4 45.6 %all-gather.12.cloned.1.call-done = bf16[2,768,3072]{2,1,0:T(8,128)(2,1)} async-done(((bf16[2,24,3072]{2,1,0:T(8,128)(2,1)}), bf16[2,768,3072]{2,1,0:T(8,128)(2,1)}) %all-gather.12.cloned.1.call-update) | async-done | bytes 9437200 | tf_op jit(solution)/shard_map/all_gather | solution.py:57
  546.5 32.5 %multiply_convert_fusion.7 = (bf16[512,3072]{1,0:T(8,128)(2,1)S(1)}, f32[512,3072]{1,0:T(8,128)}, bf16[512,3072]{1,0:T(8,128)(2,1)S(1)}, f32[512,3072]{1,0:T(8,128)}, f32[512,3072]{1,0:T(8,128)}) fusion(f32[3072]{0:T(1024)S(1)} %copy-done.375, f32[512,3072]{1,0:T(8,128)S(1)} %fusion.80, bf16[2,768,3072]{2,1,0:T(8,128)(2,1)S(1)} %copy-done.409, ...), kind=kOutput, calls=%fused_computation.84 | convolution fusion | flops 2625503232 | bytes 37771264 | tf_op jit(solution)/shard_map/dot_general | solution.py:135
  605.8 10.1 convert_reduce_fusion
  615.9 6.1 fusion.183
  622.0 7.2 convert_reduce_fusion.2
  629.2 6.0 fusion.181
  635.3 11.0 convert_reduce_fusion.1
  646.3 9.0 multiply_reduce_fusion.15
  655.4 6.3 convert_reduce_fusion.4
  671.6 7.3 convert_reduce_fusion.3
  679.0 7.6 multiply_reduce_fusion.14
  707.6 14.1 multiply_reduce_fusion.1
  721.8 8.5 convert_reduce_fusion.28
  762.4 10.5 multiply_reduce_fusion
  772.9 9.6 convert_reduce_fusion.17
  808.4 6.4 convolution_bitcast_fusion.7
  820.2 6.0 convolution_bitcast_fusion.3
  844.9 6.4 convolution_bitcast_fusion.5
  873.4 7.2 multiply_convert_fusion.1
  888.3 11.2 multiply_convert_fusion.3
  912.8 6.4 multiply_convert_fusion.5
  932.7 7.1 multiply_convert_fusion
  947.5 11.2 multiply_convert_fusion.2
  1027.6 6.0 constant_dynamic-update-slice_fusion.5
  1038.4 12.1 copy.226
  1050.6 8.3 pad_maximum_fusion
  1059.0 16.3 %constant_dynamic-update-slice_fusion.3 = (f32[2,768,3072]{2,1,0:T(8,128)S(1)}, f32[2,768,2304]{2,1,0:T(8,128)}) fusion(f32[2,768,3072]{2,1,0:T(8,128)S(1)} %pad_maximum_fusion, f32[1,768,2304]{2,1,0:T(8,128)} %convolution_bitcast_fusion.2, f32[1,768,2304]{2,1,0:T(8,128)} %convolution_bitcast_fusion.3, f32[1,768,3072]{2,1,0:T(8,128)} %convolution_bitcast_fusion.6, ...), kind=kLoop, calls=%fused_computation.745 | loop fusion | flops 10616832 | bytes 61341696 | tf_op jit(solution)/shard_map/scatter-add | solution.py:311
  1075.3 11.4 constant_dynamic-update-slice_fusion.2
  1091.2 11.5 maximum_add_fusion
  1108.8 12.0 constant_dynamic-update-slice_fusion.1
  1120.9 6.9 constant_dynamic-update-slice_fusion
  1156.7 40.2 %all-reduce.19 = f32[12,768]{1,0:T(8,128)S(1)} all-reduce(f32[12,768]{1,0:T(8,128)S(1)} %add_add_fusion.8), channel_id=4, replica_groups=mesh['wide'=8,'narrow'=4] {'wide','narrow'}, use_global_device_ids=true, to_apply=%region_150.151.clone | all-reduce | flops 9216 | bytes 73728
  1232.5 7.8 fusion.216
  1240.3 5.9 fusion.217
  1255.3 197.2 %reduce-scatter.3.cloned.1.call-done = f32[2,24,3072]{2,1,0:T(8,128)} async-done(((f32[2,768,3072]{2,1,0:T(8,128)}), f32[2,24,3072]{2,1,0:T(8,128)}) %reduce-scatter.3.cloned.1.call-update) | async-done | bytes 589840 | tf_op jit(solution)/shard_map/reduce_scatter | solution.py:316
  (1380 shorter events, 525.0 us)
Async XLA Ops:
  7.2 53.2 %copy-start.403 = (s32[2,1,512]{2,1,0:T(1,128)S(1)}, s32[2,1,512]{2,1,0:T(1,128)}, u32[]{:S(2)}) copy-start(s32[2,1,512]{2,1,0:T(1,128)} %param.54) | copy-start | bytes 12292
  7.2 59.9 %all-gather.22.cloned.1.call-start = ((), (), s32[]{:S(2)}) async-start(), calls=%async_computation.7 | async-start | bytes 1622016 | tf_op jit(solution)/shard_map/all_gather | solution.py:51
  8.9 58.2 %copy-start = (bf16[2,1,512,768]{3,2,1,0:T(8,128)(2,1)S(1)}, bf16[2,1,512,768]{3,2,1,0:T(8,128)(2,1)}, u32[]{:S(2)}) copy-start(bf16[2,1,512,768]{3,2,1,0:T(8,128)(2,1)} %param.52) | copy-start | bytes 4718596
  8.9 118.5 %all-gather.24.cloned.1.call-start = ((), (), s32[]{:S(2)}) async-start(), calls=%async_computation.8 | async-start | bytes 2433024 | tf_op jit(solution)/shard_map/all_gather | solution.py:57
  10.9 176.2 %all-gather.18.cloned.1.call-start = ((), (), s32[]{:S(2)}) async-start(), calls=%async_computation.5 | async-start | bytes 2433024 | tf_op jit(solution)/shard_map/all_gather | solution.py:51
  11.7 239.2 %all-gather.14.cloned.1.call-start = ((), (), s32[]{:S(2)}) async-start(), calls=%async_computation.3 | async-start | bytes 4055040 | tf_op jit(solution)/shard_map/all_gather | solution.py:51
  12.4 303.7 %all-gather.10.cloned.1.call-start = ((), (), s32[]{:S(2)}) async-start(), calls=%async_computation.1 | async-start | bytes 4866048 | tf_op jit(solution)/shard_map/all_gather | solution.py:51
  13.0 368.9 %all-gather.20.cloned.1.call-start = ((), (), s32[]{:S(2)}) async-start(), calls=%async_computation.6 | async-start | bytes 4866048 | tf_op jit(solution)/shard_map/all_gather | solution.py:57
  13.7 443.1 %all-gather.16.cloned.1.call-start = ((), (), s32[]{:S(2)}) async-start(), calls=%async_computation.4 | async-start | bytes 7299072 | tf_op jit(solution)/shard_map/all_gather | solution.py:57
  14.5 526.5 %all-gather.12.cloned.1.call-start = ((), (), s32[]{:S(2)}) async-start(), calls=%async_computation.2 | async-start | bytes 9732096 | tf_op jit(solution)/shard_map/all_gather | solution.py:57
  15.3 1235.6 %all-reduce.22.cloned.1.call-start = ((), (), s32[]{:S(2)}) async-start(), calls=%async_computation.10 | async-start | bytes 18874368
  60.3 83.7 %copy-start.401 = (f32[768]{0:T(1024)}, f32[768]{0:T(1024)S(1)}, u32[]{:S(2)}) copy-start(f32[768]{0:T(1024)S(1)} %get-tuple-element.363) | copy-start | bytes 9220
  60.6 274.5 %copy-start.35 = (pred[512,512]{0,1:T(8,128)(4,1)}, pred[512,512]{0,1:T(8,128)(4,1)S(1)}, u32[]{:S(2)}) copy-start(pred[512,512]{0,1:T(8,128)(4,1)S(1)} %broadcast_compare_fusion) | copy-start | bytes 786436
  75.0 59.5 %copy-start.32 = (f32[512,768]{1,0:T(8,128)}, f32[512,768]{1,0:T(8,128)S(1)}, u32[]{:S(2)}) copy-start(f32[512,768]{1,0:T(8,128)S(1)} %get-tuple-element.519) | copy-start | bytes 4718596
  75.2 59.3 %copy-start.295 = (f32[512]{0:T(512)}, f32[512]{0:T(512)S(1)}, u32[]{:S(2)}) copy-start(f32[512]{0:T(512)S(1)} %broadcast_multiply_fusion.4) | copy-start | bytes 6148
  75.5 59.0 %copy-start.320 = (f32[512]{0:T(512)}, f32[512]{0:T(512)S(1)}, u32[]{:S(2)}) copy-start(f32[512]{0:T(512)S(1)} %add_rsqrt_fusion.1) | copy-start | bytes 6148
  80.3 63.7 %copy-start.323 = (f32[512]{0:T(512)}, f32[512]{0:T(512)S(1)}, u32[]{:S(2)}) copy-start(f32[512]{0:T(512)S(1)} %broadcast_multiply_fusion.23) | copy-start | bytes 6148
  81.9 62.1 %copy-start.381 = (f32[512]{0:T(512)}, f32[512]{0:T(512)S(1)}, u32[]{:S(2)}) copy-start(f32[512]{0:T(512)S(1)} %add_rsqrt_fusion.7) | copy-start | bytes 6148
  145.7 44.7 %copy-start.301 = (f32[512]{0:T(512)}, f32[512]{0:T(512)S(1)}, u32[]{:S(2)}) copy-start(f32[512]{0:T(512)S(1)} %broadcast_multiply_fusion.22) | copy-start | bytes 6148
  147.5 43.0 %copy-start.38 = (pred[512,512]{0,1:T(8,128)(4,1)S(1)}, pred[512,512]{0,1:T(8,128)(4,1)}, u32[]{:S(2)}) copy-start(pred[512,512]{0,1:T(8,128)(4,1)} %broadcast_compare_fusion.1) | copy-start | bytes 786436
  197.7 195.7 %copy-start.329 = (f32[512]{0:T(512)}, f32[512]{0:T(512)S(1)}, u32[]{:S(2)}) copy-start(f32[512]{0:T(512)S(1)} %broadcast_multiply_fusion.28) | copy-start | bytes 6148
  198.0 195.4 %copy-start.384 = (f32[512]{0:T(512)}, f32[512]{0:T(512)S(1)}, u32[]{:S(2)}) copy-start(f32[512]{0:T(512)S(1)} %add_rsqrt_fusion.9) | copy-start | bytes 6148
  204.9 201.8 %copy-start.298 = (f32[512]{0:T(512)}, f32[512]{0:T(512)S(1)}, u32[]{:S(2)}) copy-start(f32[512]{0:T(512)S(1)} %broadcast_multiply_fusion.9) | copy-start | bytes 6148
  206.4 200.4 %copy-start.326 = (f32[512]{0:T(512)}, f32[512]{0:T(512)S(1)}, u32[]{:S(2)}) copy-start(f32[512]{0:T(512)S(1)} %add_rsqrt_fusion.3) | copy-start | bytes 6148
  265.4 207.1 %copy-start.332 = (f32[512]{0:T(512)}, f32[512]{0:T(512)S(1)}, u32[]{:S(2)}) copy-start(f32[512]{0:T(512)S(1)} %broadcast_multiply_fusion.33) | copy-start | bytes 6148
  265.8 206.8 %copy-start.387 = (f32[512]{0:T(512)}, f32[512]{0:T(512)S(1)}, u32[]{:S(2)}) copy-start(f32[512]{0:T(512)S(1)} %add_rsqrt_fusion.11) | copy-start | bytes 6148
  275.6 42.6 %copy-start.377 = (f32[512]{0:T(512)}, f32[512]{0:T(512)S(1)}, u32[]{:S(2)}) copy-start(f32[512]{0:T(512)S(1)} %broadcast_multiply_fusion.14) | copy-start | bytes 6148
  409.7 269.3 %copy-start.407 = (f32[512]{0:T(512)}, f32[512]{0:T(512)S(1)}, u32[]{:S(2)}) copy-start(f32[512]{0:T(512)S(1)} %add_rsqrt_fusion.13) | copy-start | bytes 6148
  409.7 257.6 %copy-start.393 = (f32[512]{0:T(512)}, f32[512]{0:T(512)S(1)}, u32[]{:S(2)}) copy-start(f32[512]{0:T(512)S(1)} %add_rsqrt_fusion.15) | copy-start | bytes 6148
  411.3 45.6 %copy-start.103 = (f32[512,768]{1,0:T(8,128)S(1)}, f32[512,768]{1,0:T(8,128)}, u32[]{:S(2)}) copy-start(f32[512,768]{1,0:T(8,128)} %copy-done.102) | copy-start | bytes 4718596
  411.3 45.6 %copy-start.376 = (f32[2304]{0:T(1024)S(1)}, f32[2304]{0:T(1024)}, u32[]{:S(2)}) copy-start(f32[2304]{0:T(1024)} %add.978) | copy-start | bytes 27652
  492.1 48.9 %copy-start.391 = (f32[512]{0:T(512)S(1)}, f32[512]{0:T(512)}, u32[]{:S(2)}) copy-start(f32[512]{0:T(512)} %copy-done.390) | copy-start | bytes 6148
  495.4 50.9 %copy-start.118 = (f32[512,768]{1,0:T(8,128)S(1)}, f32[512,768]{1,0:T(8,128)}, u32[]{:S(2)}) copy-start(f32[512,768]{1,0:T(8,128)} %copy-done.117) | copy-start | bytes 4718596
  495.4 50.9 %copy-start.336 = (f32[512]{0:T(512)S(1)}, f32[512]{0:T(512)}, u32[]{:S(2)}) copy-start(f32[512]{0:T(512)} %copy-done.335) | copy-start | bytes 6148
  495.4 50.9 %copy-start.375 = (f32[3072]{0:T(1024)S(1)}, f32[3072]{0:T(1024)}, u32[]{:S(2)}) copy-start(f32[3072]{0:T(1024)} %add.941) | copy-start | bytes 36868
  596.9 64.9 %copy-start.111 = (f32[512,768]{1,0:T(8,128)}, f32[512,768]{1,0:T(8,128)S(1)}, u32[]{:S(2)}) copy-start(f32[512,768]{1,0:T(8,128)S(1)} %get-tuple-element.454) | copy-start | bytes 4718596
  596.9 70.4 %copy-start.70 = (f32[512,768]{1,0:T(8,128)}, f32[512,768]{1,0:T(8,128)S(1)}, u32[]{:S(2)}) copy-start(f32[512,768]{1,0:T(8,128)S(1)} %get-tuple-element.452) | copy-start | bytes 4718596
  600.2 46.1 %copy-start.93 = (f32[512,768]{1,0:T(8,128)}, f32[512,768]{1,0:T(8,128)S(1)}, u32[]{:S(2)}) copy-start(f32[512,768]{1,0:T(8,128)S(1)} %get-tuple-element.446) | copy-start | bytes 4718596
  600.2 78.7 %copy-start.115 = (f32[512,768]{1,0:T(8,128)}, f32[512,768]{1,0:T(8,128)S(1)}, u32[]{:S(2)}) copy-start(f32[512,768]{1,0:T(8,128)S(1)} %get-tuple-element.448) | copy-start | bytes 4718596
  690.6 102.6 %copy-start.20 = (f32[512,768]{1,0:T(8,128)}, f32[512,768]{1,0:T(8,128)S(1)}, u32[]{:S(2)}) copy-start(f32[512,768]{1,0:T(8,128)S(1)} %get-tuple-element.486) | copy-start | bytes 4718596
  1050.6 402.0 %reduce-scatter.3.cloned.1.call-start = ((), (), s32[]{:S(2)}) async-start(), calls=%async_computation.9 | async-start | bytes 19464192 | tf_op jit(solution)/shard_map/reduce_scatter | solution.py:316
  1133.6 63.4 %copy-start.78 = (bf16[4,768,192]{2,1,0:T(8,128)(2,1)S(1)}, bf16[4,768,192]{2,1,0:T(8,128)(2,1)}, u32[]{:S(2)}) copy-start(bf16[4,768,192]{2,1,0:T(8,128)(2,1)} %all-gather.22.cloned.1.call-done) | copy-start | bytes 3538948
  1133.6 63.4 %copy-start.193 = (bf16[3,64,512]{2,1,0:T(8,128)(2,1)S(1)}, bf16[3,64,512]{2,1,0:T(8,128)(2,1)}, u32[]{:S(2)}) copy-start(bf16[3,64,512]{2,1,0:T(8,128)(2,1)} %get-tuple-element.595) | copy-start | bytes 589828
  1134.8 62.5 %copy-start.197 = (bf16[3,64,512]{2,1,0:T(8,128)(2,1)S(1)}, bf16[3,64,512]{2,1,0:T(8,128)(2,1)}, u32[]{:S(2)}) copy-start(bf16[3,64,512]{2,1,0:T(8,128)(2,1)} %fusion.235) | copy-start | bytes 589828
  1249.5 203.0 %copy-start.174 = (f32[2,24,3072]{2,1,0:T(8,128)S(1)}, f32[2,24,3072]{2,1,0:T(8,128)}, u32[]{:S(2)}) copy-start(f32[2,24,3072]{2,1,0:T(8,128)} %param.58) | copy-start | bytes 1769476
  1249.5 203.0 %copy-start.252 = (f32[2,24,3072]{2,1,0:T(8,128)S(1)}, f32[2,24,3072]{2,1,0:T(8,128)}, u32[]{:S(2)}) copy-start(f32[2,24,3072]{2,1,0:T(8,128)} %param.59) | copy-start | bytes 1769476
  1250.2 204.4 %copy-start.314 = (f32[12,24]{1,0:T(8,128)}, f32[12,24]{1,0:T(8,128)S(1)}, u32[]{:S(2)}) copy-start(f32[12,24]{1,0:T(8,128)S(1)} %get-tuple-element.370) | copy-start | bytes 3460
  1253.1 201.6 %copy-start.253 = (f32[2,24,3072]{2,1,0:T(8,128)S(1)}, f32[2,24,3072]{2,1,0:T(8,128)}, u32[]{:S(2)}) copy-start(f32[2,24,3072]{2,1,0:T(8,128)} %param.60) | copy-start | bytes 1769476
  (423 other events, 2557.3 us)
Sparse Core Ops, SparseCore 0:
  11.5 55.5 all-gather.21
  70.6 56.8 all-gather.23
  130.9 56.1 all-gather.17
  190.5 60.3 all-gather.13
  253.6 62.5 all-gather.9
  319.4 62.4 all-gather.19
  385.3 71.4 all-gather.15
  460.3 80.6 all-gather.11
  1050.7 189.3 all-reduce.21
  1247.4 205.0 reduce-scatter.2
where the time goes:
time: 1470 us; the launch traced here: 1460 us
  matrix products  589 us (40%)
  waiting for transfers between devices  467 us (32%)
  other arithmetic  209 us (14%)
  local copies, waits for them, and re-layouts  94.1 us (6%)
  blocking collectives  84.1 us (6%)
  between operations  19.7 us (1%)
    reduce_scatter x1, waiting for transfers between devices, body(): lax.psum_scatter(feedforward_total, ('wide', 'narrow'), scatter_dimension...  197 us
    all_gather x4, waiting for transfers between devices, fetch_prefix(): lax.all_gather(feedforward_weights[:, :, :hidden_used].astype(jnp.bfloat1...  142 us
    all_gather x4, waiting for transfers between devices, fetch_prefix(): lax.all_gather(attention_weights[:, :, :head_width].astype(jnp.bfloat16),...  126 us
    dot_general x48, matrix products, dot_last(): lax.dot_general(left, right, (((1,), (1,)), ((), ())), preferred_element_...  119 us
    dot_general x48, matrix products, dot_first(): lax.dot_general(left, right, (((0,), (0,)), ((), ())), preferred_element_...  111 us
    dot_general x8, matrix products, forward_pass(): jnp.dot(first_low, feedforward_slab[0], preferred_element_type=jnp.float32)  104 us
    scatter-add x6, other arithmetic, body(): feedforward_total.at[:, :, :hidden_used].add(grad_feedforward)  56.6 us
    convert_element_type x8, other arithmetic, backward_pass(): (probability * (grad_probability - row_inner)).astype(jnp.bfloat16)  51.7 us
  transfers between devices with their start and end apart: 10, of which 9 were waited for; matrix products, arithmetic and copies ran while one was open for 24% of the time, Pallas kernels for 0%

commit v1 on v0

v1 whole, which is shorter than its diff:
```python
from functools import partial
import math

import jax
import jax.numpy as jnp
from jax import lax
from jax.experimental import pallas as pl
from jax.experimental.pallas import tpu as pltpu
from jax.sharding import PartitionSpec as P

D = 768
HEADS = 12
HEAD_DIM = 64
FF = 3072
SLICES = FF // D
PAIRS = HEADS // 2
HALF = 256
WINDOW = 384

EPSILON = 1e-12
SCALING = 0.125
MASKED = -1000000000.0
MOMENTUM = 0.5
DECAY = 0.5
BF = jnp.bfloat16
F32 = jnp.float32

VMEM_LIMIT = 60 * 1024 * 1024


def dot(left, right):
    return lax.dot_general(left, right, (((1,), (0,)), ((), ())), preferred_element_type=F32)


def dot_last(left, right):
    return lax.dot_general(left, right, (((1,), (1,)), ((), ())), preferred_element_type=F32)


def dot_first(left, right):
    return lax.dot_general(left, right, (((0,), (0,)), ((), ())), preferred_element_type=F32)


def whole(shape):
    zeros = (0,) * len(shape)
    return pl.BlockSpec(shape, lambda *_: zeros, pipeline_mode=pl.Buffered(1))


def params():
    return pltpu.CompilerParams(vmem_limit_bytes=VMEM_LIMIT)


PIECES = 8
UNITS = 16
UNIT = D // UNITS
OWN = UNIT // 2
HALF_D = D // 2
NARROW = 128


def load(pieces, place_ref, moves, semaphore):
    for own in (True, False):
        for turn in range(4):
            piece = pieces[turn if own else 4 + turn]
            for index in range(4):
                start = pl.multiple_of(place_ref[4 * turn + index] * UNIT, UNIT)
                for lane, lanes, target in moves:
                    pltpu.make_async_copy(
                        piece.at[index, :, lane : lane + lanes],
                        target(own).at[pl.ds(start, UNIT), :],
                        semaphore,
                    ).start()


def all_arrived(ref, semaphore):
    pltpu.make_async_copy(ref, ref, semaphore).wait()


def cost(flops, size):
    return pl.CostEstimate(flops=int(flops), bytes_accessed=int(size), transcendentals=0)


def attention_forward_kernel(place_ref, x_ref, column_ref, row_ref, *refs):
    pieces, refs = refs[:PIECES], refs[PIECES:]
    q_ref, k_ref, v_ref, o_ref, p_ref, weights_ref, vector_ref, table_ref, semaphore = refs

    @pl.when(pl.program_id(0) == 0)
    def _():
        core = place_ref[UNITS]

        def half(own):
            which = core if own else 1 - core
            return weights_ref.at[1, :, pl.ds(pl.multiple_of(HALF_D * which, NARROW), HALF_D)]

        load(
            pieces,
            place_ref,
            (
                (0, D, lambda own: weights_ref.at[2 * (core if own else 1 - core)]),
                (D, HALF_D, half),
            ),
            semaphore.at[0],
        )
        for turn in range(4):
            pltpu.make_async_copy(
                pieces[turn].at[:, :, D + HALF_D : D + HALF_D + NARROW],
                table_ref.at[pl.ds(4 * turn, 4)],
                semaphore.at[1],
            ).start()
        all_arrived(table_ref, semaphore.at[1])
        vector = jnp.zeros((16, D), F32)
        for slot in range(UNITS):
            unit = table_ref[slot].astype(F32)
            for one in range(2):
                part = unit[OWN * one : OWN * one + 16]
                wide = jnp.concatenate([part, jnp.zeros((16, D - NARROW), F32)], axis=1)
                vector = vector + pltpu.roll(wide, UNIT * place_ref[slot] + OWN * one, 1)
        vector_ref[...] = vector
        all_arrived(weights_ref, semaphore.at[0])

    rows = x_ref[0]
    queries = (dot(rows, weights_ref[0]) + vector_ref[0:1, :]).astype(BF)
    q_ref[0] = queries * jnp.asarray(SCALING, BF)
    k_ref[0] = dot(rows, weights_ref[1]).astype(BF)
    v_ref[0] = (dot(rows, weights_ref[2]) + vector_ref[1:2, :]).astype(BF)
    length = rows.shape[0]
    lane = lax.broadcasted_iota(jnp.int32, (length, 128), 1)
    masks = [
        column_ref[0, HALF * part : HALF * (part + 1), :]
        == row_ref[0, :, 128 * part : 128 * part + WINDOW]
        for part in range(2)
    ]
    for pair in range(PAIRS):
        cols = slice(128 * pair, 128 * (pair + 1))
        q_pair = q_ref[0, :, cols]
        k_pair = k_ref[0, :, cols]
        v_pair = v_ref[0, :, cols]
        results = []
        for side in range(2):
            q_one = jnp.where((lane >= 64) == bool(side), q_pair, jnp.zeros_like(q_pair))
            parts = []
            for part in range(2):
                window = slice(128 * part, 128 * part + WINDOW)
                scores = dot_last(q_one[HALF * part : HALF * (part + 1)], k_pair[window])
                scores = jnp.where(masks[part], scores, MASKED)
                peak = jnp.max(scores, axis=-1, keepdims=True)
                exponent = jnp.exp(scores - peak)
                total = jnp.sum(exponent, axis=-1, keepdims=True)
                low = (exponent * (1.0 / total)).astype(BF)
                p_ref[0, 2 * pair + side, part] = low
                parts.append(dot(low, v_pair[window]))
            results.append(jnp.concatenate(parts, axis=0))
        o_ref[0, :, cols] = jnp.where(lane >= 64, results[1], results[0]).astype(BF)


def attention_forward(inputs, documents, place, pieces):
    micro, length, _ = inputs.shape
    block = pl.BlockSpec((1, length, D), lambda i: (i, 0, 0))
    shape = jax.ShapeDtypeStruct((micro, length, D), BF)
    return pl.pallas_call(
        attention_forward_kernel,
        grid=(micro,),
        in_specs=[
            pl.BlockSpec(memory_space=pltpu.SMEM),
            block,
            pl.BlockSpec((1, length, 1), lambda i: (i, 0, 0)),
            pl.BlockSpec((1, 1, length), lambda i: (i, 0, 0)),
        ]
        + [pl.BlockSpec(memory_space=pl.ANY)] * PIECES,
        out_specs=[block] * 4
        + [
            pl.BlockSpec((1, HEADS, 2, HALF, WINDOW), lambda i: (i, 0, 0, 0, 0)),
            whole((3, D, D)),
            whole((16, D)),
        ],
        out_shape=[shape] * 4
        + [
            jax.ShapeDtypeStruct((micro, HEADS, 2, HALF, WINDOW), BF),
            jax.ShapeDtypeStruct((3, D, D), BF),
            jax.ShapeDtypeStruct((16, D), F32),
        ],
        scratch_shapes=[pltpu.VMEM((UNITS, UNIT, NARROW), BF), pltpu.SemaphoreType.DMA((2,))],
        cost_estimate=cost(18e9, 20e6),
        compiler_params=params(),
        name="attention_forward",
    )(place, inputs, documents[:, :, None], documents[:, None, :], *pieces)


def gelu_terms(pre):
    size = jnp.abs(pre)
    scale = 1.0 / (1.0 + 0.23164188 * size)
    bell = jnp.exp(pre * pre * -0.5)
    tail = scale * (
        0.127414796
        + scale * (-0.142248368 + scale * (0.7107068705 + scale * (-0.7265760135 + scale * 0.5307027145)))
    )
    tail = tail * bell
    below = jnp.where(pre < 0.0, tail, 1.0 - tail)
    return pre * below, below + pre * bell * 0.3989422804014327


def mean_of(value):
    return jnp.sum(value, axis=-1, keepdims=True) * (1.0 / D)


def norm_forward(summed):
    centered = summed - mean_of(summed)
    inverse = lax.rsqrt(mean_of(centered * centered) + EPSILON)
    return centered * inverse, inverse


def norm_backward(scaled, normed, inverse):
    return inverse * (scaled - mean_of(scaled) - normed * mean_of(scaled * normed))


def ffn_kernel(quarter, first, layout, *refs):
    refs = list(refs)
    place_ref, x_ref, o_ref, cotangent_ref, vector_ref = refs[:5]
    refs = refs[5:]
    if not first:
        wo_ref, refs = refs[0], refs[1:]
    chunks, refs = refs[: PIECES * len(layout)], refs[PIECES * len(layout) :]
    if not first:
        before_ref, vg_before_ref = refs[:2]
        refs = refs[2:]
    x1_ref, dm_ref, g_ref, du_ref, da_ref, dh1_ref, vg_ref = refs[:7]
    refs = refs[7:]
    if quarter == SLICES:
        out_ref = refs[0]
        refs = refs[1:]
    if first:
        wo_ref, refs = refs[0], refs[1:]
    slope_ref, weights_ref, semaphore = refs

    @pl.when(pl.program_id(0) == 0)
    def _():
        core = place_ref[UNITS]

        def half(own):
            which = core if own else 1 - core
            return wo_ref.at[:, pl.ds(pl.multiple_of(HALF_D * which, NARROW), HALF_D)]

        for index, (slices, lane) in enumerate(layout):
            pieces = chunks[PIECES * index : PIECES * (index + 1)]
            if index == 0 and first:
                load(pieces, place_ref, ((0, HALF_D, half),), semaphore.at[SLICES])
            for turn, which in enumerate(slices):
                if which < quarter:
                    load(
                        pieces,
                        place_ref,
                        (
                            (
                                lane + D * turn,
                                D,
                                lambda own, which=which: weights_ref.at[which, core if own else 1 - core],
                            ),
                        ),
                        semaphore.at[which],
                    )
        if first:
            vg_ref[...] = jnp.zeros_like(vg_ref)
        else:
            vg_ref[...] = vg_before_ref[...]

    def arrived(index):
        @pl.when(pl.program_id(0) == 0)
        def _():
            all_arrived(weights_ref.at[index], semaphore.at[index])

    def vector(index):
        return vector_ref[index : index + 1, :]

    def add_row(index, value):
        vg_ref[index : index + 1, :] += jnp.sum(value, axis=0, keepdims=True)

    if first:

        @pl.when(pl.program_id(0) == 0)
        def _():
            all_arrived(wo_ref, semaphore.at[SLICES])

    width = 192 * quarter
    padded = -(-width // 128) * 128
    attended = o_ref[:, :padded]
    if padded != width:
        lane = lax.broadcasted_iota(jnp.int32, attended.shape, 1)
        attended = jnp.where(lane < width, attended, jnp.zeros_like(attended))
    branch = dot_last(attended, wo_ref[:, :padded]) + vector(2)
    normed_one, inverse_one = norm_forward(x_ref[...].astype(F32) + branch)
    first_norm = normed_one * vector(8) + vector(9)
    low = first_norm.astype(BF)
    x1_ref[...] = low
    total = first_norm + vector(7)
    for index in range(quarter):
        cols = slice(D * index, D * (index + 1))
        arrived(index)
        pre = dot(low, weights_ref[index, 0]) + vector(3 + index)
        value, slope = gelu_terms(pre)
        value = value.astype(BF)
        g_ref[:, cols] = value
        slope_ref[:, cols] = slope
        total = total + dot_last(value, weights_ref[index, 1])
    normed_two, inverse_two = norm_forward(total)
    upstream = cotangent_ref[...].astype(F32)
    if quarter == SLICES:
        out_ref[...] = (normed_two * vector(10) + vector(11)).astype(BF)
    add_row(11, upstream)
    add_row(10, upstream * normed_two)
    grad = norm_backward(upstream * vector(10), normed_two, inverse_two)
    low = grad.astype(BF)
    dm_ref[...] = low
    add_row(7, low.astype(F32))
    for index in range(quarter):
        cols = slice(D * index, D * (index + 1))
        pre = (dot(low, weights_ref[index, 1]) * slope_ref[:, cols]).astype(BF)
        du_ref[:, cols] = pre
        add_row(3 + index, pre.astype(F32))
        grad = grad + dot_last(pre, weights_ref[index, 0])
    add_row(9, grad)
    add_row(8, grad * normed_one)
    grad = norm_backward(grad * vector(8), normed_one, inverse_one)
    low = grad.astype(BF)
    da_ref[...] = low
    add_row(2, low.astype(F32))
    if first:
        dh1_ref[...] = grad
    else:
        dh1_ref[...] = before_ref[...] + grad


def ffn(quarter, place, inputs, attended, cotangent, vector, wo, chunks, before, block=512):
    tokens = inputs.shape[0]
    hidden = D * quarter
    rows = pl.BlockSpec((block, D), lambda i: (i, 0))
    wide = pl.BlockSpec((block, hidden), lambda i: (i, 0))
    first = wo is None
    low = jax.ShapeDtypeStruct((tokens, D), BF)
    low_wide = jax.ShapeDtypeStruct((tokens, hidden), BF)
    anywhere = pl.BlockSpec(memory_space=pl.ANY)
    chunks = [chunk for chunk in chunks if min(chunk[1]) < quarter]
    in_specs = [pl.BlockSpec(memory_space=pltpu.SMEM), rows, rows, rows, whole((16, D))]
    args = [place, inputs, attended, cotangent, vector]
    if not first:
        in_specs.append(whole((D, D)))
        args.append(wo)
    for chunk in chunks:
        in_specs += [anywhere] * PIECES
        args += list(chunk[0])
    if not first:
        in_specs += [rows, whole((16, D))]
        args += list(before)
    out_specs = [rows, rows, wide, wide, rows, rows, whole((16, D))]
    out_shape = [
        low,
        low,
        low_wide,
        low_wide,
        low,
        jax.ShapeDtypeStruct((tokens, D), F32),
        jax.ShapeDtypeStruct((16, D), F32),
    ]
    if quarter == SLICES:
        out_specs.append(rows)
        out_shape.append(low)
    if first:
        out_specs.append(whole((D, D)))
        out_shape.append(jax.ShapeDtypeStruct((D, D), BF))
    layout = [(chunk[1], chunk[2]) for chunk in chunks]
    return pl.pallas_call(
        partial(ffn_kernel, quarter, first, layout),
        grid=(tokens // block,),
        in_specs=in_specs,
        out_specs=out_specs,
        out_shape=out_shape,
        scratch_shapes=[
            pltpu.VMEM((block, hidden), F32),
            pltpu.VMEM((quarter, 2, D, D), BF),
            pltpu.SemaphoreType.DMA((SLICES + 1,)),
        ],
        compiler_params=params(),
        cost_estimate=cost(8e9 + quarter * 9e9, 20e6),
        name=f"ffn_{quarter}",
    )(*args)


def share(total_ref, place_ref, send_ref, keep_ref, lanes):
    core = place_ref[UNITS]
    for slot in range(UNITS):
        start = UNIT * place_ref[slot]
        other = total_ref[pl.ds(pl.multiple_of(start + OWN * (1 - core), 8), OWN), :]
        send_ref[slot, :, lanes] = other.astype(BF)
        keep_ref[slot, :, lanes] = total_ref[pl.ds(pl.multiple_of(start + OWN * core, 8), OWN), :]


def ffn_gradient_kernel(count, steps, *refs):
    place_ref, refs = refs[0], refs[1:]
    inputs, refs = refs[: 4 * count], refs[4 * count :]
    send_ref, keep_ref, up_ref, down_ref = refs
    step = pl.program_id(0)

    @pl.when(step == 0)
    def _():
        up_ref[...] = jnp.zeros_like(up_ref)
        down_ref[...] = jnp.zeros_like(down_ref)

    for index in range(count):
        x1_ref, dm_ref, g_ref, du_ref = inputs[4 * index : 4 * index + 4]

        @pl.when(step // steps == index)
        def _():
            up_ref[...] += dot_first(x1_ref[...], du_ref[...])
            down_ref[...] += dot_first(dm_ref[...], g_ref[...])

    @pl.when(step == count * steps - 1)
    def _():
        for index, ref in enumerate((up_ref, down_ref)):
            share(ref, place_ref, send_ref, keep_ref, slice(D * index, D * (index + 1)))


def ffn_gradient(column, place, states, block=512):
    tokens = states[0][0].shape[0]
    steps = tokens // block
    count = len(states)
    in_specs, args = [pl.BlockSpec(memory_space=pltpu.SMEM)], [place]
    for index, state in enumerate(states):
        def narrow(i, index=index):
            return (jnp.clip(i - index * steps, 0, steps - 1), 0)

        def wide(i, index=index):
            return (jnp.clip(i - index * steps, 0, steps - 1), column)

        in_specs += [
            pl.BlockSpec((block, D), narrow),
            pl.BlockSpec((block, D), narrow),
            pl.BlockSpec((block, D), wide),
            pl.BlockSpec((block, D), wide),
        ]
        args += list(state)
    return pl.pallas_call(
        partial(ffn_gradient_kernel, count, steps),
        grid=(count * steps,),
        in_specs=in_specs,
        out_specs=[whole((UNITS, OWN, 2 * D))] * 2,
        out_shape=[
            jax.ShapeDtypeStruct((UNITS, OWN, 2 * D), BF),
            jax.ShapeDtypeStruct((UNITS, OWN, 2 * D), F32),
        ],
        scratch_shapes=[pltpu.VMEM((D, D), F32)] * 2,
        cost_estimate=cost(count * 5e9, 20e6),
        compiler_params=params(),
        name=f"ffn_gradient_{column}",
    )(*args)


def attention_backward_kernel(
    place_ref, x_ref, q_ref, k_ref, v_ref, o_ref, p_ref, da4_ref, da3_ref, da2_ref, da1_ref, dh1_ref, weights_ref, wo_ref,
    vg_ref, *refs
):
    (
        dx_ref, send_ref, keep_ref, dw_ref, table_ref, do_ref, sum_ref, dq_ref, dk_ref, dv_ref,
    ) = refs

    @pl.when(pl.program_id(0) == 0)
    def _():
        dw_ref[...] = jnp.zeros_like(dw_ref)
        table_ref[...] = vg_ref[...]

    length = x_ref.shape[1]
    running = da4_ref[0].astype(F32)
    sum_ref[3] = da4_ref[0]
    for index, ref in ((2, da3_ref), (1, da2_ref), (0, da1_ref)):
        running = running + ref[0].astype(F32)
        sum_ref[index] = running.astype(BF)
    lane = lax.broadcasted_iota(jnp.int32, (length, 256), 1)
    for block in range(3):
        cols = slice(256 * block, 256 * (block + 1))
        edge = 192 * (block + 1) - 256 * block
        do_ref[:, cols] = jnp.where(
            lane < edge,
            dot(sum_ref[block], wo_ref[:, cols]),
            dot(sum_ref[block + 1], wo_ref[:, cols]),
        ).astype(BF)
        attended = o_ref[0, :, cols]
        nothing = jnp.zeros_like(attended)
        dw_ref[3, :, cols] += dot_first(
            sum_ref[block], jnp.where(lane < edge, attended, nothing)
        ) + dot_first(sum_ref[block + 1], jnp.where(lane < edge, nothing, attended))
    lane = lax.broadcasted_iota(jnp.int32, (length, 128), 1)
    dv_ref[...] = jnp.zeros_like(dv_ref)
    dk_ref[...] = jnp.zeros_like(dk_ref)
    for pair in range(PAIRS):
        cols = slice(128 * pair, 128 * (pair + 1))
        q_pair = q_ref[0, :, cols]
        k_pair = k_ref[0, :, cols]
        v_pair = v_ref[0, :, cols]
        do_pair = do_ref[:, cols]
        q_turned = q_pair.T
        do_turned = do_pair.T
        results = []
        for side in range(2):
            do_one = jnp.where((lane >= 64) == bool(side), do_pair, jnp.zeros_like(do_pair))
            heads = slice(64 * side, 64 * (side + 1))
            out = slice(128 * pair + 64 * side, 128 * pair + 64 * (side + 1))
            parts = []
            for part in range(2):
                window = slice(128 * part, 128 * part + WINDOW)
                rows = slice(HALF * part, HALF * (part + 1))
                low = p_ref[0, 2 * pair + side, part]
                dp = dot_last(do_one[rows], v_pair[window])
                prob = low.astype(F32)
                mixed = prob * dp
                ds = (mixed - prob * jnp.sum(mixed, axis=-1, keepdims=True)).astype(BF)
                dv_ref[out, window] += dot(do_turned[heads, rows], low)
                dk_ref[out, window] += dot(q_turned[heads, rows], ds)
                parts.append(dot(ds, k_pair[window]))
            results.append(jnp.concatenate(parts, axis=0))
        dq_ref[:, cols] = (jnp.where(lane >= 64, results[1], results[0]) * SCALING).astype(BF)
    dq = dq_ref[...]
    dk = dk_ref[...].astype(BF).T
    dv = dv_ref[...].astype(BF).T
    dx_ref[0] = (
        dh1_ref[0]
        + dot_last(dq, weights_ref[0])
        + dot_last(dk, weights_ref[1])
        + dot_last(dv, weights_ref[2])
    ).astype(BF)
    turned = x_ref[0].T
    dw_ref[0] += dot(turned, dq)
    dw_ref[1] += dot(turned, dk)
    dw_ref[2] += dot(turned, dv)
    table_ref[0:1, :] += jnp.sum(dq.astype(F32), axis=0, keepdims=True)
    table_ref[1:2, :] += jnp.sum(dv.astype(F32), axis=0, keepdims=True)

    @pl.when(pl.program_id(0) == pl.num_programs(0) - 1)
    def _():
        for index in range(4):
            share(dw_ref.at[index], place_ref, send_ref, keep_ref, slice(D * index, D * (index + 1)))
        core = place_ref[UNITS]
        lanes = slice(4 * D, 4 * D + NARROW)
        table = table_ref[...]
        nothing = jnp.zeros((OWN - table.shape[0], NARROW), F32)
        for slot in range(UNITS):
            for one, ref in ((1 - core, send_ref), (core, keep_ref)):
                turned = pltpu.roll(table, lax.rem(D - UNIT * place_ref[slot] - OWN * one, D), 1)[:, :NARROW]
                ref[slot, :, lanes] = jnp.concatenate([turned, nothing], axis=0).astype(ref.dtype)


def attention_backward(place, inputs, q, k, v, o, p, das, dh1, weights, wo, table):
    micro, length, _ = inputs.shape
    block = pl.BlockSpec((1, length, D), lambda i: (i, 0, 0))
    lanes = 4 * D + NARROW
    return pl.pallas_call(
        attention_backward_kernel,
        grid=(micro,),
        in_specs=[pl.BlockSpec(memory_space=pltpu.SMEM)]
        + [block] * 5
        + [pl.BlockSpec((1, HEADS, 2, HALF, WINDOW), lambda i: (i, 0, 0, 0, 0))]
        + [block] * 5
        + [whole((3, D, D)), whole((D, D)), whole((16, D))],
        out_specs=[block, whole((UNITS, OWN, lanes)), whole((UNITS, OWN, lanes))],
        out_shape=[
            jax.ShapeDtypeStruct((micro, length, D), BF),
            jax.ShapeDtypeStruct((UNITS, OWN, lanes), BF),
            jax.ShapeDtypeStruct((UNITS, OWN, lanes), F32),
        ],
        scratch_shapes=[
            pltpu.VMEM((4, D, D), F32),
            pltpu.VMEM((16, D), F32),
            pltpu.VMEM((length, D), BF),
            pltpu.VMEM((4, length, D), BF),
            pltpu.VMEM((length, D), BF),
            pltpu.VMEM((D, length), F32),
            pltpu.VMEM((D, length), F32),
        ],
        compiler_params=params(),
        cost_estimate=cost(40e9, 30e6),
        name="attention_backward",
    )(place, inputs, q, k, v, o, p, *das, dh1, weights, wo, table)


AXES = ("wide", "narrow")
PLANE = (0, 4, 2, 6)
ALONG = (0, 8, 16, 24)
DEVICES = 32


def flip(value, bits):
    return lax.ppermute(value, AXES, [(device, device ^ bits) for device in range(DEVICES)])


def tie(value, *earlier):
    return lax.optimization_barrier((value, *earlier))[0] if earlier else value


class Gather:
    def __init__(self, parts, core):
        mine = jnp.where(core == 0, parts[0], parts[1])
        theirs = flip(jnp.where(core == 0, parts[1], parts[0]), 1)
        self.unit = jnp.where(core == 0, jnp.concatenate([mine, theirs]), jnp.concatenate([theirs, mine]))

    def along(self, *earlier):
        self.unit = tie(self.unit, *earlier)
        self.near = jnp.stack([self.unit if bits == 0 else flip(self.unit, bits) for bits in ALONG])

    def plane(self, *earlier):
        self.near = tie(self.near, *earlier)
        self.own = [self.near if bits == 0 else flip(self.near, bits) for bits in PLANE]

    def peers(self, *earlier):
        own = [tie(piece, *earlier) for piece in self.own]
        self.peer = [flip(piece, 1) for piece in own]
        return self.own + self.peer


def gather_plain(parts):
    full = [lax.all_gather(part, AXES, axis=0, tiled=True).reshape(UNITS, UNIT, -1) for part in parts]
    return [value[4 * turn : 4 * turn + 4] for value in full for turn in range(4)]


class Reduce:
    def __init__(self, send, keep):
        self.keep = keep
        self.out = [send]
        self.arrived = [flip(send, 1)]

    def wait(self, earlier):
        if earlier:
            self.arrived = list(lax.optimization_barrier((*self.arrived, *earlier)))[: len(self.arrived)]

    def plane(self, *earlier):
        self.wait(earlier)

        def piece(turn):
            part = slice(4 * turn, 4 * turn + 4)
            return self.keep[part] + self.arrived[0][part].astype(F32)

        self.out = [piece(turn).astype(BF) for turn in (1, 2, 3)]
        self.total = piece(0)
        self.arrived = [flip(value, bits) for value, bits in zip(self.out, PLANE[1:])]

    def along(self, *earlier):
        self.wait(earlier)
        total = self.total
        for value in self.arrived:
            total = total + value.astype(F32)
        self.out = [total[turn].astype(BF) for turn in (1, 2, 3)]
        self.total = total[0]
        self.arrived = [flip(value, bits) for value, bits in zip(self.out, ALONG[1:])]

    def result(self, *earlier):
        self.wait(earlier)
        total = self.total
        for value in self.arrived:
            total = total + value.astype(F32)
        return total


class ReducePlain:
    def __init__(self, send, keep):
        self.send, self.keep, self.out = send, keep, [send]

    def plane(self, *earlier):
        pass

    along = plane

    def result(self, *earlier):
        both = jnp.stack([self.keep.astype(BF), self.send], axis=1).reshape(D, -1)
        return lax.psum_scatter(both, AXES, scatter_dimension=0, tiled=True).astype(F32)


def update(weights_now, momentum_now, average_now, gradient, rate):
    momentum_next = MOMENTUM * momentum_now + gradient
    weights_next = weights_now - rate * (gradient + MOMENTUM * momentum_next)
    average_next = DECAY * average_now + (1.0 - DECAY) * weights_next
    return (weights_next, momentum_next, average_next, weights_next.astype(BF))


def body(
    inputs,
    cotangent,
    doc_ids,
    attention_weights,
    attention_momentum,
    attention_average,
    feedforward_weights,
    feedforward_momentum,
    feedforward_average,
    vector_weights,
    vector_momentum,
    vector_average,
):
    micro, _, length, _ = inputs.shape
    count = lax.axis_size("wide") * lax.axis_size("narrow")
    me = lax.axis_index("wide") * lax.axis_size("narrow") + lax.axis_index("narrow")
    rows = attention_weights.shape[1]
    names = vector_weights.shape[0]
    paired = count == DEVICES
    if paired:
        core = me % 2
        offsets = [(plane ^ along) // 2 for plane in PLANE for along in ALONG]
        slots = me // 2 ^ jnp.asarray(offsets, jnp.int32)
    else:
        core = jnp.zeros((), jnp.int32)
        slots = jnp.arange(UNITS, dtype=jnp.int32)
    place = jnp.concatenate([slots, jnp.full((UNITS,), core, jnp.int32)])

    attention_low = attention_weights.astype(BF)
    hidden_low = feedforward_weights.astype(BF)
    vector_low = vector_weights.astype(BF)

    def halves(value):
        return value[:, :HALF_D], value[:, HALF_D:]

    def parts_of(columns):
        return [jnp.concatenate([column[which] for column in columns], axis=1) for which in (0, 1)]

    def hidden(which):
        return tuple(hidden_low[c, :, D * which : D * (which + 1)] for c in (0, 1))

    groups = ((0, 1), (2, 3))
    parts = [
        parts_of([(attention_low[0], attention_low[2]), halves(attention_low[1])]),
        parts_of([halves(attention_low[3])] + [hidden(which) for which in groups[0]]),
        parts_of([hidden(which) for which in groups[1]]),
    ]
    inputs_rows, cotangent_rows = inputs[:, 0], cotangent[:, 0]

    def flat(value):
        return value.reshape(micro * length, D)

    def split(value):
        return value.reshape(micro, length, D)

    def forward(pieces, place):
        return attention_forward(inputs_rows, doc_ids[:, 0], place, pieces)

    if paired:
        table = jnp.pad(vector_low, ((0, OWN - names), (0, NARROW - OWN)))
        parts[0] = [jnp.concatenate([part, table], axis=1) for part in parts[0]]
        one, two, three = [Gather(part, core) for part in parts]
        one.along()
        one.plane()
        first_pieces = one.peers()
        two.along(one.near)
        two.plane(*one.peer)
        three.along(two.near)
        q, k, v, o, p, weights, vector = forward(first_pieces, tie(place, two.near, three.near))
        second_pieces = two.peers(q)
        three.plane(q, *two.peer)
        ready = three.near
    else:
        table = lax.all_gather(vector_low, AXES, axis=1, tiled=True)
        table = table.reshape(names, UNITS, 2, OWN).transpose(1, 2, 0, 3)
        table = jnp.pad(table, ((0, 0), (0, 0), (0, OWN - names), (0, NARROW - OWN)))
        table = table.reshape(UNITS, UNIT, NARROW)
        first_pieces, second_pieces, third_pieces = [gather_plain(part) for part in parts]
        first_pieces = [
            jnp.concatenate([piece, table[4 * (turn % 4) : 4 * (turn % 4) + 4]], axis=2)
            for turn, piece in enumerate(first_pieces)
        ]
        q, k, v, o, p, weights, vector = forward(first_pieces, place)
        ready = place
    chunks = [(second_pieces, groups[0], HALF_D)]

    states, before, wo = {}, None, None

    def widths(quarter, *earlier):
        nonlocal before, wo
        result = ffn(
            quarter, tie(place, *earlier), flat(inputs_rows), flat(o), flat(cotangent_rows), vector, wo, chunks, before
        )
        states[quarter] = result[:5]
        before = (result[5], result[6])
        if wo is None:
            wo = result[-1]
        return result

    def gradient(which, *earlier):
        return ffn_gradient(
            which, tie(place, *earlier), [states[quarter][:4] for quarter in range(which + 1, SLICES + 1)]
        )

    reduce = Reduce if paired else ReducePlain
    widths(1, ready)
    chunks.append((three.peers(before[0]) if paired else third_pieces, groups[1], 0))
    layer_out = split(widths(4)[7])
    three = reduce(*gradient(3))
    widths(3, *three.out)
    three.plane(before[0])
    two = reduce(*gradient(2, *three.out))
    widths(2, *two.out)
    three.along(before[0])
    two.plane(before[0])
    input_grad, send, keep = attention_backward(
        tie(place, *three.out, *two.out), inputs_rows, q, k, v, o, p,
        [split(states[quarter][4]) for quarter in (4, 3, 2, 1)],
        split(before[0]), weights, wo, before[1],
    )
    attention = reduce(send, keep)
    two.along(send)
    one = reduce(*gradient(1, *attention.out, *two.out))
    last = one.out[0]
    attention.plane(last)
    zero = reduce(*gradient(0, last, *attention.out))
    last = zero.out[0]
    attention.along(last)
    one.plane(*attention.out)
    zero.plane(*one.out)
    attention_sum = attention.result(*zero.out)
    one.along(*zero.out)
    zero.along(*one.out)
    sums = [zero.result(), one.result(*zero.out), two.result(last), three.result(last)]

    attention_gradient = jnp.stack([attention_sum[:, D * c : D * (c + 1)] for c in range(4)])
    feedforward_gradient = jnp.stack(
        [jnp.concatenate([sums[s][:, D * c : D * (c + 1)] for s in range(SLICES)], axis=1) for c in (0, 1)]
    )
    if paired:
        vector_gradient = attention_sum[:names, 4 * D : 4 * D + rows]
    else:
        table = jnp.stack([keep, send.astype(F32)], axis=1)[:, :, :names, 4 * D : 4 * D + OWN]
        table = table.transpose(2, 0, 1, 3).reshape(names, D)
        vector_gradient = lax.psum_scatter(table, AXES, scatter_dimension=1, tiled=True)

    rate = 0.05 / math.sqrt(micro * length * count)
    return (
        layer_out[:, None],
        input_grad[:, None],
        *update(attention_weights, attention_momentum, attention_average, attention_gradient, rate),
        *update(feedforward_weights, feedforward_momentum, feedforward_average, feedforward_gradient, rate),
        *update(vector_weights, vector_momentum, vector_average, vector_gradient, rate),
    )


def solution(mesh):
    row = P(None, AXES, None, None)
    matrix = P(None, AXES, None)
    table = P(None, AXES)
    in_specs = (row, row, matrix) + (matrix,) * 6 + (table,) * 3
    out_specs = (row, row) + (matrix,) * 8 + (table,) * 4
    return jax.shard_map(body, mesh=mesh, in_specs=in_specs, out_specs=out_specs, check_vma=False)
```

time: 1470 us -> 446 us (0.30)
  matrix products: 589 us -> 0 us
  waiting for transfers between devices: 467 us -> 100 us
  Pallas kernels: 0 us -> 248 us
  other arithmetic: 209 us -> 22.4 us
  local copies, waits for them, and re-layouts: 94.1 us -> 3.35 us
  blocking collectives: 84.1 us -> 0 us
  starting transfers between devices: 0.41 us -> 67.3 us
  between operations: 19.7 us -> 1.68 us
    dot_general x192 -> x0, matrix products: 589 us -> none  [the longest x48 119 us: dot_last(): lax.dot_general(left, right, (((1,), (1,)), ((), ())), preferred_element_...]
    all_gather x8 -> x0, waiting for transfers between devices: 268 us -> none  [the longest x4 142 us: fetch_prefix(): lax.all_gather(feedforward_weights[:, :, :hidden_used].astype(jnp.bfloat1...]
    pallas_call x0 -> x10, Pallas kernels: none -> 248 us  [the longest x4 119 us: ffn(): pl.pallas_call(partial(ffn_kernel, quarter, first, layout), grid=(tokens...]
    reduce_scatter x1 -> x0, waiting for transfers between devices: 197 us -> none  [body(): lax.psum_scatter(feedforward_total, ('wide', 'narrow'), scatter_dimension...]
    ppermute x0 -> x68, waiting for transfers between devices: none -> 100 us  [flip(): lax.ppermute(value, AXES, [(device, device ^ bits) for device in range(DE...]
    scatter-add x12 -> x0, other arithmetic: 74 us -> none  [the longest x6 56.6 us: body(): feedforward_total.at[:, :, :hidden_used].add(grad_feedforward)]
    ppermute x0 -> x68, starting transfers between devices: none -> 67.3 us  [flip(): lax.ppermute(value, AXES, [(device, device ^ bits) for device in range(DE...]
    convert_element_type x13 -> x11, other arithmetic: 58 us -> 10.3 us  [the longest x5 6.03 us: plane(): self.out = [piece(turn).astype(BF) for turn in (1, 2, 3)]]
  transfers between devices with their start and end apart: 10 -> 68, of which waited for: 9 -> 24; matrix products, arithmetic and copies ran while one was open for 24% -> 4% of each run, Pallas kernels for 0% -> 45%
where the time goes in v1:
time: 446 us; the launch traced here: 443 us
  Pallas kernels  248 us (56%)
  waiting for transfers between devices  100 us (22%)
  starting transfers between devices  67.3 us (15%)
  other arithmetic  22.4 us (5%)
    pallas_call x4, Pallas kernels, ffn(): pl.pallas_call(partial(ffn_kernel, quarter, first, layout), grid=(tokens...  119 us
    ppermute x68, waiting for transfers between devices, flip(): lax.ppermute(value, AXES, [(device, device ^ bits) for device in range(DE...  100 us
    ppermute x68, starting transfers between devices, flip(): lax.ppermute(value, AXES, [(device, device ^ bits) for device in range(DE...  67.3 us
    pallas_call x4, Pallas kernels, ffn_gradient(): pl.pallas_call(partial(ffn_gradient_kernel, count, steps), grid=(count *...  54.9 us
    pallas_call x1, Pallas kernels, attention_backward(): pl.pallas_call(attention_backward_kernel, grid=(micro,), in_specs=[pl.Blo...  43.9 us
    pallas_call x1, Pallas kernels, attention_forward(): pl.pallas_call(attention_forward_kernel, grid=(micro,), in_specs=[pl.Bloc...  30.3 us
  transfers between devices with their start and end apart: 68, of which 24 were waited for; matrix products, arithmetic and copies ran while one was open for 4% of the time, Pallas kernels for 45%

profile of v1, /device:TPU:0, one launch (start us, length us, event | category | flops | bytes accessed | tf_op | source)
XLA Modules:
  0.0 442.7 jit_solution(193400698931704279)
XLA Ops:
  3.9 5.0 %collective-permute-start.4 = (bf16[48,1280]{1,0:T(8,128)(2,1)S(1)}, bf16[48,1280]{1,0:T(8,128)(2,1)S(1)}, u32[]{:S(2)}, u32[]{:S(2)}) collective-permute-start(bf16[48,1280]{1,0:T(8,128)(2,1)S(1)} %maximum_select_fusion.3), channel_id=1, source_target_pairs={{0,24},{1,25},{2,26},{3,27},{4,28},{5,29},{6,30},{7,31},{8,16},{9,... | collective-permute-start | bytes 368648 | tf_op jit(solution)/shard_map/ppermute | solution.py:588
  9.6 3.5 collective-permute-done.4
  13.1 6.5 %collective-permute-done.3 = bf16[48,1280]{1,0:T(8,128)(2,1)S(1)} collective-permute-done((bf16[48,1280]{1,0:T(8,128)(2,1)S(1)}, bf16[48,1280]{1,0:T(8,128)(2,1)S(1)}, u32[]{:S(2)}, u32[]{:S(2)}) %collective-permute-start.3) | collective-permute-done | bytes 122912 | tf_op jit(solution)/shard_map/ppermute | solution.py:588
  19.7 2.5 collective-permute-start.13
  23.4 2.6 collective-permute-start.7
  26.0 6.8 %collective-permute-done.7 = bf16[48,1920]{1,0:T(8,128)(2,1)S(1)} collective-permute-done((bf16[48,1920]{1,0:T(8,128)(2,1)S(1)}, bf16[48,1920]{1,0:T(8,128)(2,1)S(1)}, u32[]{:S(2)}, u32[]{:S(2)}) %collective-permute-start.7) | collective-permute-done | bytes 184352 | tf_op jit(solution)/shard_map/ppermute | solution.py:588
  32.8 2.0 collective-permute-done.13.refs_3_
  34.9 8.8 %collective-permute-done.11.refs_2_ = bf16[4,48,1280]{2,1,0:T(8,128)(2,1)S(1)} collective-permute-done((bf16[4,48,1280]{2,1,0:T(8,128)(2,1)S(1)}, bf16[4,48,1280]{2,1,0:T(8,128)(2,1)S(1)}, u32[]{:S(2)}, u32[]{:S(2)}) %collective-permute-start.11) | collective-permute-done | bytes 491552 | tf_op jit(solution)/shard_map/ppermute | solution.py:588
  44.2 6.6 %collective-permute-done.5 = bf16[48,1920]{1,0:T(8,128)(2,1)S(1)} collective-permute-done((bf16[48,1920]{1,0:T(8,128)(2,1)S(1)}, bf16[48,1920]{1,0:T(8,128)(2,1)S(1)}, u32[]{:S(2)}, u32[]{:S(2)}) %collective-permute-start.5) | collective-permute-done | bytes 184352 | tf_op jit(solution)/shard_map/ppermute | solution.py:588
  51.0 2.6 collective-permute-start.18
  53.6 1.9 collective-permute-start.16
  57.0 1.7 collective-permute-start.24
  61.1 4.4 %collective-permute-done.17 = bf16[48,1536]{1,0:T(8,128)(2,1)S(1)} collective-permute-done((bf16[48,1536]{1,0:T(8,128)(2,1)S(1)}, bf16[48,1536]{1,0:T(8,128)(2,1)S(1)}, u32[]{:S(2)}, u32[]{:S(2)}) %collective-permute-start.17) | collective-permute-done | bytes 147488 | tf_op jit(solution)/shard_map/ppermute | solution.py:588
  65.7 30.3 %attention_forward.1 = (bf16[2,512,768]{2,1,0:T(8,128)(2,1)}, bf16[2,512,768]{2,1,0:T(8,128)(2,1)}, bf16[2,512,768]{2,1,0:T(8,128)(2,1)}, bf16[2,512,768]{2,1,0:...) custom-call(s32[32]{0:T(128)} %concatenate.89.place_ref.refs_0_, ...), custom_call_target="tpu_custom_call" | custom-call | flops 17999998976 | bytes 20000000 | tf_op jit(solution)/shard_map/attention_forward/pallas_call | solution.py:159
  98.3 2.3 collective-permute-done.21.refs_10_.refs_11_
  101.7 1.8 collective-permute-start.28
  105.2 17.5 %ffn_1.1 = (bf16[1024,768]{1,0:T(8,128)(2,1)}, bf16[1024,768]{1,0:T(8,128)(2,1)}, bf16[1024,768]{1,0:T(8,128)(2,1)}, bf16[1024,768]{1,0:T(8,128)(2,1)}, bf16[102...) custom-call(s32[32]{0:T(128)} %concatenate.89.place_ref.refs_0_, ...), custom_call_target="tpu_custom_call" | custom-call | flops 16999999488 | bytes 20000000 | tf_op jit(solution)/shard_map/ffn_1/pallas_call | solution.py:369
  122.9 7.7 %collective-permute-done.27.refs_16_ = bf16[4,48,1536]{2,1,0:T(8,128)(2,1)S(1)} collective-permute-done((bf16[4,48,1536]{2,1,0:T(8,128)(2,1)S(1)}, bf16[4,48,1536]{2,1,0:T(8,128)(2,1)S(1)}, u32[]{:S(2)}, u32[]{:S(2)}) %collective-permute-start.27) | collective-permute-done | bytes 589856 | tf_op jit(solution)/shard_map/ppermute | solution.py:588
  131.3 2.5 collective-permute-done.30.refs_19_
  135.3 42.5 %ffn_4.1 = (bf16[1024,768]{1,0:T(8,128)(2,1)}, bf16[1024,768]{1,0:T(8,128)(2,1)}, bf16[1024,3072]{1,0:T(8,128)(2,1)}, bf16[1024,3072]{1,0:T(8,128)(2,1)}, bf16[1...) custom-call(s32[32]{0:T(128)} %concatenate.89.place_ref.refs_0_, ...), custom_call_target="tpu_custom_call" | custom-call | flops 44000002048 | bytes 20000000 | tf_op jit(solution)/shard_map/ffn_4/pallas_call | solution.py:369
  177.8 7.2 %ffn_gradient_3.1 = (bf16[16,24,1536]{2,1,0:T(8,128)(2,1)}, f32[16,24,1536]{2,1,0:T(8,128)}) custom-call(s32[32]{0:T(128)} %concatenate.89.place_ref.refs_0_, bf16[1024,768]{1,0:T(8,128)(2,1)} %get-tuple-element.135.refs_1_.refs_5_.refs_9_.refs_13_, bf16[1024,768]{1,0:T(8,128)(2,1)} %get-tuple-element.136.refs_2_.refs_6_.refs_10_.refs_14_, ...), custom_call_target="tpu_custom_call" | custom-call | flops 5000000000 | bytes 20000000 | tf_op jit(solution)/shard_map/ffn_gradient_3/pallas_call | solution.py:439
  185.0 33.3 %ffn_3.1 = (bf16[1024,768]{1,0:T(8,128)(2,1)}, bf16[1024,768]{1,0:T(8,128)(2,1)}, bf16[1024,2304]{1,0:T(8,128)(2,1)}, bf16[1024,2304]{1,0:T(8,128)(2,1)}, bf16[1...) custom-call(s32[32]{0:T(128)} %concatenate.89.place_ref.refs_0_, bf16[1024,768]{1,0:T(8,128)(2,1)} %bitcast.154, ...), custom_call_target="tpu_custom_call" | custom-call | flops 35000000512 | bytes 20000000 | tf_op jit(solution)/shard_map/ffn_3/pallas_call | solution.py:369
  223.1 11.6 %ffn_gradient_2.1 = (bf16[16,24,1536]{2,1,0:T(8,128)(2,1)}, f32[16,24,1536]{2,1,0:T(8,128)}) custom-call(s32[32]{0:T(128)} %concatenate.89.place_ref.refs_0_, bf16[1024,768]{1,0:T(8,128)(2,1)} %get-tuple-element.147.refs_1_.refs_5_.refs_9_, bf16[1024,768]{1,0:T(8,128)(2,1)} %get-tuple-element.148.refs_2_.refs_6_.refs_10_, ...), custom_call_target="tpu_custom_call" | custom-call | flops 10000000000 | bytes 20000000 | tf_op jit(solution)/shard_map/ffn_gradient_2/pallas_call | solution.py:439
  234.7 25.3 %ffn_2.1 = (bf16[1024,768]{1,0:T(8,128)(2,1)}, bf16[1024,768]{1,0:T(8,128)(2,1)}, bf16[1024,1536]{1,0:T(8,128)(2,1)}, bf16[1024,1536]{1,0:T(8,128)(2,1)}, bf16[1...) custom-call(s32[32]{0:T(128)} %concatenate.89.place_ref.refs_0_, bf16[1024,768]{1,0:T(8,128)(2,1)} %bitcast.155, ...), custom_call_target="tpu_custom_call" | custom-call | flops 25999998976 | bytes 20000000 | tf_op jit(solution)/shard_map/ffn_2/pallas_call | solution.py:369
  260.1 2.4 fusion.25
  267.7 43.9 %attention_backward.1 = (bf16[2,512,768]{2,1,0:T(8,128)(2,1)}, bf16[16,24,3200]{2,1,0:T(8,128)(2,1)}, f32[16,24,3200]{2,1,0:T(8,128)}) custom-call(s32[32]{0:T(128)} %concatenate.89.place_ref.refs_0_, bf16[2,512,768]{2,1,0:T(8,128)(2,1)} %bitcast.156, bf16[2,512,768]{2,1,0:T(8,128)(2,1)} %get-tuple-element.120.q_ref, ...), custom_call_target="tpu_custom_call" | custom-call | flops 40000000000 | bytes 30000000 | tf_op jit(solution)/shard_map/attention_backward/pallas_call | solution.py:552
  311.7 2.6 collective-permute-start.67
  314.3 1.9 collective-permute-start.65
  316.1 2.3 fusion.24
  318.5 2.6 collective-permute-start.64
  321.0 15.8 %ffn_gradient_1.1 = (bf16[16,24,1536]{2,1,0:T(8,128)(2,1)}, f32[16,24,1536]{2,1,0:T(8,128)}) custom-call(s32[32]{0:T(128)} %concatenate.89.place_ref.refs_0_, bf16[1024,768]{1,0:T(8,128)(2,1)} %get-tuple-element.177.refs_1_.refs_5_, bf16[1024,768]{1,0:T(8,128)(2,1)} %get-tuple-element.178.refs_2_.refs_6_, ...), custom_call_target="tpu_custom_call" | custom-call | flops 15000000512 | bytes 20000000 | tf_op jit(solution)/shard_map/ffn_gradient_1/pallas_call | solution.py:439
  336.9 3.3 add_convert_fusion
  340.2 20.4 %ffn_gradient_0.1 = (bf16[16,24,1536]{2,1,0:T(8,128)(2,1)}, f32[16,24,1536]{2,1,0:T(8,128)}) custom-call(s32[32]{0:T(128)} %concatenate.89.place_ref.refs_0_, bf16[1024,768]{1,0:T(8,128)(2,1)} %get-tuple-element.184.refs_1_, bf16[1024,768]{1,0:T(8,128)(2,1)} %get-tuple-element.185.refs_2_, bf16[1024,768]{1,0:T(8,128)(2,1)} %get-tuple-element.186.refs_3_, ...), custom_call_target="tpu_custom_call" | custom-call | flops 20000000000 | bytes 20000000 | tf_op jit(solution)/shard_map/ffn_gradient_0/pallas_call | solution.py:439
  360.6 1.9 collective-permute-start.62
  362.6 1.6 collective-permute-start.44
  368.3 12.1 %collective-permute-done.44 = bf16[4,24,3200]{2,1,0:T(8,128)(2,1)S(1)} collective-permute-done((bf16[4,24,3200]{2,1,0:T(8,128)(2,1)}, bf16[4,24,3200]{2,1,0:T(8,128)(2,1)S(1)}, u32[]{:S(2)}, u32[]{:S(2)}) %collective-permute-start.44) | collective-permute-done | bytes 614432 | tf_op jit(solution)/shard_map/ppermute | solution.py:588
  380.4 12.7 %collective-permute-done.43 = bf16[4,24,3200]{2,1,0:T(8,128)(2,1)S(1)} collective-permute-done((bf16[4,24,3200]{2,1,0:T(8,128)(2,1)S(1)}, bf16[4,24,3200]{2,1,0:T(8,128)(2,1)S(1)}, u32[]{:S(2)}, u32[]{:S(2)}) %collective-permute-start.43) | collective-permute-done | bytes 614432 | tf_op jit(solution)/shard_map/ppermute | solution.py:588
  393.1 1.8 fusion.23
  395.0 2.6 collective-permute-start.47
  397.8 1.6 collective-permute-start.55
  401.6 7.1 %collective-permute-done.55 = bf16[4,24,1536]{2,1,0:T(8,128)(2,1)S(1)} collective-permute-done((bf16[4,24,1536]{2,1,0:T(8,128)(2,1)S(1)}, bf16[4,24,1536]{2,1,0:T(8,128)(2,1)S(1)}, u32[]{:S(2)}, u32[]{:S(2)}) %collective-permute-start.55) | collective-permute-done | bytes 294944 | tf_op jit(solution)/shard_map/ppermute | solution.py:588
  408.7 1.9 collective-permute-start.45
  410.6 3.1 collective-permute-done.54
  419.7 1.7 collective-permute-start.60
  426.2 3.7 collective-permute-done.51
  431.6 1.7 collective-permute-start.57
  434.7 2.1 collective-permute-done.58
  436.8 3.4 collective-permute-done.57
  (225 shorter events, 49.9 us)
Async XLA Ops:
  3.1 20.3 %collective-permute-start = (bf16[24,1920]{1,0:T(8,128)(2,1)S(1)}, bf16[24,1920]{1,0:T(8,128)(2,1)S(1)}, u32[]{:S(2)}, u32[]{:S(2)}) collective-permute-start(bf16[24,1920]{1,0:T(8,128)(2,1)S(1)} %get-tuple-element.304), channel_id=1, source_target_pairs={{0,1},{1,0},{2,3},{3,2},{4,5},{5,4},{6,7},{7,6},{8,9},{9,8},{10,11... | collective-permute-start | bytes 276488 | tf_op jit(solution)/shard_map/ppermute | solution.py:588
  8.9 10.7 %collective-permute-start.3 = (bf16[48,1280]{1,0:T(8,128)(2,1)S(1)}, bf16[48,1280]{1,0:T(8,128)(2,1)S(1)}, u32[]{:S(2)}, u32[]{:S(2)}) collective-permute-start(bf16[48,1280]{1,0:T(8,128)(2,1)S(1)} %maximum_select_fusion.3), channel_id=1, source_target_pairs={{0,16},{1,17},{2,18},{3,19},{4,20},{5,21},{6,22},{7,23},{8,24},{9,... | collective-permute-start | bytes 368648 | tf_op jit(solution)/shard_map/ppermute | solution.py:588
  8.9 10.7 %collective-permute-start.2 = (bf16[48,1280]{1,0:T(8,128)(2,1)S(1)}, bf16[48,1280]{1,0:T(8,128)(2,1)S(1)}, u32[]{:S(2)}, u32[]{:S(2)}) collective-permute-start(bf16[48,1280]{1,0:T(8,128)(2,1)S(1)} %maximum_select_fusion.3), channel_id=1, source_target_pairs={{0,8},{1,9},{2,10},{3,11},{4,12},{5,13},{6,14},{7,15},{8,0},{9,1},... | collective-permute-start | bytes 368648 | tf_op jit(solution)/shard_map/ppermute | solution.py:588
  19.7 15.2 %collective-permute-start.13 = (bf16[4,48,1280]{2,1,0:T(8,128)(2,1)S(1)}, bf16[4,48,1280]{2,1,0:T(8,128)(2,1)S(1)}, u32[]{:S(2)}, u32[]{:S(2)}) collective-permute-start(bf16[4,48,1280]{2,1,0:T(8,128)(2,1)S(1)} %pad_maximum_fusion.3.refs_0_), channel_id=1, source_target_pairs={{0,6},{1,7},{2,4},{3,5},{4,2},{5,3},{6,0},{7,1},{8,14},{9,15},{10,... | collective-permute-start | bytes 1474568 | tf_op jit(solution)/shard_map/ppermute | solution.py:588
  22.2 21.4 %collective-permute-start.11 = (bf16[4,48,1280]{2,1,0:T(8,128)(2,1)S(1)}, bf16[4,48,1280]{2,1,0:T(8,128)(2,1)S(1)}, u32[]{:S(2)}, u32[]{:S(2)}) collective-permute-start(bf16[4,48,1280]{2,1,0:T(8,128)(2,1)S(1)} %pad_maximum_fusion.3.refs_0_), channel_id=1, source_target_pairs={{0,2},{1,3},{2,0},{3,1},{4,6},{5,7},{6,4},{7,5},{8,10},{9,11},{10,... | collective-permute-start | bytes 1474568 | tf_op jit(solution)/shard_map/ppermute | solution.py:588
  22.7 21.0 %collective-permute-start.9 = (bf16[4,48,1280]{2,1,0:T(8,128)(2,1)S(1)}, bf16[4,48,1280]{2,1,0:T(8,128)(2,1)S(1)}, u32[]{:S(2)}, u32[]{:S(2)}) collective-permute-start(bf16[4,48,1280]{2,1,0:T(8,128)(2,1)S(1)} %pad_maximum_fusion.3.refs_0_), channel_id=1, source_target_pairs={{0,4},{1,5},{2,6},{3,7},{4,0},{5,1},{6,2},{7,3},{8,12},{9,13},{10,... | collective-permute-start | bytes 1474568 | tf_op jit(solution)/shard_map/ppermute | solution.py:588
  23.4 9.4 %collective-permute-start.7 = (bf16[48,1920]{1,0:T(8,128)(2,1)S(1)}, bf16[48,1920]{1,0:T(8,128)(2,1)S(1)}, u32[]{:S(2)}, u32[]{:S(2)}) collective-permute-start(bf16[48,1920]{1,0:T(8,128)(2,1)S(1)} %maximum_select_fusion), channel_id=1, source_target_pairs={{0,24},{1,25},{2,26},{3,27},{4,28},{5,29},{6,30},{7,31},{8,16},{9,... | collective-permute-start | bytes 552968 | tf_op jit(solution)/shard_map/ppermute | solution.py:588
  26.0 18.2 %collective-permute-start.6 = (bf16[48,1920]{1,0:T(8,128)(2,1)S(1)}, bf16[48,1920]{1,0:T(8,128)(2,1)S(1)}, u32[]{:S(2)}, u32[]{:S(2)}) collective-permute-start(bf16[48,1920]{1,0:T(8,128)(2,1)S(1)} %maximum_select_fusion), channel_id=1, source_target_pairs={{0,16},{1,17},{2,18},{3,19},{4,20},{5,21},{6,22},{7,23},{8,24},{9,... | collective-permute-start | bytes 552968 | tf_op jit(solution)/shard_map/ppermute | solution.py:588
  32.8 18.1 %collective-permute-start.8 = (bf16[4,48,1280]{2,1,0:T(8,128)(2,1)S(1)}, bf16[4,48,1280]{2,1,0:T(8,128)(2,1)}, u32[]{:S(2)}, u32[]{:S(2)}) collective-permute-start(bf16[4,48,1280]{2,1,0:T(8,128)(2,1)S(1)} %pad_maximum_fusion.3.refs_0_), channel_id=1, source_target_pairs={{0,1},{1,0},{2,3},{3,2},{4,5},{5,4},{6,7},{7,6},{8,9},{9,8},{10,11... | collective-permute-start | bytes 1474568 | tf_op jit(solution)/shard_map/ppermute | solution.py:588
  34.9 16.1 %collective-permute-start.14 = (bf16[4,48,1280]{2,1,0:T(8,128)(2,1)S(1)}, bf16[4,48,1280]{2,1,0:T(8,128)(2,1)}, u32[]{:S(2)}, u32[]{:S(2)}) collective-permute-start(bf16[4,48,1280]{2,1,0:T(8,128)(2,1)S(1)} %collective-permute-done.13.refs_3_), channel_id=1, source_target_pairs={{0,1},{1,0},{2,3},{3,2},{4,5},{5,4},{6,7},{7,6},{8,9},{9,8},{10,11... | collective-permute-start | bytes 1474568 | tf_op jit(solution)/shard_map/ppermute | solution.py:588
  53.6 12.0 %collective-permute-start.17 = (bf16[48,1536]{1,0:T(8,128)(2,1)S(1)}, bf16[48,1536]{1,0:T(8,128)(2,1)S(1)}, u32[]{:S(2)}, u32[]{:S(2)}) collective-permute-start(bf16[48,1536]{1,0:T(8,128)(2,1)S(1)} %maximum_select_fusion.1), channel_id=1, source_target_pairs={{0,16},{1,17},{2,18},{3,19},{4,20},{5,21},{6,22},{7,23},{8,24},{9,... | collective-permute-start | bytes 442376 | tf_op jit(solution)/shard_map/ppermute | solution.py:588
  53.6 12.0 %collective-permute-start.16 = (bf16[48,1536]{1,0:T(8,128)(2,1)S(1)}, bf16[48,1536]{1,0:T(8,128)(2,1)S(1)}, u32[]{:S(2)}, u32[]{:S(2)}) collective-permute-start(bf16[48,1536]{1,0:T(8,128)(2,1)S(1)} %maximum_select_fusion.1), channel_id=1, source_target_pairs={{0,8},{1,9},{2,10},{3,11},{4,12},{5,13},{6,14},{7,15},{8,0},{9,1},... | collective-permute-start | bytes 442376 | tf_op jit(solution)/shard_map/ppermute | solution.py:588
  57.0 39.1 %collective-permute-start.24 = (bf16[4,48,1920]{2,1,0:T(8,128)(2,1)S(1)}, bf16[4,48,1920]{2,1,0:T(8,128)(2,1)S(1)}, u32[]{:S(2)}, u32[]{:S(2)}) collective-permute-start(bf16[4,48,1920]{2,1,0:T(8,128)(2,1)S(1)} %pad_maximum_fusion.refs_5_.refs_6_), channel_id=1, source_target_pairs={{0,6},{1,7},{2,4},{3,5},{4,2},{5,3},{6,0},{7,1},{8,14},{9,15},{10,... | collective-permute-start | bytes 2211848 | tf_op jit(solution)/shard_map/ppermute | solution.py:588
  58.8 37.3 %collective-permute-start.22 = (bf16[4,48,1920]{2,1,0:T(8,128)(2,1)S(1)}, bf16[4,48,1920]{2,1,0:T(8,128)(2,1)}, u32[]{:S(2)}, u32[]{:S(2)}) collective-permute-start(bf16[4,48,1920]{2,1,0:T(8,128)(2,1)S(1)} %pad_maximum_fusion.refs_5_.refs_6_), channel_id=1, source_target_pairs={{0,2},{1,3},{2,0},{3,1},{4,6},{5,7},{6,4},{7,5},{8,10},{9,11},{10,... | collective-permute-start | bytes 2211848 | tf_op jit(solution)/shard_map/ppermute | solution.py:588
  60.0 36.1 %collective-permute-start.20 = (bf16[4,48,1920]{2,1,0:T(8,128)(2,1)S(1)}, bf16[4,48,1920]{2,1,0:T(8,128)(2,1)}, u32[]{:S(2)}, u32[]{:S(2)}) collective-permute-start(bf16[4,48,1920]{2,1,0:T(8,128)(2,1)S(1)} %pad_maximum_fusion.refs_5_.refs_6_), channel_id=1, source_target_pairs={{0,4},{1,5},{2,6},{3,7},{4,0},{5,1},{6,2},{7,3},{8,12},{9,13},{10,... | collective-permute-start | bytes 2211848 | tf_op jit(solution)/shard_map/ppermute | solution.py:588
  101.7 21.2 %collective-permute-start.28 = (bf16[4,48,1536]{2,1,0:T(8,128)(2,1)S(1)}, bf16[4,48,1536]{2,1,0:T(8,128)(2,1)S(1)}, u32[]{:S(2)}, u32[]{:S(2)}) collective-permute-start(bf16[4,48,1536]{2,1,0:T(8,128)(2,1)S(1)} %pad_maximum_fusion.1.refs_14_), channel_id=1, source_target_pairs={{0,6},{1,7},{2,4},{3,5},{4,2},{5,3},{6,0},{7,1},{8,14},{9,15},{10,... | collective-permute-start | bytes 1769480 | tf_op jit(solution)/shard_map/ppermute | solution.py:588
  103.5 27.1 %collective-permute-start.27 = (bf16[4,48,1536]{2,1,0:T(8,128)(2,1)S(1)}, bf16[4,48,1536]{2,1,0:T(8,128)(2,1)S(1)}, u32[]{:S(2)}, u32[]{:S(2)}) collective-permute-start(bf16[4,48,1536]{2,1,0:T(8,128)(2,1)S(1)} %pad_maximum_fusion.1.refs_14_), channel_id=1, source_target_pairs={{0,2},{1,3},{2,0},{3,1},{4,6},{5,7},{6,4},{7,5},{8,10},{9,11},{10,... | collective-permute-start | bytes 1769480 | tf_op jit(solution)/shard_map/ppermute | solution.py:588
  104.7 26.1 %collective-permute-start.26 = (bf16[4,48,1536]{2,1,0:T(8,128)(2,1)S(1)}, bf16[4,48,1536]{2,1,0:T(8,128)(2,1)}, u32[]{:S(2)}, u32[]{:S(2)}) collective-permute-start(bf16[4,48,1536]{2,1,0:T(8,128)(2,1)S(1)} %pad_maximum_fusion.1.refs_14_), channel_id=1, source_target_pairs={{0,4},{1,5},{2,6},{3,7},{4,0},{5,1},{6,2},{7,3},{8,12},{9,13},{10,... | collective-permute-start | bytes 1769480 | tf_op jit(solution)/shard_map/ppermute | solution.py:588
  184.9 33.5 %collective-permute-start.33 = (bf16[16,24,1536]{2,1,0:T(8,128)(2,1)}, bf16[16,24,1536]{2,1,0:T(8,128)(2,1)S(1)}, u32[]{:S(2)}, u32[]{:S(2)}) collective-permute-start(bf16[16,24,1536]{2,1,0:T(8,128)(2,1)} %get-tuple-element.140), channel_id=1, source_target_pairs={{0,1},{1,0},{2,3},{3,2},{4,5},{5,4},{6,7},{7,6},{8,9},{9,8},{10,11... | collective-permute-start | bytes 3538952 | tf_op jit(solution)/shard_map/ppermute | solution.py:588
  219.6 40.5 %collective-permute-start.36 = (bf16[4,24,1536]{2,1,0:T(8,128)(2,1)}, bf16[4,24,1536]{2,1,0:T(8,128)(2,1)}, u32[]{:S(2)}, u32[]{:S(2)}) collective-permute-start(bf16[4,24,1536]{2,1,0:T(8,128)(2,1)} %get-tuple-element.273), channel_id=1, source_target_pairs={{0,6},{1,7},{2,4},{3,5},{4,2},{5,3},{6,0},{7,1},{8,14},{9,15},{10,... | collective-permute-start | bytes 884744 | tf_op jit(solution)/shard_map/ppermute | solution.py:588
  221.1 38.9 %collective-permute-start.35 = (bf16[4,24,1536]{2,1,0:T(8,128)(2,1)}, bf16[4,24,1536]{2,1,0:T(8,128)(2,1)}, u32[]{:S(2)}, u32[]{:S(2)}) collective-permute-start(bf16[4,24,1536]{2,1,0:T(8,128)(2,1)} %get-tuple-element.274), channel_id=1, source_target_pairs={{0,2},{1,3},{2,0},{3,1},{4,6},{5,7},{6,4},{7,5},{8,10},{9,11},{10,... | collective-permute-start | bytes 884744 | tf_op jit(solution)/shard_map/ppermute | solution.py:588
  222.3 37.7 %collective-permute-start.34 = (bf16[4,24,1536]{2,1,0:T(8,128)(2,1)S(1)}, bf16[4,24,1536]{2,1,0:T(8,128)(2,1)}, u32[]{:S(2)}, u32[]{:S(2)}) collective-permute-start(bf16[4,24,1536]{2,1,0:T(8,128)(2,1)S(1)} %get-tuple-element.275), channel_id=1, source_target_pairs={{0,4},{1,5},{2,6},{3,7},{4,0},{5,1},{6,2},{7,3},{8,12},{9,13},{10,... | collective-permute-start | bytes 884744 | tf_op jit(solution)/shard_map/ppermute | solution.py:588
  234.7 28.4 %collective-permute-start.37 = (bf16[16,24,1536]{2,1,0:T(8,128)(2,1)}, bf16[16,24,1536]{2,1,0:T(8,128)(2,1)S(1)}, u32[]{:S(2)}, u32[]{:S(2)}) collective-permute-start(bf16[16,24,1536]{2,1,0:T(8,128)(2,1)} %get-tuple-element.151), channel_id=1, source_target_pairs={{0,1},{1,0},{2,3},{3,2},{4,5},{5,4},{6,7},{7,6},{8,9},{9,8},{10,11... | collective-permute-start | bytes 3538952 | tf_op jit(solution)/shard_map/ppermute | solution.py:588
  264.2 50.1 %collective-permute-start.41 = (bf16[4,24,1536]{2,1,0:T(8,128)(2,1)}, bf16[4,24,1536]{2,1,0:T(8,128)(2,1)}, u32[]{:S(2)}, u32[]{:S(2)}) collective-permute-start(bf16[4,24,1536]{2,1,0:T(8,128)(2,1)} %get-tuple-element.270), channel_id=1, source_target_pairs={{0,6},{1,7},{2,4},{3,5},{4,2},{5,3},{6,0},{7,1},{8,14},{9,15},{10,... | collective-permute-start | bytes 884744 | tf_op jit(solution)/shard_map/ppermute | solution.py:588
  265.7 48.5 %collective-permute-start.40 = (bf16[4,24,1536]{2,1,0:T(8,128)(2,1)}, bf16[4,24,1536]{2,1,0:T(8,128)(2,1)}, u32[]{:S(2)}, u32[]{:S(2)}) collective-permute-start(bf16[4,24,1536]{2,1,0:T(8,128)(2,1)} %get-tuple-element.271), channel_id=1, source_target_pairs={{0,2},{1,3},{2,0},{3,1},{4,6},{5,7},{6,4},{7,5},{8,10},{9,11},{10,... | collective-permute-start | bytes 884744 | tf_op jit(solution)/shard_map/ppermute | solution.py:588
  266.9 49.2 %collective-permute-start.39 = (bf16[4,24,1536]{2,1,0:T(8,128)(2,1)S(1)}, bf16[4,24,1536]{2,1,0:T(8,128)(2,1)}, u32[]{:S(2)}, u32[]{:S(2)}) collective-permute-start(bf16[4,24,1536]{2,1,0:T(8,128)(2,1)S(1)} %get-tuple-element.272), channel_id=1, source_target_pairs={{0,4},{1,5},{2,6},{3,7},{4,0},{5,1},{6,2},{7,3},{8,12},{9,13},{10,... | collective-permute-start | bytes 884744 | tf_op jit(solution)/shard_map/ppermute | solution.py:588
  311.6 25.3 %collective-permute-start.38 = (bf16[16,24,3200]{2,1,0:T(8,128)(2,1)}, bf16[16,24,3200]{2,1,0:T(8,128)(2,1)S(1)}, u32[]{:S(2)}, u32[]{:S(2)}) collective-permute-start(bf16[16,24,3200]{2,1,0:T(8,128)(2,1)} %get-tuple-element.172), channel_id=1, source_target_pairs={{0,1},{1,0},{2,3},{3,2},{4,5},{5,4},{6,7},{7,6},{8,9},{9,8},{10,11... | collective-permute-start | bytes 7372808 | tf_op jit(solution)/shard_map/ppermute | solution.py:588
  311.7 48.9 %collective-permute-start.67 = (bf16[24,1536]{1,0:T(8,128)(2,1)}, bf16[24,1536]{1,0:T(8,128)(2,1)}, u32[]{:S(2)}, u32[]{:S(2)}) collective-permute-start(bf16[24,1536]{1,0:T(8,128)(2,1)} %get-tuple-element.292), channel_id=1, source_target_pairs={{0,24},{1,25},{2,26},{3,27},{4,28},{5,29},{6,30},{7,31},{8,16},{9,... | collective-permute-start | bytes 221192 | tf_op jit(solution)/shard_map/ppermute | solution.py:588
  314.2 48.3 %collective-permute-start.66 = (bf16[24,1536]{1,0:T(8,128)(2,1)S(1)}, bf16[24,1536]{1,0:T(8,128)(2,1)}, u32[]{:S(2)}, u32[]{:S(2)}) collective-permute-start(bf16[24,1536]{1,0:T(8,128)(2,1)S(1)} %get-tuple-element.293), channel_id=1, source_target_pairs={{0,16},{1,17},{2,18},{3,19},{4,20},{5,21},{6,22},{7,23},{8,24},{9,... | collective-permute-start | bytes 221192 | tf_op jit(solution)/shard_map/ppermute | solution.py:588
  314.3 48.3 %collective-permute-start.65 = (bf16[24,1536]{1,0:T(8,128)(2,1)S(1)}, bf16[24,1536]{1,0:T(8,128)(2,1)}, u32[]{:S(2)}, u32[]{:S(2)}) collective-permute-start(bf16[24,1536]{1,0:T(8,128)(2,1)S(1)} %get-tuple-element.294), channel_id=1, source_target_pairs={{0,8},{1,9},{2,10},{3,11},{4,12},{5,13},{6,14},{7,15},{8,0},{9,1},... | collective-permute-start | bytes 221192 | tf_op jit(solution)/shard_map/ppermute | solution.py:588
  318.5 46.8 %collective-permute-start.64 = (bf16[24,1536]{1,0:T(8,128)(2,1)S(1)}, bf16[24,1536]{1,0:T(8,128)(2,1)}, u32[]{:S(2)}, u32[]{:S(2)}) collective-permute-start(bf16[24,1536]{1,0:T(8,128)(2,1)S(1)} %get-tuple-element.289), channel_id=1, source_target_pairs={{0,24},{1,25},{2,26},{3,27},{4,28},{5,29},{6,30},{7,31},{8,16},{9,... | collective-permute-start | bytes 221192 | tf_op jit(solution)/shard_map/ppermute | solution.py:588
  336.9 29.7 %collective-permute-start.63 = (bf16[24,1536]{1,0:T(8,128)(2,1)S(1)}, bf16[24,1536]{1,0:T(8,128)(2,1)}, u32[]{:S(2)}, u32[]{:S(2)}) collective-permute-start(bf16[24,1536]{1,0:T(8,128)(2,1)S(1)} %get-tuple-element.290), channel_id=1, source_target_pairs={{0,16},{1,17},{2,18},{3,19},{4,20},{5,21},{6,22},{7,23},{8,24},{9,... | collective-permute-start | bytes 221192 | tf_op jit(solution)/shard_map/ppermute | solution.py:588
  362.5 35.0 %collective-permute-start.49 = (bf16[16,24,1536]{2,1,0:T(8,128)(2,1)}, bf16[16,24,1536]{2,1,0:T(8,128)(2,1)S(1)}, u32[]{:S(2)}, u32[]{:S(2)}) collective-permute-start(bf16[16,24,1536]{2,1,0:T(8,128)(2,1)} %get-tuple-element.181), channel_id=1, source_target_pairs={{0,1},{1,0},{2,3},{3,2},{4,5},{5,4},{6,7},{7,6},{8,9},{9,8},{10,11... | collective-permute-start | bytes 3538952 | tf_op jit(solution)/shard_map/ppermute | solution.py:588
  362.6 17.9 %collective-permute-start.44 = (bf16[4,24,3200]{2,1,0:T(8,128)(2,1)}, bf16[4,24,3200]{2,1,0:T(8,128)(2,1)S(1)}, u32[]{:S(2)}, u32[]{:S(2)}) collective-permute-start(bf16[4,24,3200]{2,1,0:T(8,128)(2,1)} %get-tuple-element.261), channel_id=1, source_target_pairs={{0,6},{1,7},{2,4},{3,5},{4,2},{5,3},{6,0},{7,1},{8,14},{9,15},{10,... | collective-permute-start | bytes 1843208 | tf_op jit(solution)/shard_map/ppermute | solution.py:588
  365.3 27.8 %collective-permute-start.43 = (bf16[4,24,3200]{2,1,0:T(8,128)(2,1)S(1)}, bf16[4,24,3200]{2,1,0:T(8,128)(2,1)S(1)}, u32[]{:S(2)}, u32[]{:S(2)}) collective-permute-start(bf16[4,24,3200]{2,1,0:T(8,128)(2,1)S(1)} %get-tuple-element.262), channel_id=1, source_target_pairs={{0,2},{1,3},{2,0},{3,1},{4,6},{5,7},{6,4},{7,5},{8,10},{9,11},{10,... | collective-permute-start | bytes 1843208 | tf_op jit(solution)/shard_map/ppermute | solution.py:588
  366.5 26.6 %collective-permute-start.42 = (bf16[4,24,3200]{2,1,0:T(8,128)(2,1)S(1)}, bf16[4,24,3200]{2,1,0:T(8,128)(2,1)S(1)}, u32[]{:S(2)}, u32[]{:S(2)}) collective-permute-start(bf16[4,24,3200]{2,1,0:T(8,128)(2,1)S(1)} %get-tuple-element.263), channel_id=1, source_target_pairs={{0,4},{1,5},{2,6},{3,7},{4,0},{5,1},{6,2},{7,3},{8,12},{9,13},{10,... | collective-permute-start | bytes 1843208 | tf_op jit(solution)/shard_map/ppermute | solution.py:588
  367.3 33.3 %collective-permute-start.48 = (bf16[16,24,1536]{2,1,0:T(8,128)(2,1)}, bf16[16,24,1536]{2,1,0:T(8,128)(2,1)S(1)}, u32[]{:S(2)}, u32[]{:S(2)}) collective-permute-start(bf16[16,24,1536]{2,1,0:T(8,128)(2,1)} %get-tuple-element.188), channel_id=1, source_target_pairs={{0,1},{1,0},{2,3},{3,2},{4,5},{5,4},{6,7},{7,6},{8,9},{9,8},{10,11... | collective-permute-start | bytes 3538952 | tf_op jit(solution)/shard_map/ppermute | solution.py:588
  395.0 21.8 %collective-permute-start.47 = (bf16[24,3200]{1,0:T(8,128)(2,1)S(1)}, bf16[24,3200]{1,0:T(8,128)(2,1)S(1)}, u32[]{:S(2)}, u32[]{:S(2)}) collective-permute-start(bf16[24,3200]{1,0:T(8,128)(2,1)S(1)} %get-tuple-element.276), channel_id=1, source_target_pairs={{0,24},{1,25},{2,26},{3,27},{4,28},{5,29},{6,30},{7,31},{8,16},{9,... | collective-permute-start | bytes 460808 | tf_op jit(solution)/shard_map/ppermute | solution.py:588
  397.5 20.0 %collective-permute-start.46 = (bf16[24,3200]{1,0:T(8,128)(2,1)S(1)}, bf16[24,3200]{1,0:T(8,128)(2,1)S(1)}, u32[]{:S(2)}, u32[]{:S(2)}) collective-permute-start(bf16[24,3200]{1,0:T(8,128)(2,1)S(1)} %get-tuple-element.277), channel_id=1, source_target_pairs={{0,16},{1,17},{2,18},{3,19},{4,20},{5,21},{6,22},{7,23},{8,24},{9,... | collective-permute-start | bytes 460808 | tf_op jit(solution)/shard_map/ppermute | solution.py:588
  397.8 10.9 %collective-permute-start.55 = (bf16[4,24,1536]{2,1,0:T(8,128)(2,1)S(1)}, bf16[4,24,1536]{2,1,0:T(8,128)(2,1)S(1)}, u32[]{:S(2)}, u32[]{:S(2)}) collective-permute-start(bf16[4,24,1536]{2,1,0:T(8,128)(2,1)S(1)} %get-tuple-element.267), channel_id=1, source_target_pairs={{0,6},{1,7},{2,4},{3,5},{4,2},{5,3},{6,0},{7,1},{8,14},{9,15},{10,... | collective-permute-start | bytes 884744 | tf_op jit(solution)/shard_map/ppermute | solution.py:588
  399.4 14.4 %collective-permute-start.54 = (bf16[4,24,1536]{2,1,0:T(8,128)(2,1)S(1)}, bf16[4,24,1536]{2,1,0:T(8,128)(2,1)S(1)}, u32[]{:S(2)}, u32[]{:S(2)}) collective-permute-start(bf16[4,24,1536]{2,1,0:T(8,128)(2,1)S(1)} %get-tuple-element.268), channel_id=1, source_target_pairs={{0,2},{1,3},{2,0},{3,1},{4,6},{5,7},{6,4},{7,5},{8,10},{9,11},{10,... | collective-permute-start | bytes 884744 | tf_op jit(solution)/shard_map/ppermute | solution.py:588
  400.6 14.7 %collective-permute-start.53 = (bf16[4,24,1536]{2,1,0:T(8,128)(2,1)S(1)}, bf16[4,24,1536]{2,1,0:T(8,128)(2,1)S(1)}, u32[]{:S(2)}, u32[]{:S(2)}) collective-permute-start(bf16[4,24,1536]{2,1,0:T(8,128)(2,1)S(1)} %get-tuple-element.269), channel_id=1, source_target_pairs={{0,4},{1,5},{2,6},{3,7},{4,0},{5,1},{6,2},{7,3},{8,12},{9,13},{10,... | collective-permute-start | bytes 884744 | tf_op jit(solution)/shard_map/ppermute | solution.py:588
  413.8 10.8 %collective-permute-start.52 = (bf16[4,24,1536]{2,1,0:T(8,128)(2,1)S(1)}, bf16[4,24,1536]{2,1,0:T(8,128)(2,1)S(1)}, u32[]{:S(2)}, u32[]{:S(2)}) collective-permute-start(bf16[4,24,1536]{2,1,0:T(8,128)(2,1)S(1)} %get-tuple-element.264), channel_id=1, source_target_pairs={{0,6},{1,7},{2,4},{3,5},{4,2},{5,3},{6,0},{7,1},{8,14},{9,15},{10,... | collective-permute-start | bytes 884744 | tf_op jit(solution)/shard_map/ppermute | solution.py:588
  415.3 14.6 %collective-permute-start.51 = (bf16[4,24,1536]{2,1,0:T(8,128)(2,1)S(1)}, bf16[4,24,1536]{2,1,0:T(8,128)(2,1)S(1)}, u32[]{:S(2)}, u32[]{:S(2)}) collective-permute-start(bf16[4,24,1536]{2,1,0:T(8,128)(2,1)S(1)} %get-tuple-element.265), channel_id=1, source_target_pairs={{0,2},{1,3},{2,0},{3,1},{4,6},{5,7},{6,4},{7,5},{8,10},{9,11},{10,... | collective-permute-start | bytes 884744 | tf_op jit(solution)/shard_map/ppermute | solution.py:588
  416.8 13.1 %collective-permute-start.50 = (bf16[4,24,1536]{2,1,0:T(8,128)(2,1)S(1)}, bf16[4,24,1536]{2,1,0:T(8,128)(2,1)S(1)}, u32[]{:S(2)}, u32[]{:S(2)}) collective-permute-start(bf16[4,24,1536]{2,1,0:T(8,128)(2,1)S(1)} %get-tuple-element.266), channel_id=1, source_target_pairs={{0,4},{1,5},{2,6},{3,7},{4,0},{5,1},{6,2},{7,3},{8,12},{9,13},{10,... | collective-permute-start | bytes 884744 | tf_op jit(solution)/shard_map/ppermute | solution.py:588
  418.3 15.0 %collective-permute-start.61 = (bf16[24,1536]{1,0:T(8,128)(2,1)S(1)}, bf16[24,1536]{1,0:T(8,128)(2,1)S(1)}, u32[]{:S(2)}, u32[]{:S(2)}) collective-permute-start(bf16[24,1536]{1,0:T(8,128)(2,1)S(1)} %get-tuple-element.286), channel_id=1, source_target_pairs={{0,24},{1,25},{2,26},{3,27},{4,28},{5,29},{6,30},{7,31},{8,16},{9,... | collective-permute-start | bytes 221192 | tf_op jit(solution)/shard_map/ppermute | solution.py:588
  419.7 15.0 %collective-permute-start.60 = (bf16[24,1536]{1,0:T(8,128)(2,1)S(1)}, bf16[24,1536]{1,0:T(8,128)(2,1)S(1)}, u32[]{:S(2)}, u32[]{:S(2)}) collective-permute-start(bf16[24,1536]{1,0:T(8,128)(2,1)S(1)} %get-tuple-element.287), channel_id=1, source_target_pairs={{0,16},{1,17},{2,18},{3,19},{4,20},{5,21},{6,22},{7,23},{8,24},{9,... | collective-permute-start | bytes 221192 | tf_op jit(solution)/shard_map/ppermute | solution.py:588
  424.6 10.1 %collective-permute-start.59 = (bf16[24,1536]{1,0:T(8,128)(2,1)S(1)}, bf16[24,1536]{1,0:T(8,128)(2,1)S(1)}, u32[]{:S(2)}, u32[]{:S(2)}) collective-permute-start(bf16[24,1536]{1,0:T(8,128)(2,1)S(1)} %get-tuple-element.288), channel_id=1, source_target_pairs={{0,8},{1,9},{2,10},{3,11},{4,12},{5,13},{6,14},{7,15},{8,0},{9,1},... | collective-permute-start | bytes 221192 | tf_op jit(solution)/shard_map/ppermute | solution.py:588
  (57 other events, 549.8 us)

commit v2 on v1

--- a/solution.py
+++ b/solution.py
@@ -25,6 +25,8 @@
 BF = jnp.bfloat16
 F32 = jnp.float32
 
+TILE = 256
+TALL = 256
 VMEM_LIMIT = 60 * 1024 * 1024
 
 
@@ -61,14 +63,12 @@
     for own in (True, False):
         for turn in range(4):
             piece = pieces[turn if own else 4 + turn]
-            for index in range(4):
-                start = pl.multiple_of(place_ref[4 * turn + index] * UNIT, UNIT)
-                for lane, lanes, target in moves:
-                    pltpu.make_async_copy(
-                        piece.at[index, :, lane : lane + lanes],
-                        target(own).at[pl.ds(start, UNIT), :],
-                        semaphore,
-                    ).start()
+            for lane, lanes, target in moves:
+                pltpu.make_async_copy(
+                    piece.at[:, :, lane : lane + lanes],
+                    target(own).at[:, place_ref[UNITS + 4 + turn]],
+                    semaphore,
+                ).start()
 
 
 def all_arrived(ref, semaphore):
@@ -83,13 +83,14 @@
     pieces, refs = refs[:PIECES], refs[PIECES:]
     q_ref, k_ref, v_ref, o_ref, p_ref, weights_ref, vector_ref, table_ref, semaphore = refs
 
+
     @pl.when(pl.program_id(0) == 0)
     def _():
         core = place_ref[UNITS]
 
         def half(own):
             which = core if own else 1 - core
-            return weights_ref.at[1, :, pl.ds(pl.multiple_of(HALF_D * which, NARROW), HALF_D)]
+            return weights_ref.at[1, :, :, :, pl.ds(pl.multiple_of(HALF_D * which, NARROW), HALF_D)]
 
         load(
             pieces,
@@ -113,15 +114,16 @@
             for one in range(2):
                 part = unit[OWN * one : OWN * one + 16]
                 wide = jnp.concatenate([part, jnp.zeros((16, D - NARROW), F32)], axis=1)
-                vector = vector + pltpu.roll(wide, UNIT * place_ref[slot] + OWN * one, 1)
+                unit_number = 4 * (slot % 4) + place_ref[UNITS + 4 + slot // 4]
+                vector = vector + pltpu.roll(wide, UNIT * unit_number + OWN * one, 1)
         vector_ref[...] = vector
         all_arrived(weights_ref, semaphore.at[0])
 
     rows = x_ref[0]
-    queries = (dot(rows, weights_ref[0]) + vector_ref[0:1, :]).astype(BF)
+    queries = (dot(rows, weights_ref[0].reshape(D, D)) + vector_ref[0:1, :]).astype(BF)
     q_ref[0] = queries * jnp.asarray(SCALING, BF)
-    k_ref[0] = dot(rows, weights_ref[1]).astype(BF)
-    v_ref[0] = (dot(rows, weights_ref[2]) + vector_ref[1:2, :]).astype(BF)
+    k_ref[0] = dot(rows, weights_ref[1].reshape(D, D)).astype(BF)
+    v_ref[0] = (dot(rows, weights_ref[2].reshape(D, D)) + vector_ref[1:2, :]).astype(BF)
     length = rows.shape[0]
     lane = lax.broadcasted_iota(jnp.int32, (length, 128), 1)
     masks = [
@@ -169,13 +171,13 @@
         out_specs=[block] * 4
         + [
             pl.BlockSpec((1, HEADS, 2, HALF, WINDOW), lambda i: (i, 0, 0, 0, 0)),
-            whole((3, D, D)),
+            whole((3, 4, 4, UNIT, D)),
             whole((16, D)),
         ],
         out_shape=[shape] * 4
         + [
             jax.ShapeDtypeStruct((micro, HEADS, 2, HALF, WINDOW), BF),
-            jax.ShapeDtypeStruct((3, D, D), BF),
+            jax.ShapeDtypeStruct((3, 4, 4, UNIT, D), BF),
             jax.ShapeDtypeStruct((16, D), F32),
         ],
         scratch_shapes=[pltpu.VMEM((UNITS, UNIT, NARROW), BF), pltpu.SemaphoreType.DMA((2,))],
@@ -186,16 +188,9 @@
 
 
 def gelu_terms(pre):
-    size = jnp.abs(pre)
-    scale = 1.0 / (1.0 + 0.23164188 * size)
-    bell = jnp.exp(pre * pre * -0.5)
-    tail = scale * (
-        0.127414796
-        + scale * (-0.142248368 + scale * (0.7107068705 + scale * (-0.7265760135 + scale * 0.5307027145)))
-    )
-    tail = tail * bell
-    below = jnp.where(pre < 0.0, tail, 1.0 - tail)
-    return pre * below, below + pre * bell * 0.3989422804014327
+    below = 0.5 + 0.5 * lax.erf(pre * math.sqrt(0.5))
+    bell = jnp.exp2(pre * pre * (-0.5 * math.log2(math.e)))
+    return pre * below, below + (pre * (1.0 / math.sqrt(2.0 * math.pi))) * bell
 
 
 def mean_of(value):
@@ -229,7 +224,7 @@
         refs = refs[1:]
     if first:
         wo_ref, refs = refs[0], refs[1:]
-    slope_ref, weights_ref, semaphore = refs
+    slope_ref, total_ref, weights_ref, semaphore = refs
 
     @pl.when(pl.program_id(0) == 0)
     def _():
@@ -237,26 +232,20 @@
 
         def half(own):
             which = core if own else 1 - core
-            return wo_ref.at[:, pl.ds(pl.multiple_of(HALF_D * which, NARROW), HALF_D)]
+            return wo_ref.at[:, :, :, pl.ds(pl.multiple_of(HALF_D * which, NARROW), HALF_D)]
 
         for index, (slices, lane) in enumerate(layout):
             pieces = chunks[PIECES * index : PIECES * (index + 1)]
             if index == 0 and first:
                 load(pieces, place_ref, ((0, HALF_D, half),), semaphore.at[SLICES])
-            for turn, which in enumerate(slices):
-                if which < quarter:
-                    load(
-                        pieces,
-                        place_ref,
-                        (
-                            (
-                                lane + D * turn,
-                                D,
-                                lambda own, which=which: weights_ref.at[which, core if own else 1 - core],
-                            ),
-                        ),
-                        semaphore.at[which],
-                    )
+            count = min(len(slices), quarter - slices[0])
+            lanes = slice(D * slices[0], D * (slices[0] + count))
+            load(
+                pieces,
+                place_ref,
+                ((lane, D * count, lambda own, lanes=lanes: weights_ref.at[core if own else 1 - core, :, :, :, lanes]),),
+                semaphore.at[index],
+            )
         if first:
             vg_ref[...] = jnp.zeros_like(vg_ref)
         else:
@@ -265,13 +254,13 @@
     def arrived(index):
         @pl.when(pl.program_id(0) == 0)
         def _():
-            all_arrived(weights_ref.at[index], semaphore.at[index])
+            slices = layout[index][0]
+            count = min(len(slices), quarter - slices[0])
+            ref = weights_ref.at[:, :, :, :, D * slices[0] : D * (slices[0] + count)]
+            all_arrived(ref, semaphore.at[index])
 
     def vector(index):
         return vector_ref[index : index + 1, :]
-
-    def add_row(index, value):
-        vg_ref[index : index + 1, :] += jnp.sum(value, axis=0, keepdims=True)
 
     if first:
 
@@ -279,53 +268,77 @@
         def _():
             all_arrived(wo_ref, semaphore.at[SLICES])
 
+    def add_row(index, value, lanes=slice(0, D)):
+        vg_ref[index : index + 1, lanes] += jnp.sum(value, axis=0, keepdims=True)
+
     width = 192 * quarter
     padded = -(-width // 128) * 128
-    attended = o_ref[:, :padded]
-    if padded != width:
-        lane = lax.broadcasted_iota(jnp.int32, attended.shape, 1)
-        attended = jnp.where(lane < width, attended, jnp.zeros_like(attended))
-    branch = dot_last(attended, wo_ref[:, :padded]) + vector(2)
-    normed_one, inverse_one = norm_forward(x_ref[...].astype(F32) + branch)
-    first_norm = normed_one * vector(8) + vector(9)
-    low = first_norm.astype(BF)
-    x1_ref[...] = low
-    total = first_norm + vector(7)
+    length = x_ref.shape[0]
+    tops = range(0, length, TALL)
+    ones, centers = {}, {}
+    wo = wo_ref[...].reshape(D, D)[:, :padded]
+    for top in tops:
+        rows = slice(top, top + TALL)
+        attended = o_ref[rows, :padded]
+        if padded != width:
+            lane = lax.broadcasted_iota(jnp.int32, attended.shape, 1)
+            attended = jnp.where(lane < width, attended, jnp.zeros_like(attended))
+        branch = dot_last(attended, wo) + vector(2)
+        ones[top] = norm_forward(x_ref[rows, :].astype(F32) + branch)
+        first_norm = ones[top][0] * vector(8) + vector(9)
+        x1_ref[rows, :] = first_norm.astype(BF)
+        total_ref[rows, :] = first_norm + vector(7)
     for index in range(quarter):
-        cols = slice(D * index, D * (index + 1))
-        arrived(index)
-        pre = dot(low, weights_ref[index, 0]) + vector(3 + index)
-        value, slope = gelu_terms(pre)
-        value = value.astype(BF)
-        g_ref[:, cols] = value
-        slope_ref[:, cols] = slope
-        total = total + dot_last(value, weights_ref[index, 1])
-    normed_two, inverse_two = norm_forward(total)
-    upstream = cotangent_ref[...].astype(F32)
-    if quarter == SLICES:
-        out_ref[...] = (normed_two * vector(10) + vector(11)).astype(BF)
-    add_row(11, upstream)
-    add_row(10, upstream * normed_two)
-    grad = norm_backward(upstream * vector(10), normed_two, inverse_two)
-    low = grad.astype(BF)
-    dm_ref[...] = low
-    add_row(7, low.astype(F32))
+        for number, (slices, _) in enumerate(layout):
+            if slices[0] == index:
+                arrived(number)
+        for top in range(0, length, TILE):
+            for column in range(D * index, D * (index + 1), TILE):
+                rows, cols = slice(top, top + TILE), slice(column, column + TILE)
+                lanes = slice(column % D, column % D + TILE)
+                matrix = weights_ref[0, :, :, :, cols].reshape(D, TILE)
+                pre = dot(x1_ref[rows, :], matrix) + vector_ref[3 + index : 4 + index, lanes]
+                value, slope = gelu_terms(pre)
+                g_ref[rows, cols] = value.astype(BF)
+                slope_ref[rows, cols] = slope
+    down = weights_ref[1].reshape(D, D * quarter)
+    for top in tops:
+        rows = slice(top, top + TALL)
+        normed, inverse = norm_forward(total_ref[rows, :] + dot_last(g_ref[rows, :], down))
+        upstream = cotangent_ref[rows, :].astype(F32)
+        if quarter == SLICES:
+            out_ref[rows, :] = (normed * vector(10) + vector(11)).astype(BF)
+            add_row(11, upstream * float(SLICES))
+        add_row(10, upstream * normed)
+        grad = norm_backward(upstream * vector(10), normed, inverse)
+        low = grad.astype(BF)
+        dm_ref[rows, :] = low
+        add_row(7, low.astype(F32))
+        total_ref[rows, :] = grad
     for index in range(quarter):
-        cols = slice(D * index, D * (index + 1))
-        pre = (dot(low, weights_ref[index, 1]) * slope_ref[:, cols]).astype(BF)
-        du_ref[:, cols] = pre
-        add_row(3 + index, pre.astype(F32))
-        grad = grad + dot_last(pre, weights_ref[index, 0])
-    add_row(9, grad)
-    add_row(8, grad * normed_one)
-    grad = norm_backward(grad * vector(8), normed_one, inverse_one)
-    low = grad.astype(BF)
-    da_ref[...] = low
-    add_row(2, low.astype(F32))
-    if first:
-        dh1_ref[...] = grad
-    else:
-        dh1_ref[...] = before_ref[...] + grad
+        for top in range(0, length, TILE):
+            for column in range(D * index, D * (index + 1), TILE):
+                rows, cols = slice(top, top + TILE), slice(column, column + TILE)
+                lanes = slice(column % D, column % D + TILE)
+                matrix = weights_ref[1, :, :, :, cols].reshape(D, TILE)
+                pre = (dot(dm_ref[rows, :], matrix) * slope_ref[rows, cols]).astype(BF)
+                du_ref[rows, cols] = pre
+                add_row(3 + index, pre.astype(F32), lanes)
+    up = weights_ref[0].reshape(D, D * quarter)
+    for top in tops:
+        rows = slice(top, top + TALL)
+        normed, inverse = ones[top]
+        grad = total_ref[rows, :] + dot_last(du_ref[rows, :], up)
+        add_row(9, grad)
+        add_row(8, grad * normed)
+        grad = norm_backward(grad * vector(8), normed, inverse)
+        low = grad.astype(BF)
+        da_ref[rows, :] = low
+        add_row(2, low.astype(F32))
+        if first:
+            dh1_ref[rows, :] = grad
+        else:
+            dh1_ref[rows, :] = before_ref[rows, :] + grad
 
 
 def ffn(quarter, place, inputs, attended, cotangent, vector, wo, chunks, before, block=512):
@@ -341,7 +354,7 @@
     in_specs = [pl.BlockSpec(memory_space=pltpu.SMEM), rows, rows, rows, whole((16, D))]
     args = [place, inputs, attended, cotangent, vector]
     if not first:
-        in_specs.append(whole((D, D)))
+        in_specs.append(whole((4, 4, UNIT, D)))
         args.append(wo)
     for chunk in chunks:
         in_specs += [anywhere] * PIECES
@@ -363,8 +376,8 @@
         out_specs.append(rows)
         out_shape.append(low)
     if first:
-        out_specs.append(whole((D, D)))
-        out_shape.append(jax.ShapeDtypeStruct((D, D), BF))
+        out_specs.append(whole((4, 4, UNIT, D)))
+        out_shape.append(jax.ShapeDtypeStruct((4, 4, UNIT, D), BF))
     layout = [(chunk[1], chunk[2]) for chunk in chunks]
     return pl.pallas_call(
         partial(ffn_kernel, quarter, first, layout),
@@ -374,7 +387,8 @@
         out_shape=out_shape,
         scratch_shapes=[
             pltpu.VMEM((block, hidden), F32),
-            pltpu.VMEM((quarter, 2, D, D), BF),
+            pltpu.VMEM((block, D), F32),
+            pltpu.VMEM((2, 4, 4, UNIT, hidden), BF),
             pltpu.SemaphoreType.DMA((SLICES + 1,)),
         ],
         compiler_params=params(),
@@ -383,87 +397,94 @@
     )(*args)
 
 
-def share(total_ref, place_ref, send_ref, keep_ref, lanes):
+def blocks():
+    for plane in range(4):
+        for along in range(4):
+            start = UNIT * (4 * along + plane)
+            yield plane, along, slice(start, start + UNIT)
+
+
+def ffn_gradient_kernel(column, count, place_ref, *refs):
+    inputs, refs = refs[: 4 * count], refs[4 * count :]
+    send_ref, keep_ref, x1_ref, du_ref, dm_ref, g_ref, total_ref, semaphore, keep_semaphore = refs
+    size = inputs[0].shape[0]
+    cols = slice(D * column, D * (column + 1))
+
+    def copies(index, turn):
+        rows = slice(size * index, size * (index + 1))
+        low, grad, value, pre = inputs[4 * index : 4 * index + 4]
+        pairs = (((low, x1_ref), (pre.at[:, cols], du_ref)), ((grad, dm_ref), (value.at[:, cols], g_ref)))[turn]
+        return [pltpu.make_async_copy(source, target.at[rows], semaphore.at[index, turn]) for source, target in pairs]
+
+    def start(index, turn):
+        for copy in copies(index, turn):
+            copy.start()
+
+    order = [(index, turn) for index in range(count) for turn in range(2)]
+    for item in order[:1]:
+        start(*item)
+    for number, (index, turn) in enumerate(order):
+        for copy in copies(index, turn):
+            copy.wait()
+        for item in order[2 * number + 1 : 2 * number + 3]:
+            start(*item)
+        rows = slice(size * index, size * (index + 1))
+        left, right = ((x1_ref, du_ref), (dm_ref, g_ref))[turn]
+        product = dot_first(left[rows, :], right[rows, :])
+        if index == 0:
+            total_ref[turn] = product
+        else:
+            total_ref[turn] += product
     core = place_ref[UNITS]
-    for slot in range(UNITS):
-        start = UNIT * place_ref[slot]
-        other = total_ref[pl.ds(pl.multiple_of(start + OWN * (1 - core), 8), OWN), :]
-        send_ref[slot, :, lanes] = other.astype(BF)
-        keep_ref[slot, :, lanes] = total_ref[pl.ds(pl.multiple_of(start + OWN * core, 8), OWN), :]
-
-
-def ffn_gradient_kernel(count, steps, *refs):
-    place_ref, refs = refs[0], refs[1:]
-    inputs, refs = refs[: 4 * count], refs[4 * count :]
-    send_ref, keep_ref, up_ref, down_ref = refs
-    step = pl.program_id(0)
-
-    @pl.when(step == 0)
-    def _():
-        up_ref[...] = jnp.zeros_like(up_ref)
-        down_ref[...] = jnp.zeros_like(down_ref)
-
-    for index in range(count):
-        x1_ref, dm_ref, g_ref, du_ref = inputs[4 * index : 4 * index + 4]
-
-        @pl.when(step // steps == index)
-        def _():
-            up_ref[...] += dot_first(x1_ref[...], du_ref[...])
-            down_ref[...] += dot_first(dm_ref[...], g_ref[...])
-
-    @pl.when(step == count * steps - 1)
-    def _():
-        for index, ref in enumerate((up_ref, down_ref)):
-            share(ref, place_ref, send_ref, keep_ref, slice(D * index, D * (index + 1)))
-
-
-def ffn_gradient(column, place, states, block=512):
+    for plane, along, rows in blocks():
+        pltpu.make_async_copy(total_ref.at[core, rows], keep_ref.at[plane, along], keep_semaphore).start()
+    for plane, along, rows in blocks():
+        send_ref[plane, along] = total_ref[1 - core, rows, :].astype(BF)
+    all_arrived(keep_ref, keep_semaphore)
+
+
+def ffn_gradient(column, place, states):
     tokens = states[0][0].shape[0]
-    steps = tokens // block
     count = len(states)
-    in_specs, args = [pl.BlockSpec(memory_space=pltpu.SMEM)], [place]
-    for index, state in enumerate(states):
-        def narrow(i, index=index):
-            return (jnp.clip(i - index * steps, 0, steps - 1), 0)
-
-        def wide(i, index=index):
-            return (jnp.clip(i - index * steps, 0, steps - 1), column)
-
-        in_specs += [
-            pl.BlockSpec((block, D), narrow),
-            pl.BlockSpec((block, D), narrow),
-            pl.BlockSpec((block, D), wide),
-            pl.BlockSpec((block, D), wide),
-        ]
-        args += list(state)
+    anywhere = pl.BlockSpec(memory_space=pl.ANY)
     return pl.pallas_call(
-        partial(ffn_gradient_kernel, count, steps),
-        grid=(count * steps,),
-        in_specs=in_specs,
-        out_specs=[whole((UNITS, OWN, 2 * D))] * 2,
-        out_shape=[
-            jax.ShapeDtypeStruct((UNITS, OWN, 2 * D), BF),
-            jax.ShapeDtypeStruct((UNITS, OWN, 2 * D), F32),
-        ],
-        scratch_shapes=[pltpu.VMEM((D, D), F32)] * 2,
+        partial(ffn_gradient_kernel, column, count),
+        in_specs=[pl.BlockSpec(memory_space=pltpu.SMEM)] + [anywhere] * (4 * count),
+        out_specs=[pl.BlockSpec(memory_space=pltpu.VMEM), anywhere],
+        out_shape=[jax.ShapeDtypeStruct((4, 4, UNIT, D), BF), jax.ShapeDtypeStruct((4, 4, UNIT, D), F32)],
+        scratch_shapes=[pltpu.VMEM((count * tokens, D), BF)] * 4
+        + [pltpu.VMEM((2, D, D), F32), pltpu.SemaphoreType.DMA((count, 2)), pltpu.SemaphoreType.DMA],
+        compiler_params=params(),
         cost_estimate=cost(count * 5e9, 20e6),
-        compiler_params=params(),
         name=f"ffn_gradient_{column}",
-    )(*args)
+    )(place, *[value for state in states for value in state])
 
 
 def attention_backward_kernel(
-    place_ref, x_ref, q_ref, k_ref, v_ref, o_ref, p_ref, da4_ref, da3_ref, da2_ref, da1_ref, dh1_ref, weights_ref, wo_ref,
+    place_ref, x_ref, q_ref, k_ref, v_ref, o_ref, p_hbm_ref, da4_ref, da3_ref, da2_ref, da1_ref, dh1_ref, weights_hbm_ref, wo_ref,
     vg_ref, *refs
 ):
     (
         dx_ref, send_ref, keep_ref, dw_ref, table_ref, do_ref, sum_ref, dq_ref, dk_ref, dv_ref,
+        p_ref, weights_ref, semaphore,
     ) = refs
+
+    step = pl.program_id(0)
+
+    def probabilities(row):
+        slot = lax.rem(row, 2)
+        return pltpu.make_async_copy(p_hbm_ref.at[row], p_ref.at[slot], semaphore.at[slot])
 
     @pl.when(pl.program_id(0) == 0)
     def _():
         dw_ref[...] = jnp.zeros_like(dw_ref)
         table_ref[...] = vg_ref[...]
+        probabilities(0).start()
+        pltpu.make_async_copy(weights_hbm_ref, weights_ref, semaphore.at[2]).start()
+
+    @pl.when(step + 1 < pl.num_programs(0))
+    def _():
+        probabilities(step + 1).start()
 
     length = x_ref.shape[1]
     running = da4_ref[0].astype(F32)
@@ -486,6 +507,8 @@
             sum_ref[block], jnp.where(lane < edge, attended, nothing)
         ) + dot_first(sum_ref[block + 1], jnp.where(lane < edge, nothing, attended))
     lane = lax.broadcasted_iota(jnp.int32, (length, 128), 1)
+    probabilities(step).wait()
+    slot = lax.rem(step, 2)
     dv_ref[...] = jnp.zeros_like(dv_ref)
     dk_ref[...] = jnp.zeros_like(dk_ref)
     for pair in range(PAIRS):
@@ -505,7 +528,7 @@
             for part in range(2):
                 window = slice(128 * part, 128 * part + WINDOW)
                 rows = slice(HALF * part, HALF * (part + 1))
-                low = p_ref[0, 2 * pair + side, part]
+                low = p_ref[slot, 2 * pair + side, part]
                 dp = dot_last(do_one[rows], v_pair[window])
                 prob = low.astype(F32)
                 mixed = prob * dp
@@ -516,6 +539,11 @@
             results.append(jnp.concatenate(parts, axis=0))
         dq_ref[:, cols] = (jnp.where(lane >= 64, results[1], results[0]) * SCALING).astype(BF)
     dq = dq_ref[...]
+
+    @pl.when(step == 0)
+    def _():
+        all_arrived(weights_ref, semaphore.at[2])
+
     dk = dk_ref[...].astype(BF).T
     dv = dv_ref[...].astype(BF).T
     dx_ref[0] = (
@@ -533,35 +561,40 @@
 
     @pl.when(pl.program_id(0) == pl.num_programs(0) - 1)
     def _():
-        for index in range(4):
-            share(dw_ref.at[index], place_ref, send_ref, keep_ref, slice(D * index, D * (index + 1)))
         core = place_ref[UNITS]
-        lanes = slice(4 * D, 4 * D + NARROW)
+        for index in range(2):
+            lanes = slice(D * index, D * (index + 1))
+            for plane, along, rows in blocks():
+                keep_ref[plane, along, :, lanes] = dw_ref[2 * core + index, rows, :]
+                send_ref[plane, along, :, lanes] = dw_ref[2 * (1 - core) + index, rows, :].astype(BF)
+        lanes = slice(2 * D, 2 * D + NARROW)
         table = table_ref[...]
-        nothing = jnp.zeros((OWN - table.shape[0], NARROW), F32)
-        for slot in range(UNITS):
-            for one, ref in ((1 - core, send_ref), (core, keep_ref)):
-                turned = pltpu.roll(table, lax.rem(D - UNIT * place_ref[slot] - OWN * one, D), 1)[:, :NARROW]
-                ref[slot, :, lanes] = jnp.concatenate([turned, nothing], axis=0).astype(ref.dtype)
+        nothing = jnp.zeros((UNIT - table.shape[0], NARROW), F32)
+        for plane, along, rows in blocks():
+            turned = pltpu.roll(table, (D - rows.start) % D, 1)[:, :NARROW]
+            turned = jnp.concatenate([turned, nothing], axis=0)
+            keep_ref[plane, along, :, lanes] = turned
+            send_ref[plane, along, :, lanes] = turned.astype(BF)
 
 
 def attention_backward(place, inputs, q, k, v, o, p, das, dh1, weights, wo, table):
     micro, length, _ = inputs.shape
     block = pl.BlockSpec((1, length, D), lambda i: (i, 0, 0))
-    lanes = 4 * D + NARROW
+    anywhere = pl.BlockSpec(memory_space=pl.ANY)
+    lanes = 2 * D + NARROW
     return pl.pallas_call(
         attention_backward_kernel,
         grid=(micro,),
         in_specs=[pl.BlockSpec(memory_space=pltpu.SMEM)]
         + [block] * 5
-        + [pl.BlockSpec((1, HEADS, 2, HALF, WINDOW), lambda i: (i, 0, 0, 0, 0))]
+        + [anywhere]
         + [block] * 5
-        + [whole((3, D, D)), whole((D, D)), whole((16, D))],
-        out_specs=[block, whole((UNITS, OWN, lanes)), whole((UNITS, OWN, lanes))],
+        + [anywhere, whole((D, D)), whole((16, D))],
+        out_specs=[block, whole((4, 4, UNIT, lanes)), whole((4, 4, UNIT, lanes))],
         out_shape=[
             jax.ShapeDtypeStruct((micro, length, D), BF),
-            jax.ShapeDtypeStruct((UNITS, OWN, lanes), BF),
-            jax.ShapeDtypeStruct((UNITS, OWN, lanes), F32),
+            jax.ShapeDtypeStruct((4, 4, UNIT, lanes), BF),
+            jax.ShapeDtypeStruct((4, 4, UNIT, lanes), F32),
         ],
         scratch_shapes=[
             pltpu.VMEM((4, D, D), F32),
@@ -571,6 +604,9 @@
             pltpu.VMEM((length, D), BF),
             pltpu.VMEM((D, length), F32),
             pltpu.VMEM((D, length), F32),
+            pltpu.VMEM((2, HEADS, 2, HALF, WINDOW), BF),
+            pltpu.VMEM((3, D, D), BF),
+            pltpu.SemaphoreType.DMA((3,)),
         ],
         compiler_params=params(),
         cost_estimate=cost(40e9, 30e6),
@@ -593,14 +629,18 @@
 
 
 class Gather:
-    def __init__(self, parts, core):
+    def __init__(self, parts, core, z):
+        self.z = z
         mine = jnp.where(core == 0, parts[0], parts[1])
         theirs = flip(jnp.where(core == 0, parts[1], parts[0]), 1)
         self.unit = jnp.where(core == 0, jnp.concatenate([mine, theirs]), jnp.concatenate([theirs, mine]))
 
     def along(self, *earlier):
         self.unit = tie(self.unit, *earlier)
-        self.near = jnp.stack([self.unit if bits == 0 else flip(self.unit, bits) for bits in ALONG])
+        value = [self.unit if bits == 0 else flip(self.unit, bits) for bits in ALONG]
+        one, two = self.z % 2 == 1, self.z >= 2
+        value = [jnp.where(one, value[index ^ 1], value[index]) for index in range(4)]
+        self.near = jnp.stack([jnp.where(two, value[index ^ 2], value[index]) for index in range(4)])
 
     def plane(self, *earlier):
         self.near = tie(self.near, *earlier)
@@ -613,15 +653,16 @@
 
 
 def gather_plain(parts):
-    full = [lax.all_gather(part, AXES, axis=0, tiled=True).reshape(UNITS, UNIT, -1) for part in parts]
-    return [value[4 * turn : 4 * turn + 4] for value in full for turn in range(4)]
+    full = [lax.all_gather(part, AXES, axis=0, tiled=True).reshape(4, 4, UNIT, -1) for part in parts]
+    return [value[:, turn] for value in full for turn in range(4)]
 
 
 class Reduce:
-    def __init__(self, send, keep):
+    def __init__(self, me, send, keep, *earlier):
+        self.core, self.place, self.z = me % 2, me // 2 % 4, me // 8
         self.keep = keep
-        self.out = [send]
-        self.arrived = [flip(send, 1)]
+        self.out = [keep]
+        self.arrived = [flip(tie(send, *earlier), 1)]
 
     def wait(self, earlier):
         if earlier:
@@ -630,34 +671,49 @@
     def plane(self, *earlier):
         self.wait(earlier)
 
-        def piece(turn):
-            part = slice(4 * turn, 4 * turn + 4)
-            return self.keep[part] + self.arrived[0][part].astype(F32)
-
-        self.out = [piece(turn).astype(BF) for turn in (1, 2, 3)]
+        def piece(bits):
+            def part(value):
+                return lax.dynamic_index_in_dim(value, self.place ^ (bits // 2), 0, keepdims=False)
+
+            return part(self.keep) + part(self.arrived[0]).astype(F32)
+
+        self.out = [piece(bits).astype(BF) for bits in PLANE[1:]]
         self.total = piece(0)
         self.arrived = [flip(value, bits) for value, bits in zip(self.out, PLANE[1:])]
 
-    def along(self, *earlier):
-        self.wait(earlier)
-        total = self.total
-        for value in self.arrived:
-            total = total + value.astype(F32)
-        self.out = [total[turn].astype(BF) for turn in (1, 2, 3)]
-        self.total = total[0]
-        self.arrived = [flip(value, bits) for value, bits in zip(self.out, ALONG[1:])]
-
-    def result(self, *earlier):
-        self.wait(earlier)
+    def sum(self):
         total = self.total
         for value in self.arrived:
             total = total + value.astype(F32)
         return total
 
+    def along(self, *earlier):
+        self.wait(earlier)
+        total = self.sum()
+
+        def piece(bits):
+            return lax.dynamic_index_in_dim(total, self.z ^ (bits // 8), 0, keepdims=False)
+
+        self.out = [piece(bits).astype(BF) for bits in ALONG[1:]]
+        self.total = piece(0)
+        self.arrived = [flip(value, bits) for value, bits in zip(self.out, ALONG[1:])]
+
+    def result(self, *earlier):
+        self.wait(earlier)
+        total = self.sum().reshape(2, OWN, -1)
+        self.unit = total
+        mine = lax.dynamic_index_in_dim(total, self.core, 0, keepdims=False)
+        other = flip(lax.dynamic_index_in_dim(total, 1 - self.core, 0, keepdims=False), 1)
+        return jnp.where(self.core == 0, mine, other), jnp.where(self.core == 0, other, mine)
+
+
+def in_rows(value):
+    return value.swapaxes(0, 1).reshape(D, -1)
+
 
 class ReducePlain:
-    def __init__(self, send, keep):
-        self.send, self.keep, self.out = send, keep, [send]
+    def __init__(self, me, send, keep, *earlier):
+        self.send, self.keep, self.out, self.arrived = send, keep, [keep], []
 
     def plane(self, *earlier):
         pass
@@ -665,8 +721,10 @@
     along = plane
 
     def result(self, *earlier):
-        both = jnp.stack([self.keep.astype(BF), self.send], axis=1).reshape(D, -1)
-        return lax.psum_scatter(both, AXES, scatter_dimension=0, tiled=True).astype(F32)
+        return [
+            lax.psum_scatter(in_rows(value).astype(BF), AXES, scatter_dimension=0, tiled=True).astype(F32)
+            for value in (self.keep, self.send)
+        ]
 
 
 def update(weights_now, momentum_now, average_now, gradient, rate):
@@ -700,10 +758,12 @@
         core = me % 2
         offsets = [(plane ^ along) // 2 for plane in PLANE for along in ALONG]
         slots = me // 2 ^ jnp.asarray(offsets, jnp.int32)
+        planes = me // 2 % 4 ^ jnp.asarray([plane // 2 for plane in PLANE], jnp.int32)
     else:
         core = jnp.zeros((), jnp.int32)
         slots = jnp.arange(UNITS, dtype=jnp.int32)
-    place = jnp.concatenate([slots, jnp.full((UNITS,), core, jnp.int32)])
+        planes = jnp.arange(4, dtype=jnp.int32)
+    place = jnp.concatenate([slots, jnp.full((4,), core, jnp.int32), planes])
 
     attention_low = attention_weights.astype(BF)
     hidden_low = feedforward_weights.astype(BF)
@@ -738,25 +798,25 @@
     if paired:
         table = jnp.pad(vector_low, ((0, OWN - names), (0, NARROW - OWN)))
         parts[0] = [jnp.concatenate([part, table], axis=1) for part in parts[0]]
-        one, two, three = [Gather(part, core) for part in parts]
+        one, two, three = [Gather(part, core, me // 8) for part in parts]
         one.along()
         one.plane()
         first_pieces = one.peers()
         two.along(one.near)
         two.plane(*one.peer)
         three.along(two.near)
-        q, k, v, o, p, weights, vector = forward(first_pieces, tie(place, two.near, three.near))
-        second_pieces = two.peers(q)
+        q, k, v, o, p, weights, vector = forward(first_pieces, tie(place, two.near))
+        second_pieces = two.peers(q, three.near)
         three.plane(q, *two.peer)
         ready = three.near
     else:
         table = lax.all_gather(vector_low, AXES, axis=1, tiled=True)
         table = table.reshape(names, UNITS, 2, OWN).transpose(1, 2, 0, 3)
         table = jnp.pad(table, ((0, 0), (0, 0), (0, OWN - names), (0, NARROW - OWN)))
-        table = table.reshape(UNITS, UNIT, NARROW)
+        table = table.reshape(4, 4, UNIT, NARROW)
         first_pieces, second_pieces, third_pieces = [gather_plain(part) for part in parts]
         first_pieces = [
-            jnp.concatenate([piece, table[4 * (turn % 4) : 4 * (turn % 4) + 4]], axis=2)
+            jnp.concatenate([piece, table[:, turn % 4]], axis=2)
             for turn, piece in enumerate(first_pieces)
         ]
         q, k, v, o, p, weights, vector = forward(first_pieces, place)
@@ -785,42 +845,44 @@
     widths(1, ready)
     chunks.append((three.peers(before[0]) if paired else third_pieces, groups[1], 0))
     layer_out = split(widths(4)[7])
-    three = reduce(*gradient(3))
+    three = reduce(me, *gradient(3))
     widths(3, *three.out)
     three.plane(before[0])
-    two = reduce(*gradient(2, *three.out))
+    two = reduce(me, *gradient(2, *three.out))
     widths(2, *two.out)
     three.along(before[0])
-    two.plane(before[0])
+    two.plane(*three.out)
+    send, keep = gradient(1, *two.out)
+    two.along(keep, *three.arrived)
+    one = reduce(me, send, keep, *two.out)
+    one.plane(*two.out)
     input_grad, send, keep = attention_backward(
-        tie(place, *three.out, *two.out), inputs_rows, q, k, v, o, p,
+        tie(place, *one.out), inputs_rows, q, k, v, o, p,
         [split(states[quarter][4]) for quarter in (4, 3, 2, 1)],
-        split(before[0]), weights, wo, before[1],
+        split(before[0]), weights.reshape(3, D, D), wo.reshape(D, D), before[1],
     )
-    attention = reduce(send, keep)
-    two.along(send)
-    one = reduce(*gradient(1, *attention.out, *two.out))
-    last = one.out[0]
-    attention.plane(last)
-    zero = reduce(*gradient(0, last, *attention.out))
-    last = zero.out[0]
-    attention.along(last)
-    one.plane(*attention.out)
-    zero.plane(*one.out)
+    one.along(keep)
+    attention = reduce(me, send, keep, *one.out, *two.arrived)
+    attention.plane(*one.out)
+    send, keep = gradient(0, *attention.out)
+    attention.along(keep, *one.arrived)
+    zero = reduce(me, send, keep, *attention.out)
+    zero.plane(*attention.out)
+    three_sum, two_sum, one_sum = [value.result(*zero.out) for value in (three, two, one)]
     attention_sum = attention.result(*zero.out)
-    one.along(*zero.out)
-    zero.along(*one.out)
-    sums = [zero.result(), one.result(*zero.out), two.result(last), three.result(last)]
-
-    attention_gradient = jnp.stack([attention_sum[:, D * c : D * (c + 1)] for c in range(4)])
-    feedforward_gradient = jnp.stack(
-        [jnp.concatenate([sums[s][:, D * c : D * (c + 1)] for s in range(SLICES)], axis=1) for c in (0, 1)]
+    zero.along(*zero.out)
+    sums = [zero.result(), one_sum, two_sum, three_sum]
+
+    attention_gradient = jnp.stack(
+        [attention_sum[index // 2][:, D * (index % 2) : D * (index % 2 + 1)] for index in range(4)]
     )
+    feedforward_gradient = jnp.stack([jnp.concatenate([value[c] for value in sums], axis=1) for c in (0, 1)])
     if paired:
-        vector_gradient = attention_sum[:names, 4 * D : 4 * D + rows]
+        table = attention.unit[0, :names, 2 * D : 2 * D + UNIT]
+        vector_gradient = lax.dynamic_slice_in_dim(table, OWN * core, OWN, 1)
     else:
-        table = jnp.stack([keep, send.astype(F32)], axis=1)[:, :, :names, 4 * D : 4 * D + OWN]
-        table = table.transpose(2, 0, 1, 3).reshape(names, D)
+        table = in_rows(attention.keep)[:, 2 * D : 2 * D + UNIT].reshape(UNITS, UNIT, UNIT)[:, :names]
+        table = table.transpose(1, 0, 2).reshape(names, D)
         vector_gradient = lax.psum_scatter(table, AXES, scatter_dimension=1, tiled=True)
 
     rate = 0.05 / math.sqrt(micro * length * count)

time: 446 us -> 408 us (0.915)
  waiting for transfers between devices: 100 us -> 66.4 us
  Pallas kernels: 248 us -> 227 us
  starting transfers between devices: 67.3 us -> 75.4 us
  other arithmetic: 22.4 us -> 28 us
    ppermute x68 -> x73, waiting for transfers between devices: 100 us -> 66.4 us  [flip(): lax.ppermute(value, AXES, [(device, device ^ bits) for device in range(DE...]
    pallas_call x4, Pallas kernels: 119 us -> 98.4 us  [ffn(): pl.pallas_call(partial(ffn_kernel, quarter, first, layout), grid=(tokens...]
    ppermute x68 -> x73, starting transfers between devices: 67.3 us -> 75.4 us  [flip(): lax.ppermute(value, AXES, [(device, device ^ bits) for device in range(DE...]
    add x5 -> x9, other arithmetic: 2.24 us -> 10.1 us  [sum(): total = total + value.astype(F32)]
    another operation x9 -> x8, other arithmetic: 7.2 us -> 0.52 us  [the longest x6 0.47 us: along(): jnp.stack([jnp.where(two, value[index ^ 2], value[index]) for index in ra...]
  transfers between devices with their start and end apart: 68 -> 73, of which waited for: 24 -> 26; matrix products, arithmetic and copies ran while one was open for 4% -> 5% of each run, Pallas kernels for 45% -> 46%
where the time goes in v2:
time: 408 us; the launch traced here: 405 us
  Pallas kernels  227 us (56%)
  starting transfers between devices  75.4 us (18%)
  waiting for transfers between devices  66.4 us (16%)
  other arithmetic  28 us (7%)
  local copies, waits for them, and re-layouts  6.39 us (2%)
    pallas_call x4, Pallas kernels, ffn(): pl.pallas_call(partial(ffn_kernel, quarter, first, layout), grid=(tokens...  98.4 us
    ppermute x73, starting transfers between devices, flip(): lax.ppermute(value, AXES, [(device, device ^ bits) for device in range(DE...  75.4 us
    ppermute x73, waiting for transfers between devices, flip(): lax.ppermute(value, AXES, [(device, device ^ bits) for device in range(DE...  66.4 us
    pallas_call x4, Pallas kernels, ffn_gradient(): pl.pallas_call(partial(ffn_gradient_kernel, column, count), in_specs=[pl....  56.8 us
    pallas_call x1, Pallas kernels, attention_backward(): pl.pallas_call(attention_backward_kernel, grid=(micro,), in_specs=[pl.Blo...  41.5 us
    pallas_call x1, Pallas kernels, attention_forward(): pl.pallas_call(attention_forward_kernel, grid=(micro,), in_specs=[pl.Bloc...  30.3 us
    add x9, other arithmetic, sum(): total = total + value.astype(F32)  10.1 us
    convert_element_type x5, other arithmetic, plane(): self.out = [piece(bits).astype(BF) for bits in PLANE[1:]]  8.81 us
  transfers between devices with their start and end apart: 73, of which 26 were waited for; matrix products, arithmetic and copies ran while one was open for 5% of the time, Pallas kernels for 46%

profile of v2, /device:TPU:0, one launch (start us, length us, event | category | flops | bytes accessed | tf_op | source)
XLA Modules:
  0.0 405.0 jit_solution(4659653514695169422)
XLA Ops:
  4.3 5.1 %collective-permute-start.2 = (bf16[48,1280]{1,0:T(8,128)(2,1)S(1)}, bf16[48,1280]{1,0:T(8,128)(2,1)S(1)}, u32[]{:S(2)}, u32[]{:S(2)}) collective-permute-start(bf16[48,1280]{1,0:T(8,128)(2,1)S(1)} %maximum_select_fusion.2), channel_id=1, source_target_pairs={{0,24},{1,25},{2,26},{3,27},{4,28},{5,29},{6,30},{7,31},{8,16},{9,... | collective-permute-start | bytes 368648 | tf_op jit(solution)/shard_map/ppermute | solution.py:624
  10.2 3.4 collective-permute-done.2
  13.6 6.3 %collective-permute-done.3 = bf16[48,1280]{1,0:T(8,128)(2,1)S(1)} collective-permute-done((bf16[48,1280]{1,0:T(8,128)(2,1)S(1)}, bf16[48,1280]{1,0:T(8,128)(2,1)S(1)}, u32[]{:S(2)}, u32[]{:S(2)}) %collective-permute-start.3) | collective-permute-done | bytes 122912 | tf_op jit(solution)/shard_map/ppermute | solution.py:624
  20.1 1.6 collective-permute-start.9
  21.7 1.5 collective-permute-start.11
  23.7 2.5 collective-permute-start.5
  26.3 6.8 %collective-permute-done.5 = bf16[48,1920]{1,0:T(8,128)(2,1)S(1)} collective-permute-done((bf16[48,1920]{1,0:T(8,128)(2,1)S(1)}, bf16[48,1920]{1,0:T(8,128)(2,1)S(1)}, u32[]{:S(2)}, u32[]{:S(2)}) %collective-permute-start.5) | collective-permute-done | bytes 184352 | tf_op jit(solution)/shard_map/ppermute | solution.py:624
  33.1 5.7 %collective-permute-start.7 = (bf16[48,1920]{1,0:T(8,128)(2,1)S(1)}, bf16[48,1920]{1,0:T(8,128)(2,1)S(1)}, u32[]{:S(2)}, u32[]{:S(2)}) collective-permute-start(bf16[48,1920]{1,0:T(8,128)(2,1)S(1)} %maximum_select_fusion), channel_id=1, source_target_pairs={{0,8},{1,9},{2,10},{3,11},{4,12},{5,13},{6,14},{7,15},{8,0},{9,1},... | collective-permute-start | bytes 552968 | tf_op jit(solution)/shard_map/ppermute | solution.py:624
  40.8 3.4 collective-permute-done.11.refs_2_
  46.8 2.5 collective-permute-start.16
  50.9 1.9 collective-permute-start.18
  53.4 1.5 collective-permute-start.22
  56.9 30.3 %attention_forward.1 = (bf16[2,512,768]{2,1,0:T(8,128)(2,1)}, bf16[2,512,768]{2,1,0:T(8,128)(2,1)}, bf16[2,512,768]{2,1,0:T(8,128)(2,1)}, bf16[2,512,768]{2,1,0:...) custom-call(s32[24]{0:T(128)} %pad_add_fusion.place_ref.refs_0_, ...), custom_call_target="tpu_custom_call" | custom-call | flops 17999998976 | bytes 20000000 | tf_op jit(solution)/shard_map/attention_forward/pallas_call | solution.py:161
  89.7 2.1 collective-permute-done.21.refs_10_.refs_11_
  92.8 1.6 collective-permute-start.26
  96.4 15.4 %ffn_1.1 = (bf16[1024,768]{1,0:T(8,128)(2,1)}, bf16[1024,768]{1,0:T(8,128)(2,1)}, bf16[1024,768]{1,0:T(8,128)(2,1)}, bf16[1024,768]{1,0:T(8,128)(2,1)}, bf16[102...) custom-call(s32[24]{0:T(128)} %pad_add_fusion.place_ref.refs_0_, ...), custom_call_target="tpu_custom_call" | custom-call | flops 16999999488 | bytes 20000000 | tf_op jit(solution)/shard_map/ffn_1/pallas_call | solution.py:382
  112.4 9.8 %collective-permute-done.27.refs_16_ = bf16[4,48,1536]{2,1,0:T(8,128)(2,1)} collective-permute-done((bf16[4,48,1536]{2,1,0:T(8,128)(2,1)S(1)}, bf16[4,48,1536]{2,1,0:T(8,128)(2,1)}, u32[]{:S(2)}, u32[]{:S(2)}) %collective-permute-start.27) | collective-permute-done | bytes 589856 | tf_op jit(solution)/shard_map/ppermute | solution.py:624
  122.7 1.7 collective-permute-done.31.refs_20_
  126.1 33.9 %ffn_4.1 = (bf16[1024,768]{1,0:T(8,128)(2,1)}, bf16[1024,768]{1,0:T(8,128)(2,1)}, bf16[1024,3072]{1,0:T(8,128)(2,1)}, bf16[1024,3072]{1,0:T(8,128)(2,1)}, bf16[1...) custom-call(s32[24]{0:T(128)} %pad_add_fusion.place_ref.refs_0_, ...), custom_call_target="tpu_custom_call" | custom-call | flops 44000002048 | bytes 20000000 | tf_op jit(solution)/shard_map/ffn_4/pallas_call | solution.py:382
  160.0 8.7 %ffn_gradient_3.1 = (bf16[4,4,48,768]{3,2,1,0:T(8,128)(2,1)}, f32[4,4,48,768]{3,2,1,0:T(8,128)}) custom-call(s32[24]{0:T(128)} %pad_add_fusion.place_ref.refs_0_, bf16[1024,768]{1,0:T(8,128)(2,1)} %get-tuple-element.138.refs_0_.refs_4_.refs_8_.refs_12_, bf16[1024,768]{1,0:T(8,128)(2,1)} %get-tuple-element.139.refs_1_.refs_5_.refs_9_.refs_13_, ...), custom_call_target="tpu_custom_call" | custom-call | flops 5000000000 | bytes 20000000 | tf_op jit(solution)/shard_map/ffn_gradient_3/pallas_call | solution.py:450
  168.9 27.8 %ffn_3.1 = (bf16[1024,768]{1,0:T(8,128)(2,1)}, bf16[1024,768]{1,0:T(8,128)(2,1)}, bf16[1024,2304]{1,0:T(8,128)(2,1)}, bf16[1024,2304]{1,0:T(8,128)(2,1)}, bf16[1...) custom-call(s32[24]{0:T(128)} %pad_add_fusion.place_ref.refs_0_, bf16[1024,768]{1,0:T(8,128)(2,1)} %bitcast.253, ...), custom_call_target="tpu_custom_call" | custom-call | flops 35000000512 | bytes 20000000 | tf_op jit(solution)/shard_map/ffn_3/pallas_call | solution.py:382
  198.9 2.6 collective-permute-start.37
  201.5 12.3 %ffn_gradient_2.1 = (bf16[4,4,48,768]{3,2,1,0:T(8,128)(2,1)}, f32[4,4,48,768]{3,2,1,0:T(8,128)}) custom-call(s32[24]{0:T(128)} %pad_add_fusion.place_ref.refs_0_, bf16[1024,768]{1,0:T(8,128)(2,1)} %get-tuple-element.150.refs_0_.refs_4_.refs_8_, bf16[1024,768]{1,0:T(8,128)(2,1)} %get-tuple-element.151.refs_1_.refs_5_.refs_9_, ...), custom_call_target="tpu_custom_call" | custom-call | flops 10000000000 | bytes 20000000 | tf_op jit(solution)/shard_map/ffn_gradient_2/pallas_call | solution.py:450
  213.9 21.3 %ffn_2.1 = (bf16[1024,768]{1,0:T(8,128)(2,1)}, bf16[1024,768]{1,0:T(8,128)(2,1)}, bf16[1024,1536]{1,0:T(8,128)(2,1)}, bf16[1024,1536]{1,0:T(8,128)(2,1)}, bf16[1...) custom-call(s32[24]{0:T(128)} %pad_add_fusion.place_ref.refs_0_, bf16[1024,768]{1,0:T(8,128)(2,1)} %bitcast.254, ...), custom_call_target="tpu_custom_call" | custom-call | flops 25999998976 | bytes 20000000 | tf_op jit(solution)/shard_map/ffn_2/pallas_call | solution.py:382
  236.1 1.6 fusion.12
  238.5 4.2 %collective-permute-start.41 = (bf16[48,768]{1,0:T(8,128)(2,1)S(1)}, bf16[48,768]{1,0:T(8,128)(2,1)}, u32[]{:S(2)}, u32[]{:S(2)}) collective-permute-start(bf16[48,768]{1,0:T(8,128)(2,1)S(1)} %get-tuple-element.290), channel_id=1, source_target_pairs={{0,8},{1,9},{2,10},{3,11},{4,12},{5,13},{6,14},{7,15},{8,0},{9,1},... | collective-permute-start | bytes 221192 | tf_op jit(solution)/shard_map/ppermute | solution.py:624
  242.7 2.4 collective-permute-start.43
  247.3 2.6 collective-permute-start.40
  249.9 16.0 %ffn_gradient_1.1 = (bf16[4,4,48,768]{3,2,1,0:T(8,128)(2,1)}, f32[4,4,48,768]{3,2,1,0:T(8,128)}) custom-call(s32[24]{0:T(128)} %pad_add_fusion.place_ref.refs_0_, bf16[1024,768]{1,0:T(8,128)(2,1)} %get-tuple-element.164.refs_0_.refs_4_, bf16[1024,768]{1,0:T(8,128)(2,1)} %get-tuple-element.165.refs_1_.refs_5_, ...), custom_call_target="tpu_custom_call" | custom-call | flops 15000000512 | bytes 20000000 | tf_op jit(solution)/shard_map/ffn_gradient_1/pallas_call | solution.py:450
  272.9 2.6 collective-permute-start.47
  275.4 41.5 %attention_backward.1 = (bf16[2,512,768]{2,1,0:T(8,128)(2,1)}, bf16[4,4,48,1664]{3,2,1,0:T(8,128)(2,1)}, f32[4,4,48,1664]{3,2,1,0:T(8,128)}) custom-call(s32[24]{0:T(128)} %pad_add_fusion.place_ref.refs_0_, bf16[2,512,768]{2,1,0:T(8,128)(2,1)} %bitcast.255, bf16[2,512,768]{2,1,0:T(8,128)(2,1)} %get-tuple-element.123.q_ref, ...), custom_call_target="tpu_custom_call" | custom-call | flops 40000000000 | bytes 30000000 | tf_op jit(solution)/shard_map/attention_backward/pallas_call | solution.py:585
  316.9 1.5 collective-permute-start.50
  319.8 3.6 collective-permute-done.50
  323.5 2.0 collective-permute-start.56
  325.5 2.4 collective-permute-start.57
  328.2 4.4 %fusion.4 = (bf16[4,48,1664]{2,1,0:T(8,128)(2,1)S(1)}, bf16[4,48,1664]{2,1,0:T(8,128)(2,1)}, bf16[4,48,1664]{2,1,0:T(8,128)(2,1)}) fusion(f32[4,4,48,1664]{3,2,1,0:T(8,128)} %get-tuple-element.186, s32[]{:T(128)S(6)} %select_n.428, bf16[4,4,48,1664]{3,2,1,0:T(8,128)(2,1)S(1)} %collective-permute-done.51, s32[]{:T(128)S(6)} %select_n.427, s32[]{:T(128)S(6)} %select_n.426), kind=kLoop, calls=%fused_computation.9 | loop fusion | flops 2875392 | bytes 7667724 | tf_op jit(solution)/shard_map/convert_element_type | solution.py:680
  333.5 2.6 collective-permute-start.54
  336.1 19.7 %ffn_gradient_0.1 = (bf16[4,4,48,768]{3,2,1,0:T(8,128)(2,1)}, f32[4,4,48,768]{3,2,1,0:T(8,128)}) custom-call(s32[24]{0:T(128)} %pad_add_fusion.place_ref.refs_0_, bf16[1024,768]{1,0:T(8,128)(2,1)} %get-tuple-element.194.refs_0_, bf16[1024,768]{1,0:T(8,128)(2,1)} %get-tuple-element.195.refs_1_, bf16[1024,768]{1,0:T(8,128)(2,1)} %get-tuple-element.196.refs_2_, ...), custom_call_target="tpu_custom_call" | custom-call | flops 20000000000 | bytes 20000000 | tf_op jit(solution)/shard_map/ffn_gradient_0/pallas_call | solution.py:450
  355.8 7.3 %collective-permute-done.53 = bf16[4,48,1664]{2,1,0:T(8,128)(2,1)S(1)} collective-permute-done((bf16[4,48,1664]{2,1,0:T(8,128)(2,1)}, bf16[4,48,1664]{2,1,0:T(8,128)(2,1)S(1)}, u32[]{:S(2)}, u32[]{:S(2)}) %collective-permute-start.53) | collective-permute-done | bytes 639008 | tf_op jit(solution)/shard_map/ppermute | solution.py:624
  364.0 2.4 fusion.1
  366.6 2.0 collective-permute-start.59
  368.6 2.4 collective-permute-start.60
  371.0 1.9 fusion.26
  373.0 1.6 collective-permute-start.63
  376.9 4.6 %collective-permute-done.59 = bf16[48,1664]{1,0:T(8,128)(2,1)} collective-permute-done((bf16[48,1664]{1,0:T(8,128)(2,1)S(1)}, bf16[48,1664]{1,0:T(8,128)(2,1)}, u32[]{:S(2)}, u32[]{:S(2)}) %collective-permute-start.59) | collective-permute-done | bytes 159776 | tf_op jit(solution)/shard_map/ppermute | solution.py:624
  390.5 1.5 collective-permute-start.68
  392.0 3.0 collective-permute-start.67
  396.8 4.4 %collective-permute-done.67 = bf16[48,768]{1,0:T(8,128)(2,1)S(1)} collective-permute-done((bf16[48,768]{1,0:T(8,128)(2,1)S(1)}, bf16[48,768]{1,0:T(8,128)(2,1)S(1)}, u32[]{:S(2)}, u32[]{:S(2)}) %collective-permute-start.67) | collective-permute-done | bytes 73760 | tf_op jit(solution)/shard_map/ppermute | solution.py:624
  (284 shorter events, 55.1 us)
Async XLA Ops:
  4.1 19.5 %collective-permute-start = (bf16[24,1920]{1,0:T(8,128)(2,1)S(1)}, bf16[24,1920]{1,0:T(8,128)(2,1)S(1)}, u32[]{:S(2)}, u32[]{:S(2)}) collective-permute-start(bf16[24,1920]{1,0:T(8,128)(2,1)S(1)} %get-tuple-element.318), channel_id=1, source_target_pairs={{0,1},{1,0},{2,3},{3,2},{4,5},{5,4},{6,7},{7,6},{8,9},{9,8},{10,11... | collective-permute-start | bytes 276488 | tf_op jit(solution)/shard_map/ppermute | solution.py:624
  4.3 9.3 %collective-permute-start.2 = (bf16[48,1280]{1,0:T(8,128)(2,1)S(1)}, bf16[48,1280]{1,0:T(8,128)(2,1)S(1)}, u32[]{:S(2)}, u32[]{:S(2)}) collective-permute-start(bf16[48,1280]{1,0:T(8,128)(2,1)S(1)} %maximum_select_fusion.2), channel_id=1, source_target_pairs={{0,24},{1,25},{2,26},{3,27},{4,28},{5,29},{6,30},{7,31},{8,16},{9,... | collective-permute-start | bytes 368648 | tf_op jit(solution)/shard_map/ppermute | solution.py:624
  9.4 10.6 %collective-permute-start.3 = (bf16[48,1280]{1,0:T(8,128)(2,1)S(1)}, bf16[48,1280]{1,0:T(8,128)(2,1)S(1)}, u32[]{:S(2)}, u32[]{:S(2)}) collective-permute-start(bf16[48,1280]{1,0:T(8,128)(2,1)S(1)} %maximum_select_fusion.2), channel_id=1, source_target_pairs={{0,16},{1,17},{2,18},{3,19},{4,20},{5,21},{6,22},{7,23},{8,24},{9,... | collective-permute-start | bytes 368648 | tf_op jit(solution)/shard_map/ppermute | solution.py:624
  9.4 10.6 %collective-permute-start.4 = (bf16[48,1280]{1,0:T(8,128)(2,1)S(1)}, bf16[48,1280]{1,0:T(8,128)(2,1)S(1)}, u32[]{:S(2)}, u32[]{:S(2)}) collective-permute-start(bf16[48,1280]{1,0:T(8,128)(2,1)S(1)} %maximum_select_fusion.2), channel_id=1, source_target_pairs={{0,8},{1,9},{2,10},{3,11},{4,12},{5,13},{6,14},{7,15},{8,0},{9,1},... | collective-permute-start | bytes 368648 | tf_op jit(solution)/shard_map/ppermute | solution.py:624
  10.1 16.2 %collective-permute-start.15 = (bf16[24,1536]{1,0:T(8,128)(2,1)S(1)}, bf16[24,1536]{1,0:T(8,128)(2,1)S(1)}, u32[]{:S(2)}, u32[]{:S(2)}) collective-permute-start(bf16[24,1536]{1,0:T(8,128)(2,1)S(1)} %get-tuple-element.324), channel_id=1, source_target_pairs={{0,1},{1,0},{2,3},{3,2},{4,5},{5,4},{6,7},{7,6},{8,9},{9,8},{10,11... | collective-permute-start | bytes 221192 | tf_op jit(solution)/shard_map/ppermute | solution.py:624
  20.1 20.2 %collective-permute-start.9 = (bf16[4,48,1280]{2,1,0:T(8,128)(2,1)S(1)}, bf16[4,48,1280]{2,1,0:T(8,128)(2,1)S(1)}, u32[]{:S(2)}, u32[]{:S(2)}) collective-permute-start(bf16[4,48,1280]{2,1,0:T(8,128)(2,1)S(1)} %pad_maximum_fusion.3.refs_0_), channel_id=1, source_target_pairs={{0,4},{1,5},{2,6},{3,7},{4,0},{5,1},{6,2},{7,3},{8,12},{9,13},{10,... | collective-permute-start | bytes 1474568 | tf_op jit(solution)/shard_map/ppermute | solution.py:624
  21.7 22.6 %collective-permute-start.11 = (bf16[4,48,1280]{2,1,0:T(8,128)(2,1)S(1)}, bf16[4,48,1280]{2,1,0:T(8,128)(2,1)S(1)}, u32[]{:S(2)}, u32[]{:S(2)}) collective-permute-start(bf16[4,48,1280]{2,1,0:T(8,128)(2,1)S(1)} %pad_maximum_fusion.3.refs_0_), channel_id=1, source_target_pairs={{0,2},{1,3},{2,0},{3,1},{4,6},{5,7},{6,4},{7,5},{8,10},{9,11},{10,... | collective-permute-start | bytes 1474568 | tf_op jit(solution)/shard_map/ppermute | solution.py:624
  23.2 21.1 %collective-permute-start.13 = (bf16[4,48,1280]{2,1,0:T(8,128)(2,1)S(1)}, bf16[4,48,1280]{2,1,0:T(8,128)(2,1)S(1)}, u32[]{:S(2)}, u32[]{:S(2)}) collective-permute-start(bf16[4,48,1280]{2,1,0:T(8,128)(2,1)S(1)} %pad_maximum_fusion.3.refs_0_), channel_id=1, source_target_pairs={{0,6},{1,7},{2,4},{3,5},{4,2},{5,3},{6,0},{7,1},{8,14},{9,15},{10,... | collective-permute-start | bytes 1474568 | tf_op jit(solution)/shard_map/ppermute | solution.py:624
  23.7 9.4 %collective-permute-start.5 = (bf16[48,1920]{1,0:T(8,128)(2,1)S(1)}, bf16[48,1920]{1,0:T(8,128)(2,1)S(1)}, u32[]{:S(2)}, u32[]{:S(2)}) collective-permute-start(bf16[48,1920]{1,0:T(8,128)(2,1)S(1)} %maximum_select_fusion), channel_id=1, source_target_pairs={{0,24},{1,25},{2,26},{3,27},{4,28},{5,29},{6,30},{7,31},{8,16},{9,... | collective-permute-start | bytes 552968 | tf_op jit(solution)/shard_map/ppermute | solution.py:624
  26.2 14.1 %collective-permute-start.6 = (bf16[48,1920]{1,0:T(8,128)(2,1)S(1)}, bf16[48,1920]{1,0:T(8,128)(2,1)S(1)}, u32[]{:S(2)}, u32[]{:S(2)}) collective-permute-start(bf16[48,1920]{1,0:T(8,128)(2,1)S(1)} %maximum_select_fusion), channel_id=1, source_target_pairs={{0,16},{1,17},{2,18},{3,19},{4,20},{5,21},{6,22},{7,23},{8,24},{9,... | collective-permute-start | bytes 552968 | tf_op jit(solution)/shard_map/ppermute | solution.py:624
  33.1 11.6 %collective-permute-start.7 = (bf16[48,1920]{1,0:T(8,128)(2,1)S(1)}, bf16[48,1920]{1,0:T(8,128)(2,1)S(1)}, u32[]{:S(2)}, u32[]{:S(2)}) collective-permute-start(bf16[48,1920]{1,0:T(8,128)(2,1)S(1)} %maximum_select_fusion), channel_id=1, source_target_pairs={{0,8},{1,9},{2,10},{3,11},{4,12},{5,13},{6,14},{7,15},{8,0},{9,1},... | collective-permute-start | bytes 552968 | tf_op jit(solution)/shard_map/ppermute | solution.py:624
  50.9 36.3 %collective-permute-start.17 = (bf16[48,1536]{1,0:T(8,128)(2,1)S(1)}, bf16[48,1536]{1,0:T(8,128)(2,1)S(1)}, u32[]{:S(2)}, u32[]{:S(2)}) collective-permute-start(bf16[48,1536]{1,0:T(8,128)(2,1)S(1)} %maximum_select_fusion.1), channel_id=1, source_target_pairs={{0,16},{1,17},{2,18},{3,19},{4,20},{5,21},{6,22},{7,23},{8,24},{9,... | collective-permute-start | bytes 442376 | tf_op jit(solution)/shard_map/ppermute | solution.py:624
  50.9 36.3 %collective-permute-start.18 = (bf16[48,1536]{1,0:T(8,128)(2,1)S(1)}, bf16[48,1536]{1,0:T(8,128)(2,1)S(1)}, u32[]{:S(2)}, u32[]{:S(2)}) collective-permute-start(bf16[48,1536]{1,0:T(8,128)(2,1)S(1)} %maximum_select_fusion.1), channel_id=1, source_target_pairs={{0,8},{1,9},{2,10},{3,11},{4,12},{5,13},{6,14},{7,15},{8,0},{9,1},... | collective-permute-start | bytes 442376 | tf_op jit(solution)/shard_map/ppermute | solution.py:624
  52.9 34.6 %collective-permute-start.20 = (bf16[4,48,1920]{2,1,0:T(8,128)(2,1)S(1)}, bf16[4,48,1920]{2,1,0:T(8,128)(2,1)S(1)}, u32[]{:S(2)}, u32[]{:S(2)}) collective-permute-start(bf16[4,48,1920]{2,1,0:T(8,128)(2,1)S(1)} %pad_maximum_fusion.refs_5_.refs_6_), channel_id=1, source_target_pairs={{0,4},{1,5},{2,6},{3,7},{4,0},{5,1},{6,2},{7,3},{8,12},{9,13},{10,... | collective-permute-start | bytes 2211848 | tf_op jit(solution)/shard_map/ppermute | solution.py:624
  53.4 34.6 %collective-permute-start.22 = (bf16[4,48,1920]{2,1,0:T(8,128)(2,1)S(1)}, bf16[4,48,1920]{2,1,0:T(8,128)(2,1)S(1)}, u32[]{:S(2)}, u32[]{:S(2)}) collective-permute-start(bf16[4,48,1920]{2,1,0:T(8,128)(2,1)S(1)} %pad_maximum_fusion.refs_5_.refs_6_), channel_id=1, source_target_pairs={{0,2},{1,3},{2,0},{3,1},{4,6},{5,7},{6,4},{7,5},{8,10},{9,11},{10,... | collective-permute-start | bytes 2211848 | tf_op jit(solution)/shard_map/ppermute | solution.py:624
  55.4 32.7 %collective-permute-start.24 = (bf16[4,48,1920]{2,1,0:T(8,128)(2,1)S(1)}, bf16[4,48,1920]{2,1,0:T(8,128)(2,1)}, u32[]{:S(2)}, u32[]{:S(2)}) collective-permute-start(bf16[4,48,1920]{2,1,0:T(8,128)(2,1)S(1)} %pad_maximum_fusion.refs_5_.refs_6_), channel_id=1, source_target_pairs={{0,6},{1,7},{2,4},{3,5},{4,2},{5,3},{6,0},{7,1},{8,14},{9,15},{10,... | collective-permute-start | bytes 2211848 | tf_op jit(solution)/shard_map/ppermute | solution.py:624
  92.8 19.1 %collective-permute-start.26 = (bf16[4,48,1536]{2,1,0:T(8,128)(2,1)S(1)}, bf16[4,48,1536]{2,1,0:T(8,128)(2,1)S(1)}, u32[]{:S(2)}, u32[]{:S(2)}) collective-permute-start(bf16[4,48,1536]{2,1,0:T(8,128)(2,1)S(1)} %pad_maximum_fusion.1.refs_14_), channel_id=1, source_target_pairs={{0,4},{1,5},{2,6},{3,7},{4,0},{5,1},{6,2},{7,3},{8,12},{9,13},{10,... | collective-permute-start | bytes 1769480 | tf_op jit(solution)/shard_map/ppermute | solution.py:624
  94.4 27.8 %collective-permute-start.27 = (bf16[4,48,1536]{2,1,0:T(8,128)(2,1)S(1)}, bf16[4,48,1536]{2,1,0:T(8,128)(2,1)}, u32[]{:S(2)}, u32[]{:S(2)}) collective-permute-start(bf16[4,48,1536]{2,1,0:T(8,128)(2,1)S(1)} %pad_maximum_fusion.1.refs_14_), channel_id=1, source_target_pairs={{0,2},{1,3},{2,0},{3,1},{4,6},{5,7},{6,4},{7,5},{8,10},{9,11},{10,... | collective-permute-start | bytes 1769480 | tf_op jit(solution)/shard_map/ppermute | solution.py:624
  94.9 27.3 %collective-permute-start.28 = (bf16[4,48,1536]{2,1,0:T(8,128)(2,1)S(1)}, bf16[4,48,1536]{2,1,0:T(8,128)(2,1)}, u32[]{:S(2)}, u32[]{:S(2)}) collective-permute-start(bf16[4,48,1536]{2,1,0:T(8,128)(2,1)S(1)} %pad_maximum_fusion.1.refs_14_), channel_id=1, source_target_pairs={{0,6},{1,7},{2,4},{3,5},{4,2},{5,3},{6,0},{7,1},{8,14},{9,15},{10,... | collective-permute-start | bytes 1769480 | tf_op jit(solution)/shard_map/ppermute | solution.py:624
  111.8 10.9 %collective-permute-start.29 = (bf16[4,48,1536]{2,1,0:T(8,128)(2,1)S(1)}, bf16[4,48,1536]{2,1,0:T(8,128)(2,1)S(1)}, u32[]{:S(2)}, u32[]{:S(2)}) collective-permute-start(bf16[4,48,1536]{2,1,0:T(8,128)(2,1)S(1)} %pad_maximum_fusion.1.refs_14_), channel_id=1, source_target_pairs={{0,1},{1,0},{2,3},{3,2},{4,5},{5,4},{6,7},{7,6},{8,9},{9,8},{10,11... | collective-permute-start | bytes 1769480 | tf_op jit(solution)/shard_map/ppermute | solution.py:624
  111.9 10.8 %collective-permute-start.30 = (bf16[4,48,1536]{2,1,0:T(8,128)(2,1)S(1)}, bf16[4,48,1536]{2,1,0:T(8,128)(2,1)S(1)}, u32[]{:S(2)}, u32[]{:S(2)}) collective-permute-start(bf16[4,48,1536]{2,1,0:T(8,128)(2,1)S(1)} %collective-permute-done.26.refs_15_), channel_id=1, source_target_pairs={{0,1},{1,0},{2,3},{3,2},{4,5},{5,4},{6,7},{7,6},{8,9},{9,8},{10,11... | collective-permute-start | bytes 1769480 | tf_op jit(solution)/shard_map/ppermute | solution.py:624
  168.7 28.0 %collective-permute-start.33 = (bf16[4,4,48,768]{3,2,1,0:T(8,128)(2,1)}, bf16[4,4,48,768]{3,2,1,0:T(8,128)(2,1)S(1)}, u32[]{:S(2)}, u32[]{:S(2)}) collective-permute-start(bf16[4,4,48,768]{3,2,1,0:T(8,128)(2,1)} %get-tuple-element.143), channel_id=1, source_target_pairs={{0,1},{1,0},{2,3},{3,2},{4,5},{5,4},{6,7},{7,6},{8,9},{9,8},{10,11... | collective-permute-start | bytes 3538952 | tf_op jit(solution)/shard_map/ppermute | solution.py:624
  198.0 37.3 %collective-permute-start.35 = (bf16[4,48,768]{2,1,0:T(8,128)(2,1)}, bf16[4,48,768]{2,1,0:T(8,128)(2,1)S(1)}, u32[]{:S(2)}, u32[]{:S(2)}) collective-permute-start(bf16[4,48,768]{2,1,0:T(8,128)(2,1)} %get-tuple-element.271), channel_id=1, source_target_pairs={{0,4},{1,5},{2,6},{3,7},{4,0},{5,1},{6,2},{7,3},{8,12},{9,13},{10,... | collective-permute-start | bytes 884744 | tf_op jit(solution)/shard_map/ppermute | solution.py:624
  198.6 36.8 %collective-permute-start.36 = (bf16[4,48,768]{2,1,0:T(8,128)(2,1)}, bf16[4,48,768]{2,1,0:T(8,128)(2,1)S(1)}, u32[]{:S(2)}, u32[]{:S(2)}) collective-permute-start(bf16[4,48,768]{2,1,0:T(8,128)(2,1)} %get-tuple-element.270), channel_id=1, source_target_pairs={{0,2},{1,3},{2,0},{3,1},{4,6},{5,7},{6,4},{7,5},{8,10},{9,11},{10,... | collective-permute-start | bytes 884744 | tf_op jit(solution)/shard_map/ppermute | solution.py:624
  198.9 36.4 %collective-permute-start.37 = (bf16[4,48,768]{2,1,0:T(8,128)(2,1)}, bf16[4,48,768]{2,1,0:T(8,128)(2,1)}, u32[]{:S(2)}, u32[]{:S(2)}) collective-permute-start(bf16[4,48,768]{2,1,0:T(8,128)(2,1)} %get-tuple-element.269), channel_id=1, source_target_pairs={{0,6},{1,7},{2,4},{3,5},{4,2},{5,3},{6,0},{7,1},{8,14},{9,15},{10,... | collective-permute-start | bytes 884744 | tf_op jit(solution)/shard_map/ppermute | solution.py:624
  213.9 31.2 %collective-permute-start.34 = (bf16[4,4,48,768]{3,2,1,0:T(8,128)(2,1)}, bf16[4,4,48,768]{3,2,1,0:T(8,128)(2,1)S(1)}, u32[]{:S(2)}, u32[]{:S(2)}) collective-permute-start(bf16[4,4,48,768]{3,2,1,0:T(8,128)(2,1)} %get-tuple-element.155), channel_id=1, source_target_pairs={{0,1},{1,0},{2,3},{3,2},{4,5},{5,4},{6,7},{7,6},{8,9},{9,8},{10,11... | collective-permute-start | bytes 3538952 | tf_op jit(solution)/shard_map/ppermute | solution.py:624
  242.7 23.2 %collective-permute-start.42 = (bf16[48,768]{1,0:T(8,128)(2,1)}, bf16[48,768]{1,0:T(8,128)(2,1)}, u32[]{:S(2)}, u32[]{:S(2)}) collective-permute-start(bf16[48,768]{1,0:T(8,128)(2,1)} %get-tuple-element.289), channel_id=1, source_target_pairs={{0,16},{1,17},{2,18},{3,19},{4,20},{5,21},{6,22},{7,23},{8,24},{9,... | collective-permute-start | bytes 221192 | tf_op jit(solution)/shard_map/ppermute | solution.py:624
  242.7 23.2 %collective-permute-start.43 = (bf16[48,768]{1,0:T(8,128)(2,1)}, bf16[48,768]{1,0:T(8,128)(2,1)}, u32[]{:S(2)}, u32[]{:S(2)}) collective-permute-start(bf16[48,768]{1,0:T(8,128)(2,1)} %get-tuple-element.288), channel_id=1, source_target_pairs={{0,24},{1,25},{2,26},{3,27},{4,28},{5,29},{6,30},{7,31},{8,16},{9,... | collective-permute-start | bytes 221192 | tf_op jit(solution)/shard_map/ppermute | solution.py:624
  246.4 19.5 %collective-permute-start.38 = (bf16[4,48,768]{2,1,0:T(8,128)(2,1)}, bf16[4,48,768]{2,1,0:T(8,128)(2,1)S(1)}, u32[]{:S(2)}, u32[]{:S(2)}) collective-permute-start(bf16[4,48,768]{2,1,0:T(8,128)(2,1)} %get-tuple-element.268), channel_id=1, source_target_pairs={{0,4},{1,5},{2,6},{3,7},{4,0},{5,1},{6,2},{7,3},{8,12},{9,13},{10,... | collective-permute-start | bytes 884744 | tf_op jit(solution)/shard_map/ppermute | solution.py:624
  246.9 19.0 %collective-permute-start.39 = (bf16[4,48,768]{2,1,0:T(8,128)(2,1)}, bf16[4,48,768]{2,1,0:T(8,128)(2,1)S(1)}, u32[]{:S(2)}, u32[]{:S(2)}) collective-permute-start(bf16[4,48,768]{2,1,0:T(8,128)(2,1)} %get-tuple-element.267), channel_id=1, source_target_pairs={{0,2},{1,3},{2,0},{3,1},{4,6},{5,7},{6,4},{7,5},{8,10},{9,11},{10,... | collective-permute-start | bytes 884744 | tf_op jit(solution)/shard_map/ppermute | solution.py:624
  247.3 18.6 %collective-permute-start.40 = (bf16[4,48,768]{2,1,0:T(8,128)(2,1)}, bf16[4,48,768]{2,1,0:T(8,128)(2,1)S(1)}, u32[]{:S(2)}, u32[]{:S(2)}) collective-permute-start(bf16[4,48,768]{2,1,0:T(8,128)(2,1)} %get-tuple-element.266), channel_id=1, source_target_pairs={{0,6},{1,7},{2,4},{3,5},{4,2},{5,3},{6,0},{7,1},{8,14},{9,15},{10,... | collective-permute-start | bytes 884744 | tf_op jit(solution)/shard_map/ppermute | solution.py:624
  268.6 51.1 %collective-permute-start.48 = (bf16[48,768]{1,0:T(8,128)(2,1)}, bf16[48,768]{1,0:T(8,128)(2,1)}, u32[]{:S(2)}, u32[]{:S(2)}) collective-permute-start(bf16[48,768]{1,0:T(8,128)(2,1)} %get-tuple-element.287), channel_id=1, source_target_pairs={{0,8},{1,9},{2,10},{3,11},{4,12},{5,13},{6,14},{7,15},{8,0},{9,1},... | collective-permute-start | bytes 221192 | tf_op jit(solution)/shard_map/ppermute | solution.py:624
  269.7 50.0 %collective-permute-start.49 = (bf16[48,768]{1,0:T(8,128)(2,1)}, bf16[48,768]{1,0:T(8,128)(2,1)}, u32[]{:S(2)}, u32[]{:S(2)}) collective-permute-start(bf16[48,768]{1,0:T(8,128)(2,1)} %get-tuple-element.286), channel_id=1, source_target_pairs={{0,16},{1,17},{2,18},{3,19},{4,20},{5,21},{6,22},{7,23},{8,24},{9,... | collective-permute-start | bytes 221192 | tf_op jit(solution)/shard_map/ppermute | solution.py:624
  271.9 45.0 %collective-permute-start.45 = (bf16[4,48,768]{2,1,0:T(8,128)(2,1)S(1)}, bf16[4,48,768]{2,1,0:T(8,128)(2,1)S(1)}, u32[]{:S(2)}, u32[]{:S(2)}) collective-permute-start(bf16[4,48,768]{2,1,0:T(8,128)(2,1)S(1)} %get-tuple-element.265), channel_id=1, source_target_pairs={{0,4},{1,5},{2,6},{3,7},{4,0},{5,1},{6,2},{7,3},{8,12},{9,13},{10,... | collective-permute-start | bytes 884744 | tf_op jit(solution)/shard_map/ppermute | solution.py:624
  272.5 46.0 %collective-permute-start.46 = (bf16[4,48,768]{2,1,0:T(8,128)(2,1)S(1)}, bf16[4,48,768]{2,1,0:T(8,128)(2,1)S(1)}, u32[]{:S(2)}, u32[]{:S(2)}) collective-permute-start(bf16[4,48,768]{2,1,0:T(8,128)(2,1)S(1)} %get-tuple-element.264), channel_id=1, source_target_pairs={{0,2},{1,3},{2,0},{3,1},{4,6},{5,7},{6,4},{7,5},{8,10},{9,11},{10,... | collective-permute-start | bytes 884744 | tf_op jit(solution)/shard_map/ppermute | solution.py:624
  272.9 45.6 %collective-permute-start.47 = (bf16[4,48,768]{2,1,0:T(8,128)(2,1)S(1)}, bf16[4,48,768]{2,1,0:T(8,128)(2,1)S(1)}, u32[]{:S(2)}, u32[]{:S(2)}) collective-permute-start(bf16[4,48,768]{2,1,0:T(8,128)(2,1)S(1)} %get-tuple-element.263), channel_id=1, source_target_pairs={{0,6},{1,7},{2,4},{3,5},{4,2},{5,3},{6,0},{7,1},{8,14},{9,15},{10,... | collective-permute-start | bytes 884744 | tf_op jit(solution)/shard_map/ppermute | solution.py:624
  323.4 10.1 %collective-permute-start.55 = (bf16[48,768]{1,0:T(8,128)(2,1)S(1)}, bf16[48,768]{1,0:T(8,128)(2,1)S(1)}, u32[]{:S(2)}, u32[]{:S(2)}) collective-permute-start(bf16[48,768]{1,0:T(8,128)(2,1)S(1)} %get-tuple-element.284), channel_id=1, source_target_pairs={{0,8},{1,9},{2,10},{3,11},{4,12},{5,13},{6,14},{7,15},{8,0},{9,1},... | collective-permute-start | bytes 221192 | tf_op jit(solution)/shard_map/ppermute | solution.py:624
  323.5 32.3 %collective-permute-start.56 = (bf16[48,768]{1,0:T(8,128)(2,1)S(1)}, bf16[48,768]{1,0:T(8,128)(2,1)S(1)}, u32[]{:S(2)}, u32[]{:S(2)}) collective-permute-start(bf16[48,768]{1,0:T(8,128)(2,1)S(1)} %get-tuple-element.283), channel_id=1, source_target_pairs={{0,16},{1,17},{2,18},{3,19},{4,20},{5,21},{6,22},{7,23},{8,24},{9,... | collective-permute-start | bytes 221192 | tf_op jit(solution)/shard_map/ppermute | solution.py:624
  325.5 30.3 %collective-permute-start.57 = (bf16[48,768]{1,0:T(8,128)(2,1)S(1)}, bf16[48,768]{1,0:T(8,128)(2,1)S(1)}, u32[]{:S(2)}, u32[]{:S(2)}) collective-permute-start(bf16[48,768]{1,0:T(8,128)(2,1)S(1)} %get-tuple-element.282), channel_id=1, source_target_pairs={{0,24},{1,25},{2,26},{3,27},{4,28},{5,29},{6,30},{7,31},{8,16},{9,... | collective-permute-start | bytes 221192 | tf_op jit(solution)/shard_map/ppermute | solution.py:624
  332.6 23.3 %collective-permute-start.52 = (bf16[4,48,1664]{2,1,0:T(8,128)(2,1)}, bf16[4,48,1664]{2,1,0:T(8,128)(2,1)S(1)}, u32[]{:S(2)}, u32[]{:S(2)}) collective-permute-start(bf16[4,48,1664]{2,1,0:T(8,128)(2,1)} %get-tuple-element.259), channel_id=1, source_target_pairs={{0,4},{1,5},{2,6},{3,7},{4,0},{5,1},{6,2},{7,3},{8,12},{9,13},{10,... | collective-permute-start | bytes 1916936 | tf_op jit(solution)/shard_map/ppermute | solution.py:624
  333.1 30.0 %collective-permute-start.53 = (bf16[4,48,1664]{2,1,0:T(8,128)(2,1)}, bf16[4,48,1664]{2,1,0:T(8,128)(2,1)S(1)}, u32[]{:S(2)}, u32[]{:S(2)}) collective-permute-start(bf16[4,48,1664]{2,1,0:T(8,128)(2,1)} %get-tuple-element.258), channel_id=1, source_target_pairs={{0,2},{1,3},{2,0},{3,1},{4,6},{5,7},{6,4},{7,5},{8,10},{9,11},{10,... | collective-permute-start | bytes 1916936 | tf_op jit(solution)/shard_map/ppermute | solution.py:624
  333.5 29.7 %collective-permute-start.54 = (bf16[4,48,1664]{2,1,0:T(8,128)(2,1)S(1)}, bf16[4,48,1664]{2,1,0:T(8,128)(2,1)}, u32[]{:S(2)}, u32[]{:S(2)}) collective-permute-start(bf16[4,48,1664]{2,1,0:T(8,128)(2,1)S(1)} %get-tuple-element.257), channel_id=1, source_target_pairs={{0,6},{1,7},{2,4},{3,5},{4,2},{5,3},{6,0},{7,1},{8,14},{9,15},{10,... | collective-permute-start | bytes 1916936 | tf_op jit(solution)/shard_map/ppermute | solution.py:624
  366.6 14.9 %collective-permute-start.59 = (bf16[48,1664]{1,0:T(8,128)(2,1)S(1)}, bf16[48,1664]{1,0:T(8,128)(2,1)}, u32[]{:S(2)}, u32[]{:S(2)}) collective-permute-start(bf16[48,1664]{1,0:T(8,128)(2,1)S(1)} %get-tuple-element.273), channel_id=1, source_target_pairs={{0,16},{1,17},{2,18},{3,19},{4,20},{5,21},{6,22},{7,23},{8,24},{9,... | collective-permute-start | bytes 479240 | tf_op jit(solution)/shard_map/ppermute | solution.py:624
  368.6 12.9 %collective-permute-start.60 = (bf16[48,1664]{1,0:T(8,128)(2,1)S(1)}, bf16[48,1664]{1,0:T(8,128)(2,1)}, u32[]{:S(2)}, u32[]{:S(2)}) collective-permute-start(bf16[48,1664]{1,0:T(8,128)(2,1)S(1)} %get-tuple-element.272), channel_id=1, source_target_pairs={{0,24},{1,25},{2,26},{3,27},{4,28},{5,29},{6,30},{7,31},{8,16},{9,... | collective-permute-start | bytes 479240 | tf_op jit(solution)/shard_map/ppermute | solution.py:624
  373.0 15.6 %collective-permute-start.63 = (bf16[4,48,768]{2,1,0:T(8,128)(2,1)S(1)}, bf16[4,48,768]{2,1,0:T(8,128)(2,1)S(1)}, u32[]{:S(2)}, u32[]{:S(2)}) collective-permute-start(bf16[4,48,768]{2,1,0:T(8,128)(2,1)S(1)} %get-tuple-element.262), channel_id=1, source_target_pairs={{0,4},{1,5},{2,6},{3,7},{4,0},{5,1},{6,2},{7,3},{8,12},{9,13},{10,... | collective-permute-start | bytes 884744 | tf_op jit(solution)/shard_map/ppermute | solution.py:624
  374.5 14.6 %collective-permute-start.64 = (bf16[4,48,768]{2,1,0:T(8,128)(2,1)S(1)}, bf16[4,48,768]{2,1,0:T(8,128)(2,1)S(1)}, u32[]{:S(2)}, u32[]{:S(2)}) collective-permute-start(bf16[4,48,768]{2,1,0:T(8,128)(2,1)S(1)} %get-tuple-element.261), channel_id=1, source_target_pairs={{0,2},{1,3},{2,0},{3,1},{4,6},{5,7},{6,4},{7,5},{8,10},{9,11},{10,... | collective-permute-start | bytes 884744 | tf_op jit(solution)/shard_map/ppermute | solution.py:624
  375.5 13.6 %collective-permute-start.65 = (bf16[4,48,768]{2,1,0:T(8,128)(2,1)S(1)}, bf16[4,48,768]{2,1,0:T(8,128)(2,1)S(1)}, u32[]{:S(2)}, u32[]{:S(2)}) collective-permute-start(bf16[4,48,768]{2,1,0:T(8,128)(2,1)S(1)} %get-tuple-element.260), channel_id=1, source_target_pairs={{0,6},{1,7},{2,4},{3,5},{4,2},{5,3},{6,0},{7,1},{8,14},{9,15},{10,... | collective-permute-start | bytes 884744 | tf_op jit(solution)/shard_map/ppermute | solution.py:624
  392.0 9.3 %collective-permute-start.67 = (bf16[48,768]{1,0:T(8,128)(2,1)S(1)}, bf16[48,768]{1,0:T(8,128)(2,1)S(1)}, u32[]{:S(2)}, u32[]{:S(2)}) collective-permute-start(bf16[48,768]{1,0:T(8,128)(2,1)S(1)} %get-tuple-element.281), channel_id=1, source_target_pairs={{0,16},{1,17},{2,18},{3,19},{4,20},{5,21},{6,22},{7,23},{8,24},{9,... | collective-permute-start | bytes 221192 | tf_op jit(solution)/shard_map/ppermute | solution.py:624
  (81 other events, 579.0 us)

commit v3 on v2

--- a/solution.py
+++ b/solution.py
@@ -131,27 +131,37 @@
         == row_ref[0, :, 128 * part : 128 * part + WINDOW]
         for part in range(2)
     ]
-    for pair in range(PAIRS):
+    items = [(side, part) for side in range(2) for part in range(2)]
+
+    def scores_of(pair):
         cols = slice(128 * pair, 128 * (pair + 1))
         q_pair = q_ref[0, :, cols]
         k_pair = k_ref[0, :, cols]
+        found = []
+        for side, part in items:
+            q_one = jnp.where((lane >= 64) == bool(side), q_pair, jnp.zeros_like(q_pair))
+            window = slice(128 * part, 128 * part + WINDOW)
+            scores = dot_last(q_one[HALF * part : HALF * (part + 1)], k_pair[window])
+            found.append(jnp.where(masks[part], scores, MASKED))
+        return found
+
+    def finish(pair, found):
+        cols = slice(128 * pair, 128 * (pair + 1))
         v_pair = v_ref[0, :, cols]
-        results = []
-        for side in range(2):
-            q_one = jnp.where((lane >= 64) == bool(side), q_pair, jnp.zeros_like(q_pair))
-            parts = []
-            for part in range(2):
-                window = slice(128 * part, 128 * part + WINDOW)
-                scores = dot_last(q_one[HALF * part : HALF * (part + 1)], k_pair[window])
-                scores = jnp.where(masks[part], scores, MASKED)
-                peak = jnp.max(scores, axis=-1, keepdims=True)
-                exponent = jnp.exp(scores - peak)
-                total = jnp.sum(exponent, axis=-1, keepdims=True)
-                low = (exponent * (1.0 / total)).astype(BF)
-                p_ref[0, 2 * pair + side, part] = low
-                parts.append(dot(low, v_pair[window]))
-            results.append(jnp.concatenate(parts, axis=0))
+        lows = []
+        for (side, part), scores in zip(items, found):
+            peak = jnp.max(scores, axis=-1, keepdims=True)
+            exponent = jnp.exp(scores - peak)
+            total = jnp.sum(exponent, axis=-1, keepdims=True)
+            low = (exponent * (1.0 / total)).astype(BF)
+            p_ref[0, 2 * pair + side, part] = low
+            lows.append(low)
+        parts = [dot(low, v_pair[128 * part : 128 * part + WINDOW]) for (side, part), low in zip(items, lows)]
+        results = [jnp.concatenate(parts[:2], axis=0), jnp.concatenate(parts[2:], axis=0)]
         o_ref[0, :, cols] = jnp.where(lane >= 64, results[1], results[0]).astype(BF)
+
+    for pair in range(PAIRS):
+        finish(pair, scores_of(pair))
 
 
 def attention_forward(inputs, documents, place, pieces):
@@ -519,24 +529,27 @@
         do_pair = do_ref[:, cols]
         q_turned = q_pair.T
         do_turned = do_pair.T
-        results = []
-        for side in range(2):
+        items = [(side, part) for side in range(2) for part in range(2)]
+        windows = [slice(128 * part, 128 * part + WINDOW) for part in range(2)]
+        halves = [slice(HALF * part, HALF * (part + 1)) for part in range(2)]
+        products = []
+        for side, part in items:
             do_one = jnp.where((lane >= 64) == bool(side), do_pair, jnp.zeros_like(do_pair))
+            products.append(dot_last(do_one[halves[part]], v_pair[windows[part]]))
+        lows = []
+        for (side, part), dp in zip(items, products):
+            prob = p_ref[slot, 2 * pair + side, part].astype(F32)
+            mixed = prob * dp
+            lows.append((mixed - prob * jnp.sum(mixed, axis=-1, keepdims=True)).astype(BF))
+        parts = []
+        for (side, part), ds in zip(items, lows):
             heads = slice(64 * side, 64 * (side + 1))
             out = slice(128 * pair + 64 * side, 128 * pair + 64 * (side + 1))
-            parts = []
-            for part in range(2):
-                window = slice(128 * part, 128 * part + WINDOW)
-                rows = slice(HALF * part, HALF * (part + 1))
-                low = p_ref[slot, 2 * pair + side, part]
-                dp = dot_last(do_one[rows], v_pair[window])
-                prob = low.astype(F32)
-                mixed = prob * dp
-                ds = (mixed - prob * jnp.sum(mixed, axis=-1, keepdims=True)).astype(BF)
-                dv_ref[out, window] += dot(do_turned[heads, rows], low)
-                dk_ref[out, window] += dot(q_turned[heads, rows], ds)
-                parts.append(dot(ds, k_pair[window]))
-            results.append(jnp.concatenate(parts, axis=0))
+            window, rows = windows[part], halves[part]
+            dv_ref[out, window] += dot(do_turned[heads, rows], p_ref[slot, 2 * pair + side, part])
+            dk_ref[out, window] += dot(q_turned[heads, rows], ds)
+            parts.append(dot(ds, k_pair[window]))
+        results = [jnp.concatenate(parts[:2], axis=0), jnp.concatenate(parts[2:], axis=0)]
         dq_ref[:, cols] = (jnp.where(lane >= 64, results[1], results[0]) * SCALING).astype(BF)
     dq = dq_ref[...]
 

time: 408 us -> 403 us (0.988)
  Pallas kernels: 227 us -> 222 us
    pallas_call x4, Pallas kernels: 98.4 us -> 111 us  [ffn(): pl.pallas_call(partial(ffn_kernel, quarter, first, layout), grid=(tokens...]
    pallas_call x1, Pallas kernels: 30.3 us -> 19.6 us  [attention_forward(): pl.pallas_call(attention_forward_kernel, grid=(micro,), in_specs=[pl.Bloc...]
    pallas_call x1, Pallas kernels: 41.5 us -> 34.2 us  [attention_backward(): pl.pallas_call(attention_backward_kernel, grid=(micro,), in_specs=[pl.Blo...]
  transfers between devices with their start and end apart: 73 -> 73, of which waited for: 26 -> 27; matrix products, arithmetic and copies ran while one was open for 5% -> 5% of each run, Pallas kernels for 46% -> 45%
where the time goes in v3:
time: 403 us; the launch traced here: 398 us
  Pallas kernels  222 us (55%)
  starting transfers between devices  75.1 us (19%)
  waiting for transfers between devices  64.6 us (16%)
  other arithmetic  28.1 us (7%)
  local copies, waits for them, and re-layouts  6.32 us (2%)
    pallas_call x4, Pallas kernels, ffn(): pl.pallas_call(partial(ffn_kernel, quarter, first, layout), grid=(tokens...  111 us
    ppermute x73, starting transfers between devices, flip(): lax.ppermute(value, AXES, [(device, device ^ bits) for device in range(DE...  75.1 us
    ppermute x73, waiting for transfers between devices, flip(): lax.ppermute(value, AXES, [(device, device ^ bits) for device in range(DE...  64.6 us
    pallas_call x4, Pallas kernels, ffn_gradient(): pl.pallas_call(partial(ffn_gradient_kernel, column, count), in_specs=[pl....  56.8 us
    pallas_call x1, Pallas kernels, attention_backward(): pl.pallas_call(attention_backward_kernel, grid=(micro,), in_specs=[pl.Blo...  34.2 us
    pallas_call x1, Pallas kernels, attention_forward(): pl.pallas_call(attention_forward_kernel, grid=(micro,), in_specs=[pl.Bloc...  19.6 us
    add x9, other arithmetic, sum(): total = total + value.astype(F32)  10.1 us
    convert_element_type x5, other arithmetic, plane(): self.out = [piece(bits).astype(BF) for bits in PLANE[1:]]  8.84 us
  transfers between devices with their start and end apart: 73, of which 27 were waited for; matrix products, arithmetic and copies ran while one was open for 5% of the time, Pallas kernels for 45%

profile of v3, /device:TPU:0, one launch (start us, length us, event | category | flops | bytes accessed | tf_op | source)
XLA Modules:
  0.0 397.7 jit_solution(966807175183079568)
XLA Ops:
  4.3 5.1 %collective-permute-start.2 = (bf16[48,1280]{1,0:T(8,128)(2,1)S(1)}, bf16[48,1280]{1,0:T(8,128)(2,1)S(1)}, u32[]{:S(2)}, u32[]{:S(2)}) collective-permute-start(bf16[48,1280]{1,0:T(8,128)(2,1)S(1)} %maximum_select_fusion.2), channel_id=1, source_target_pairs={{0,24},{1,25},{2,26},{3,27},{4,28},{5,29},{6,30},{7,31},{8,16},{9,... | collective-permute-start | bytes 368648 | tf_op jit(solution)/shard_map/ppermute | solution.py:637
  10.2 3.4 collective-permute-done.2
  13.6 6.3 %collective-permute-done.3 = bf16[48,1280]{1,0:T(8,128)(2,1)S(1)} collective-permute-done((bf16[48,1280]{1,0:T(8,128)(2,1)S(1)}, bf16[48,1280]{1,0:T(8,128)(2,1)S(1)}, u32[]{:S(2)}, u32[]{:S(2)}) %collective-permute-start.3) | collective-permute-done | bytes 122912 | tf_op jit(solution)/shard_map/ppermute | solution.py:637
  20.1 1.6 collective-permute-start.9
  21.7 1.5 collective-permute-start.11
  23.7 2.5 collective-permute-start.5
  26.3 6.8 %collective-permute-done.5 = bf16[48,1920]{1,0:T(8,128)(2,1)S(1)} collective-permute-done((bf16[48,1920]{1,0:T(8,128)(2,1)S(1)}, bf16[48,1920]{1,0:T(8,128)(2,1)S(1)}, u32[]{:S(2)}, u32[]{:S(2)}) %collective-permute-start.5) | collective-permute-done | bytes 184352 | tf_op jit(solution)/shard_map/ppermute | solution.py:637
  33.1 5.7 %collective-permute-start.7 = (bf16[48,1920]{1,0:T(8,128)(2,1)S(1)}, bf16[48,1920]{1,0:T(8,128)(2,1)S(1)}, u32[]{:S(2)}, u32[]{:S(2)}) collective-permute-start(bf16[48,1920]{1,0:T(8,128)(2,1)S(1)} %maximum_select_fusion), channel_id=1, source_target_pairs={{0,8},{1,9},{2,10},{3,11},{4,12},{5,13},{6,14},{7,15},{8,0},{9,1},... | collective-permute-start | bytes 552968 | tf_op jit(solution)/shard_map/ppermute | solution.py:637
  40.8 3.4 collective-permute-done.11.refs_2_
  46.8 2.5 collective-permute-start.16
  50.9 1.9 collective-permute-start.18
  53.4 1.5 collective-permute-start.22
  56.9 19.6 %attention_forward.1 = (bf16[2,512,768]{2,1,0:T(8,128)(2,1)}, bf16[2,512,768]{2,1,0:T(8,128)(2,1)}, bf16[2,512,768]{2,1,0:T(8,128)(2,1)}, bf16[2,512,768]{2,1,0:...) custom-call(s32[24]{0:T(128)} %pad_add_fusion.place_ref.refs_0_, ...), custom_call_target="tpu_custom_call" | custom-call | flops 17999998976 | bytes 20000000 | tf_op jit(solution)/shard_map/attention_forward/pallas_call | solution.py:171
  77.3 8.4 %collective-permute-done.22.refs_7_.refs_8_ = bf16[4,48,1920]{2,1,0:T(8,128)(2,1)S(1)} collective-permute-done((bf16[4,48,1920]{2,1,0:T(8,128)(2,1)S(1)}, bf16[4,48,1920]{2,1,0:T(8,128)(2,1)S(1)}, u32[]{:S(2)}, u32[]{:S(2)}) %collective-permute-start.22) | collective-permute-done | bytes 737312 | tf_op jit(solution)/shard_map/ppermute | solution.py:637
  85.7 1.7 collective-permute-done.24.refs_8_.refs_9_
  87.9 1.9 collective-permute-done.25.refs_12_.refs_13_
  89.8 1.7 collective-permute-start.26
  93.3 28.1 %ffn_1.1 = (bf16[1024,768]{1,0:T(8,128)(2,1)}, bf16[1024,768]{1,0:T(8,128)(2,1)}, bf16[1024,768]{1,0:T(8,128)(2,1)}, bf16[1024,768]{1,0:T(8,128)(2,1)}, bf16[102...) custom-call(s32[24]{0:T(128)} %pad_add_fusion.place_ref.refs_0_, ...), custom_call_target="tpu_custom_call" | custom-call | flops 16999999488 | bytes 20000000 | tf_op jit(solution)/shard_map/ffn_1/pallas_call | solution.py:392
  123.5 1.7 collective-permute-done.30.refs_19_
  127.1 34.1 %ffn_4.1 = (bf16[1024,768]{1,0:T(8,128)(2,1)}, bf16[1024,768]{1,0:T(8,128)(2,1)}, bf16[1024,3072]{1,0:T(8,128)(2,1)}, bf16[1024,3072]{1,0:T(8,128)(2,1)}, bf16[1...) custom-call(s32[24]{0:T(128)} %pad_add_fusion.place_ref.refs_0_, ...), custom_call_target="tpu_custom_call" | custom-call | flops 44000002048 | bytes 20000000 | tf_op jit(solution)/shard_map/ffn_4/pallas_call | solution.py:392
  161.2 8.7 %ffn_gradient_3.1 = (bf16[4,4,48,768]{3,2,1,0:T(8,128)(2,1)}, f32[4,4,48,768]{3,2,1,0:T(8,128)}) custom-call(s32[24]{0:T(128)} %pad_add_fusion.place_ref.refs_0_, bf16[1024,768]{1,0:T(8,128)(2,1)} %get-tuple-element.138.refs_0_.refs_4_.refs_8_.refs_12_, bf16[1024,768]{1,0:T(8,128)(2,1)} %get-tuple-element.139.refs_1_.refs_5_.refs_9_.refs_13_, ...), custom_call_target="tpu_custom_call" | custom-call | flops 5000000000 | bytes 20000000 | tf_op jit(solution)/shard_map/ffn_gradient_3/pallas_call | solution.py:460
  170.2 27.7 %ffn_3.1 = (bf16[1024,768]{1,0:T(8,128)(2,1)}, bf16[1024,768]{1,0:T(8,128)(2,1)}, bf16[1024,2304]{1,0:T(8,128)(2,1)}, bf16[1024,2304]{1,0:T(8,128)(2,1)}, bf16[1...) custom-call(s32[24]{0:T(128)} %pad_add_fusion.place_ref.refs_0_, bf16[1024,768]{1,0:T(8,128)(2,1)} %bitcast.253, ...), custom_call_target="tpu_custom_call" | custom-call | flops 35000000512 | bytes 20000000 | tf_op jit(solution)/shard_map/ffn_3/pallas_call | solution.py:392
  199.2 1.8 collective-permute-start.35
  202.7 12.3 %ffn_gradient_2.1 = (bf16[4,4,48,768]{3,2,1,0:T(8,128)(2,1)}, f32[4,4,48,768]{3,2,1,0:T(8,128)}) custom-call(s32[24]{0:T(128)} %pad_add_fusion.place_ref.refs_0_, bf16[1024,768]{1,0:T(8,128)(2,1)} %get-tuple-element.150.refs_0_.refs_4_.refs_8_, bf16[1024,768]{1,0:T(8,128)(2,1)} %get-tuple-element.151.refs_1_.refs_5_.refs_9_, ...), custom_call_target="tpu_custom_call" | custom-call | flops 10000000000 | bytes 20000000 | tf_op jit(solution)/shard_map/ffn_gradient_2/pallas_call | solution.py:460
  215.1 21.1 %ffn_2.1 = (bf16[1024,768]{1,0:T(8,128)(2,1)}, bf16[1024,768]{1,0:T(8,128)(2,1)}, bf16[1024,1536]{1,0:T(8,128)(2,1)}, bf16[1024,1536]{1,0:T(8,128)(2,1)}, bf16[1...) custom-call(s32[24]{0:T(128)} %pad_add_fusion.place_ref.refs_0_, bf16[1024,768]{1,0:T(8,128)(2,1)} %bitcast.254, ...), custom_call_target="tpu_custom_call" | custom-call | flops 25999998976 | bytes 20000000 | tf_op jit(solution)/shard_map/ffn_2/pallas_call | solution.py:392
  237.1 1.6 fusion.12
  239.8 2.6 collective-permute-start.42
  245.1 1.7 collective-permute-start.38
  248.6 16.0 %ffn_gradient_1.1 = (bf16[4,4,48,768]{3,2,1,0:T(8,128)(2,1)}, f32[4,4,48,768]{3,2,1,0:T(8,128)}) custom-call(s32[24]{0:T(128)} %pad_add_fusion.place_ref.refs_0_, bf16[1024,768]{1,0:T(8,128)(2,1)} %get-tuple-element.164.refs_0_.refs_4_, bf16[1024,768]{1,0:T(8,128)(2,1)} %get-tuple-element.165.refs_1_.refs_5_, ...), custom_call_target="tpu_custom_call" | custom-call | flops 15000000512 | bytes 20000000 | tf_op jit(solution)/shard_map/ffn_gradient_1/pallas_call | solution.py:460
  267.4 3.0 collective-permute-start.49
  270.7 1.8 collective-permute-start.45
  274.2 34.2 %attention_backward.1 = (bf16[2,512,768]{2,1,0:T(8,128)(2,1)}, bf16[4,4,48,1664]{3,2,1,0:T(8,128)(2,1)}, f32[4,4,48,1664]{3,2,1,0:T(8,128)}) custom-call(s32[24]{0:T(128)} %pad_add_fusion.place_ref.refs_0_, bf16[2,512,768]{2,1,0:T(8,128)(2,1)} %bitcast.255, bf16[2,512,768]{2,1,0:T(8,128)(2,1)} %get-tuple-element.123.q_ref, ...), custom_call_target="tpu_custom_call" | custom-call | flops 40000000000 | bytes 30000000 | tf_op jit(solution)/shard_map/attention_backward/pallas_call | solution.py:598
  308.4 2.5 collective-permute-start.50
  312.3 2.6 collective-permute-done.50
  315.0 3.0 collective-permute-start.56
  319.7 4.4 %fusion.4 = (bf16[4,48,1664]{2,1,0:T(8,128)(2,1)S(1)}, bf16[4,48,1664]{2,1,0:T(8,128)(2,1)}, bf16[4,48,1664]{2,1,0:T(8,128)(2,1)}) fusion(f32[4,4,48,1664]{3,2,1,0:T(8,128)} %get-tuple-element.186, s32[]{:T(128)S(6)} %select_n.428, bf16[4,4,48,1664]{3,2,1,0:T(8,128)(2,1)S(1)} %collective-permute-done.51, s32[]{:T(128)S(6)} %select_n.427, s32[]{:T(128)S(6)} %select_n.426), kind=kLoop, calls=%fused_computation.9 | loop fusion | flops 2875392 | bytes 7667724 | tf_op jit(solution)/shard_map/convert_element_type | solution.py:693
  324.1 1.7 collective-permute-start.52
  327.6 19.7 %ffn_gradient_0.1 = (bf16[4,4,48,768]{3,2,1,0:T(8,128)(2,1)}, f32[4,4,48,768]{3,2,1,0:T(8,128)}) custom-call(s32[24]{0:T(128)} %pad_add_fusion.place_ref.refs_0_, bf16[1024,768]{1,0:T(8,128)(2,1)} %get-tuple-element.194.refs_0_, bf16[1024,768]{1,0:T(8,128)(2,1)} %get-tuple-element.195.refs_1_, bf16[1024,768]{1,0:T(8,128)(2,1)} %get-tuple-element.196.refs_2_, ...), custom_call_target="tpu_custom_call" | custom-call | flops 20000000000 | bytes 20000000 | tf_op jit(solution)/shard_map/ffn_gradient_0/pallas_call | solution.py:460
  347.4 8.5 %collective-permute-done.53 = bf16[4,48,1664]{2,1,0:T(8,128)(2,1)S(1)} collective-permute-done((bf16[4,48,1664]{2,1,0:T(8,128)(2,1)}, bf16[4,48,1664]{2,1,0:T(8,128)(2,1)S(1)}, u32[]{:S(2)}, u32[]{:S(2)}) %collective-permute-start.53) | collective-permute-done | bytes 639008 | tf_op jit(solution)/shard_map/ppermute | solution.py:637
  356.7 2.4 fusion.1
  359.3 3.0 collective-permute-start.59
  363.7 1.9 fusion.26
  366.3 1.6 collective-permute-start.64
  369.0 1.5 collective-permute-start.65
  370.5 3.7 collective-permute-done.59
  382.9 2.5 collective-permute-start.68
  385.4 2.4 collective-permute-start.67
  389.2 4.7 %collective-permute-done.67 = bf16[48,768]{1,0:T(8,128)(2,1)S(1)} collective-permute-done((bf16[48,768]{1,0:T(8,128)(2,1)S(1)}, bf16[48,768]{1,0:T(8,128)(2,1)S(1)}, u32[]{:S(2)}, u32[]{:S(2)}) %collective-permute-start.67) | collective-permute-done | bytes 73760 | tf_op jit(solution)/shard_map/ppermute | solution.py:637
  (284 shorter events, 57.2 us)
Async XLA Ops:
  4.1 19.5 %collective-permute-start = (bf16[24,1920]{1,0:T(8,128)(2,1)S(1)}, bf16[24,1920]{1,0:T(8,128)(2,1)S(1)}, u32[]{:S(2)}, u32[]{:S(2)}) collective-permute-start(bf16[24,1920]{1,0:T(8,128)(2,1)S(1)} %get-tuple-element.318), channel_id=1, source_target_pairs={{0,1},{1,0},{2,3},{3,2},{4,5},{5,4},{6,7},{7,6},{8,9},{9,8},{10,11... | collective-permute-start | bytes 276488 | tf_op jit(solution)/shard_map/ppermute | solution.py:637
  4.3 9.3 %collective-permute-start.2 = (bf16[48,1280]{1,0:T(8,128)(2,1)S(1)}, bf16[48,1280]{1,0:T(8,128)(2,1)S(1)}, u32[]{:S(2)}, u32[]{:S(2)}) collective-permute-start(bf16[48,1280]{1,0:T(8,128)(2,1)S(1)} %maximum_select_fusion.2), channel_id=1, source_target_pairs={{0,24},{1,25},{2,26},{3,27},{4,28},{5,29},{6,30},{7,31},{8,16},{9,... | collective-permute-start | bytes 368648 | tf_op jit(solution)/shard_map/ppermute | solution.py:637
  9.4 10.6 %collective-permute-start.3 = (bf16[48,1280]{1,0:T(8,128)(2,1)S(1)}, bf16[48,1280]{1,0:T(8,128)(2,1)S(1)}, u32[]{:S(2)}, u32[]{:S(2)}) collective-permute-start(bf16[48,1280]{1,0:T(8,128)(2,1)S(1)} %maximum_select_fusion.2), channel_id=1, source_target_pairs={{0,16},{1,17},{2,18},{3,19},{4,20},{5,21},{6,22},{7,23},{8,24},{9,... | collective-permute-start | bytes 368648 | tf_op jit(solution)/shard_map/ppermute | solution.py:637
  9.4 10.6 %collective-permute-start.4 = (bf16[48,1280]{1,0:T(8,128)(2,1)S(1)}, bf16[48,1280]{1,0:T(8,128)(2,1)S(1)}, u32[]{:S(2)}, u32[]{:S(2)}) collective-permute-start(bf16[48,1280]{1,0:T(8,128)(2,1)S(1)} %maximum_select_fusion.2), channel_id=1, source_target_pairs={{0,8},{1,9},{2,10},{3,11},{4,12},{5,13},{6,14},{7,15},{8,0},{9,1},... | collective-permute-start | bytes 368648 | tf_op jit(solution)/shard_map/ppermute | solution.py:637
  10.1 16.2 %collective-permute-start.15 = (bf16[24,1536]{1,0:T(8,128)(2,1)S(1)}, bf16[24,1536]{1,0:T(8,128)(2,1)S(1)}, u32[]{:S(2)}, u32[]{:S(2)}) collective-permute-start(bf16[24,1536]{1,0:T(8,128)(2,1)S(1)} %get-tuple-element.324), channel_id=1, source_target_pairs={{0,1},{1,0},{2,3},{3,2},{4,5},{5,4},{6,7},{7,6},{8,9},{9,8},{10,11... | collective-permute-start | bytes 221192 | tf_op jit(solution)/shard_map/ppermute | solution.py:637
  20.1 20.2 %collective-permute-start.9 = (bf16[4,48,1280]{2,1,0:T(8,128)(2,1)S(1)}, bf16[4,48,1280]{2,1,0:T(8,128)(2,1)S(1)}, u32[]{:S(2)}, u32[]{:S(2)}) collective-permute-start(bf16[4,48,1280]{2,1,0:T(8,128)(2,1)S(1)} %pad_maximum_fusion.3.refs_0_), channel_id=1, source_target_pairs={{0,4},{1,5},{2,6},{3,7},{4,0},{5,1},{6,2},{7,3},{8,12},{9,13},{10,... | collective-permute-start | bytes 1474568 | tf_op jit(solution)/shard_map/ppermute | solution.py:637
  21.7 22.6 %collective-permute-start.11 = (bf16[4,48,1280]{2,1,0:T(8,128)(2,1)S(1)}, bf16[4,48,1280]{2,1,0:T(8,128)(2,1)S(1)}, u32[]{:S(2)}, u32[]{:S(2)}) collective-permute-start(bf16[4,48,1280]{2,1,0:T(8,128)(2,1)S(1)} %pad_maximum_fusion.3.refs_0_), channel_id=1, source_target_pairs={{0,2},{1,3},{2,0},{3,1},{4,6},{5,7},{6,4},{7,5},{8,10},{9,11},{10,... | collective-permute-start | bytes 1474568 | tf_op jit(solution)/shard_map/ppermute | solution.py:637
  23.2 21.1 %collective-permute-start.13 = (bf16[4,48,1280]{2,1,0:T(8,128)(2,1)S(1)}, bf16[4,48,1280]{2,1,0:T(8,128)(2,1)S(1)}, u32[]{:S(2)}, u32[]{:S(2)}) collective-permute-start(bf16[4,48,1280]{2,1,0:T(8,128)(2,1)S(1)} %pad_maximum_fusion.3.refs_0_), channel_id=1, source_target_pairs={{0,6},{1,7},{2,4},{3,5},{4,2},{5,3},{6,0},{7,1},{8,14},{9,15},{10,... | collective-permute-start | bytes 1474568 | tf_op jit(solution)/shard_map/ppermute | solution.py:637
  23.7 9.4 %collective-permute-start.5 = (bf16[48,1920]{1,0:T(8,128)(2,1)S(1)}, bf16[48,1920]{1,0:T(8,128)(2,1)S(1)}, u32[]{:S(2)}, u32[]{:S(2)}) collective-permute-start(bf16[48,1920]{1,0:T(8,128)(2,1)S(1)} %maximum_select_fusion), channel_id=1, source_target_pairs={{0,24},{1,25},{2,26},{3,27},{4,28},{5,29},{6,30},{7,31},{8,16},{9,... | collective-permute-start | bytes 552968 | tf_op jit(solution)/shard_map/ppermute | solution.py:637
  26.2 14.1 %collective-permute-start.6 = (bf16[48,1920]{1,0:T(8,128)(2,1)S(1)}, bf16[48,1920]{1,0:T(8,128)(2,1)S(1)}, u32[]{:S(2)}, u32[]{:S(2)}) collective-permute-start(bf16[48,1920]{1,0:T(8,128)(2,1)S(1)} %maximum_select_fusion), channel_id=1, source_target_pairs={{0,16},{1,17},{2,18},{3,19},{4,20},{5,21},{6,22},{7,23},{8,24},{9,... | collective-permute-start | bytes 552968 | tf_op jit(solution)/shard_map/ppermute | solution.py:637
  33.1 11.6 %collective-permute-start.7 = (bf16[48,1920]{1,0:T(8,128)(2,1)S(1)}, bf16[48,1920]{1,0:T(8,128)(2,1)S(1)}, u32[]{:S(2)}, u32[]{:S(2)}) collective-permute-start(bf16[48,1920]{1,0:T(8,128)(2,1)S(1)} %maximum_select_fusion), channel_id=1, source_target_pairs={{0,8},{1,9},{2,10},{3,11},{4,12},{5,13},{6,14},{7,15},{8,0},{9,1},... | collective-permute-start | bytes 552968 | tf_op jit(solution)/shard_map/ppermute | solution.py:637
  50.9 25.6 %collective-permute-start.17 = (bf16[48,1536]{1,0:T(8,128)(2,1)S(1)}, bf16[48,1536]{1,0:T(8,128)(2,1)S(1)}, u32[]{:S(2)}, u32[]{:S(2)}) collective-permute-start(bf16[48,1536]{1,0:T(8,128)(2,1)S(1)} %maximum_select_fusion.1), channel_id=1, source_target_pairs={{0,16},{1,17},{2,18},{3,19},{4,20},{5,21},{6,22},{7,23},{8,24},{9,... | collective-permute-start | bytes 442376 | tf_op jit(solution)/shard_map/ppermute | solution.py:637
  50.9 25.6 %collective-permute-start.18 = (bf16[48,1536]{1,0:T(8,128)(2,1)S(1)}, bf16[48,1536]{1,0:T(8,128)(2,1)S(1)}, u32[]{:S(2)}, u32[]{:S(2)}) collective-permute-start(bf16[48,1536]{1,0:T(8,128)(2,1)S(1)} %maximum_select_fusion.1), channel_id=1, source_target_pairs={{0,8},{1,9},{2,10},{3,11},{4,12},{5,13},{6,14},{7,15},{8,0},{9,1},... | collective-permute-start | bytes 442376 | tf_op jit(solution)/shard_map/ppermute | solution.py:637
  52.9 23.9 %collective-permute-start.20 = (bf16[4,48,1920]{2,1,0:T(8,128)(2,1)S(1)}, bf16[4,48,1920]{2,1,0:T(8,128)(2,1)S(1)}, u32[]{:S(2)}, u32[]{:S(2)}) collective-permute-start(bf16[4,48,1920]{2,1,0:T(8,128)(2,1)S(1)} %pad_maximum_fusion.refs_5_.refs_6_), channel_id=1, source_target_pairs={{0,4},{1,5},{2,6},{3,7},{4,0},{5,1},{6,2},{7,3},{8,12},{9,13},{10,... | collective-permute-start | bytes 2211848 | tf_op jit(solution)/shard_map/ppermute | solution.py:637
  53.4 32.3 %collective-permute-start.22 = (bf16[4,48,1920]{2,1,0:T(8,128)(2,1)S(1)}, bf16[4,48,1920]{2,1,0:T(8,128)(2,1)S(1)}, u32[]{:S(2)}, u32[]{:S(2)}) collective-permute-start(bf16[4,48,1920]{2,1,0:T(8,128)(2,1)S(1)} %pad_maximum_fusion.refs_5_.refs_6_), channel_id=1, source_target_pairs={{0,2},{1,3},{2,0},{3,1},{4,6},{5,7},{6,4},{7,5},{8,10},{9,11},{10,... | collective-permute-start | bytes 2211848 | tf_op jit(solution)/shard_map/ppermute | solution.py:637
  55.4 32.0 %collective-permute-start.24 = (bf16[4,48,1920]{2,1,0:T(8,128)(2,1)S(1)}, bf16[4,48,1920]{2,1,0:T(8,128)(2,1)}, u32[]{:S(2)}, u32[]{:S(2)}) collective-permute-start(bf16[4,48,1920]{2,1,0:T(8,128)(2,1)S(1)} %pad_maximum_fusion.refs_5_.refs_6_), channel_id=1, source_target_pairs={{0,6},{1,7},{2,4},{3,5},{4,2},{5,3},{6,0},{7,1},{8,14},{9,15},{10,... | collective-permute-start | bytes 2211848 | tf_op jit(solution)/shard_map/ppermute | solution.py:637
  76.7 10.7 %collective-permute-start.19 = (bf16[4,48,1920]{2,1,0:T(8,128)(2,1)S(1)}, bf16[4,48,1920]{2,1,0:T(8,128)(2,1)S(1)}, u32[]{:S(2)}, u32[]{:S(2)}) collective-permute-start(bf16[4,48,1920]{2,1,0:T(8,128)(2,1)S(1)} %pad_maximum_fusion.refs_5_.refs_6_), channel_id=1, source_target_pairs={{0,1},{1,0},{2,3},{3,2},{4,5},{5,4},{6,7},{7,6},{8,9},{9,8},{10,11... | collective-permute-start | bytes 2211848 | tf_op jit(solution)/shard_map/ppermute | solution.py:637
  76.8 10.6 %collective-permute-start.21 = (bf16[4,48,1920]{2,1,0:T(8,128)(2,1)S(1)}, bf16[4,48,1920]{2,1,0:T(8,128)(2,1)S(1)}, u32[]{:S(2)}, u32[]{:S(2)}) collective-permute-start(bf16[4,48,1920]{2,1,0:T(8,128)(2,1)S(1)} %collective-permute-done.20.refs_6_.refs_7_), channel_id=1, source_target_pairs={{0,1},{1,0},{2,3},{3,2},{4,5},{5,4},{6,7},{7,6},{8,9},{9,8},{10,11... | collective-permute-start | bytes 2211848 | tf_op jit(solution)/shard_map/ppermute | solution.py:637
  89.8 31.7 %collective-permute-start.26 = (bf16[4,48,1536]{2,1,0:T(8,128)(2,1)S(1)}, bf16[4,48,1536]{2,1,0:T(8,128)(2,1)S(1)}, u32[]{:S(2)}, u32[]{:S(2)}) collective-permute-start(bf16[4,48,1536]{2,1,0:T(8,128)(2,1)S(1)} %pad_maximum_fusion.1.refs_14_), channel_id=1, source_target_pairs={{0,4},{1,5},{2,6},{3,7},{4,0},{5,1},{6,2},{7,3},{8,12},{9,13},{10,... | collective-permute-start | bytes 1769480 | tf_op jit(solution)/shard_map/ppermute | solution.py:637
  91.6 30.4 %collective-permute-start.27 = (bf16[4,48,1536]{2,1,0:T(8,128)(2,1)S(1)}, bf16[4,48,1536]{2,1,0:T(8,128)(2,1)}, u32[]{:S(2)}, u32[]{:S(2)}) collective-permute-start(bf16[4,48,1536]{2,1,0:T(8,128)(2,1)S(1)} %pad_maximum_fusion.1.refs_14_), channel_id=1, source_target_pairs={{0,2},{1,3},{2,0},{3,1},{4,6},{5,7},{6,4},{7,5},{8,10},{9,11},{10,... | collective-permute-start | bytes 1769480 | tf_op jit(solution)/shard_map/ppermute | solution.py:637
  93.1 29.0 %collective-permute-start.28 = (bf16[4,48,1536]{2,1,0:T(8,128)(2,1)S(1)}, bf16[4,48,1536]{2,1,0:T(8,128)(2,1)}, u32[]{:S(2)}, u32[]{:S(2)}) collective-permute-start(bf16[4,48,1536]{2,1,0:T(8,128)(2,1)S(1)} %pad_maximum_fusion.1.refs_14_), channel_id=1, source_target_pairs={{0,6},{1,7},{2,4},{3,5},{4,2},{5,3},{6,0},{7,1},{8,14},{9,15},{10,... | collective-permute-start | bytes 1769480 | tf_op jit(solution)/shard_map/ppermute | solution.py:637
  170.0 27.9 %collective-permute-start.33 = (bf16[4,4,48,768]{3,2,1,0:T(8,128)(2,1)}, bf16[4,4,48,768]{3,2,1,0:T(8,128)(2,1)S(1)}, u32[]{:S(2)}, u32[]{:S(2)}) collective-permute-start(bf16[4,4,48,768]{3,2,1,0:T(8,128)(2,1)} %get-tuple-element.143), channel_id=1, source_target_pairs={{0,1},{1,0},{2,3},{3,2},{4,5},{5,4},{6,7},{7,6},{8,9},{9,8},{10,11... | collective-permute-start | bytes 3538952 | tf_op jit(solution)/shard_map/ppermute | solution.py:637
  199.2 37.1 %collective-permute-start.35 = (bf16[4,48,768]{2,1,0:T(8,128)(2,1)}, bf16[4,48,768]{2,1,0:T(8,128)(2,1)S(1)}, u32[]{:S(2)}, u32[]{:S(2)}) collective-permute-start(bf16[4,48,768]{2,1,0:T(8,128)(2,1)} %get-tuple-element.271), channel_id=1, source_target_pairs={{0,4},{1,5},{2,6},{3,7},{4,0},{5,1},{6,2},{7,3},{8,12},{9,13},{10,... | collective-permute-start | bytes 884744 | tf_op jit(solution)/shard_map/ppermute | solution.py:637
  201.0 35.3 %collective-permute-start.36 = (bf16[4,48,768]{2,1,0:T(8,128)(2,1)}, bf16[4,48,768]{2,1,0:T(8,128)(2,1)S(1)}, u32[]{:S(2)}, u32[]{:S(2)}) collective-permute-start(bf16[4,48,768]{2,1,0:T(8,128)(2,1)} %get-tuple-element.270), channel_id=1, source_target_pairs={{0,2},{1,3},{2,0},{3,1},{4,6},{5,7},{6,4},{7,5},{8,10},{9,11},{10,... | collective-permute-start | bytes 884744 | tf_op jit(solution)/shard_map/ppermute | solution.py:637
  202.5 33.8 %collective-permute-start.37 = (bf16[4,48,768]{2,1,0:T(8,128)(2,1)}, bf16[4,48,768]{2,1,0:T(8,128)(2,1)}, u32[]{:S(2)}, u32[]{:S(2)}) collective-permute-start(bf16[4,48,768]{2,1,0:T(8,128)(2,1)} %get-tuple-element.269), channel_id=1, source_target_pairs={{0,6},{1,7},{2,4},{3,5},{4,2},{5,3},{6,0},{7,1},{8,14},{9,15},{10,... | collective-permute-start | bytes 884744 | tf_op jit(solution)/shard_map/ppermute | solution.py:637
  215.1 28.8 %collective-permute-start.34 = (bf16[4,4,48,768]{3,2,1,0:T(8,128)(2,1)}, bf16[4,4,48,768]{3,2,1,0:T(8,128)(2,1)S(1)}, u32[]{:S(2)}, u32[]{:S(2)}) collective-permute-start(bf16[4,4,48,768]{3,2,1,0:T(8,128)(2,1)} %get-tuple-element.155), channel_id=1, source_target_pairs={{0,1},{1,0},{2,3},{3,2},{4,5},{5,4},{6,7},{7,6},{8,9},{9,8},{10,11... | collective-permute-start | bytes 3538952 | tf_op jit(solution)/shard_map/ppermute | solution.py:637
  239.8 24.8 %collective-permute-start.42 = (bf16[48,768]{1,0:T(8,128)(2,1)}, bf16[48,768]{1,0:T(8,128)(2,1)}, u32[]{:S(2)}, u32[]{:S(2)}) collective-permute-start(bf16[48,768]{1,0:T(8,128)(2,1)} %get-tuple-element.289), channel_id=1, source_target_pairs={{0,16},{1,17},{2,18},{3,19},{4,20},{5,21},{6,22},{7,23},{8,24},{9,... | collective-permute-start | bytes 221192 | tf_op jit(solution)/shard_map/ppermute | solution.py:637
  242.5 22.2 %collective-permute-start.43 = (bf16[48,768]{1,0:T(8,128)(2,1)}, bf16[48,768]{1,0:T(8,128)(2,1)}, u32[]{:S(2)}, u32[]{:S(2)}) collective-permute-start(bf16[48,768]{1,0:T(8,128)(2,1)} %get-tuple-element.288), channel_id=1, source_target_pairs={{0,24},{1,25},{2,26},{3,27},{4,28},{5,29},{6,30},{7,31},{8,16},{9,... | collective-permute-start | bytes 221192 | tf_op jit(solution)/shard_map/ppermute | solution.py:637
  245.1 19.5 %collective-permute-start.38 = (bf16[4,48,768]{2,1,0:T(8,128)(2,1)}, bf16[4,48,768]{2,1,0:T(8,128)(2,1)S(1)}, u32[]{:S(2)}, u32[]{:S(2)}) collective-permute-start(bf16[4,48,768]{2,1,0:T(8,128)(2,1)} %get-tuple-element.268), channel_id=1, source_target_pairs={{0,4},{1,5},{2,6},{3,7},{4,0},{5,1},{6,2},{7,3},{8,12},{9,13},{10,... | collective-permute-start | bytes 884744 | tf_op jit(solution)/shard_map/ppermute | solution.py:637
  246.9 17.8 %collective-permute-start.39 = (bf16[4,48,768]{2,1,0:T(8,128)(2,1)}, bf16[4,48,768]{2,1,0:T(8,128)(2,1)S(1)}, u32[]{:S(2)}, u32[]{:S(2)}) collective-permute-start(bf16[4,48,768]{2,1,0:T(8,128)(2,1)} %get-tuple-element.267), channel_id=1, source_target_pairs={{0,2},{1,3},{2,0},{3,1},{4,6},{5,7},{6,4},{7,5},{8,10},{9,11},{10,... | collective-permute-start | bytes 884744 | tf_op jit(solution)/shard_map/ppermute | solution.py:637
  248.4 16.3 %collective-permute-start.40 = (bf16[4,48,768]{2,1,0:T(8,128)(2,1)}, bf16[4,48,768]{2,1,0:T(8,128)(2,1)S(1)}, u32[]{:S(2)}, u32[]{:S(2)}) collective-permute-start(bf16[4,48,768]{2,1,0:T(8,128)(2,1)} %get-tuple-element.266), channel_id=1, source_target_pairs={{0,6},{1,7},{2,4},{3,5},{4,2},{5,3},{6,0},{7,1},{8,14},{9,15},{10,... | collective-permute-start | bytes 884744 | tf_op jit(solution)/shard_map/ppermute | solution.py:637
  267.4 44.9 %collective-permute-start.48 = (bf16[48,768]{1,0:T(8,128)(2,1)}, bf16[48,768]{1,0:T(8,128)(2,1)}, u32[]{:S(2)}, u32[]{:S(2)}) collective-permute-start(bf16[48,768]{1,0:T(8,128)(2,1)} %get-tuple-element.287), channel_id=1, source_target_pairs={{0,8},{1,9},{2,10},{3,11},{4,12},{5,13},{6,14},{7,15},{8,0},{9,1},... | collective-permute-start | bytes 221192 | tf_op jit(solution)/shard_map/ppermute | solution.py:637
  267.4 44.9 %collective-permute-start.49 = (bf16[48,768]{1,0:T(8,128)(2,1)}, bf16[48,768]{1,0:T(8,128)(2,1)}, u32[]{:S(2)}, u32[]{:S(2)}) collective-permute-start(bf16[48,768]{1,0:T(8,128)(2,1)} %get-tuple-element.286), channel_id=1, source_target_pairs={{0,16},{1,17},{2,18},{3,19},{4,20},{5,21},{6,22},{7,23},{8,24},{9,... | collective-permute-start | bytes 221192 | tf_op jit(solution)/shard_map/ppermute | solution.py:637
  270.7 37.8 %collective-permute-start.45 = (bf16[4,48,768]{2,1,0:T(8,128)(2,1)S(1)}, bf16[4,48,768]{2,1,0:T(8,128)(2,1)S(1)}, u32[]{:S(2)}, u32[]{:S(2)}) collective-permute-start(bf16[4,48,768]{2,1,0:T(8,128)(2,1)S(1)} %get-tuple-element.265), channel_id=1, source_target_pairs={{0,4},{1,5},{2,6},{3,7},{4,0},{5,1},{6,2},{7,3},{8,12},{9,13},{10,... | collective-permute-start | bytes 884744 | tf_op jit(solution)/shard_map/ppermute | solution.py:637
  272.5 38.5 %collective-permute-start.46 = (bf16[4,48,768]{2,1,0:T(8,128)(2,1)S(1)}, bf16[4,48,768]{2,1,0:T(8,128)(2,1)S(1)}, u32[]{:S(2)}, u32[]{:S(2)}) collective-permute-start(bf16[4,48,768]{2,1,0:T(8,128)(2,1)S(1)} %get-tuple-element.264), channel_id=1, source_target_pairs={{0,2},{1,3},{2,0},{3,1},{4,6},{5,7},{6,4},{7,5},{8,10},{9,11},{10,... | collective-permute-start | bytes 884744 | tf_op jit(solution)/shard_map/ppermute | solution.py:637
  274.0 37.0 %collective-permute-start.47 = (bf16[4,48,768]{2,1,0:T(8,128)(2,1)S(1)}, bf16[4,48,768]{2,1,0:T(8,128)(2,1)S(1)}, u32[]{:S(2)}, u32[]{:S(2)}) collective-permute-start(bf16[4,48,768]{2,1,0:T(8,128)(2,1)S(1)} %get-tuple-element.263), channel_id=1, source_target_pairs={{0,6},{1,7},{2,4},{3,5},{4,2},{5,3},{6,0},{7,1},{8,14},{9,15},{10,... | collective-permute-start | bytes 884744 | tf_op jit(solution)/shard_map/ppermute | solution.py:637
  314.9 12.5 %collective-permute-start.55 = (bf16[48,768]{1,0:T(8,128)(2,1)S(1)}, bf16[48,768]{1,0:T(8,128)(2,1)S(1)}, u32[]{:S(2)}, u32[]{:S(2)}) collective-permute-start(bf16[48,768]{1,0:T(8,128)(2,1)S(1)} %get-tuple-element.284), channel_id=1, source_target_pairs={{0,8},{1,9},{2,10},{3,11},{4,12},{5,13},{6,14},{7,15},{8,0},{9,1},... | collective-permute-start | bytes 221192 | tf_op jit(solution)/shard_map/ppermute | solution.py:637
  315.0 32.3 %collective-permute-start.56 = (bf16[48,768]{1,0:T(8,128)(2,1)S(1)}, bf16[48,768]{1,0:T(8,128)(2,1)S(1)}, u32[]{:S(2)}, u32[]{:S(2)}) collective-permute-start(bf16[48,768]{1,0:T(8,128)(2,1)S(1)} %get-tuple-element.283), channel_id=1, source_target_pairs={{0,16},{1,17},{2,18},{3,19},{4,20},{5,21},{6,22},{7,23},{8,24},{9,... | collective-permute-start | bytes 221192 | tf_op jit(solution)/shard_map/ppermute | solution.py:637
  318.0 29.3 %collective-permute-start.57 = (bf16[48,768]{1,0:T(8,128)(2,1)S(1)}, bf16[48,768]{1,0:T(8,128)(2,1)S(1)}, u32[]{:S(2)}, u32[]{:S(2)}) collective-permute-start(bf16[48,768]{1,0:T(8,128)(2,1)S(1)} %get-tuple-element.282), channel_id=1, source_target_pairs={{0,24},{1,25},{2,26},{3,27},{4,28},{5,29},{6,30},{7,31},{8,16},{9,... | collective-permute-start | bytes 221192 | tf_op jit(solution)/shard_map/ppermute | solution.py:637
  324.1 23.3 %collective-permute-start.52 = (bf16[4,48,1664]{2,1,0:T(8,128)(2,1)}, bf16[4,48,1664]{2,1,0:T(8,128)(2,1)S(1)}, u32[]{:S(2)}, u32[]{:S(2)}) collective-permute-start(bf16[4,48,1664]{2,1,0:T(8,128)(2,1)} %get-tuple-element.259), channel_id=1, source_target_pairs={{0,4},{1,5},{2,6},{3,7},{4,0},{5,1},{6,2},{7,3},{8,12},{9,13},{10,... | collective-permute-start | bytes 1916936 | tf_op jit(solution)/shard_map/ppermute | solution.py:637
  325.8 30.0 %collective-permute-start.53 = (bf16[4,48,1664]{2,1,0:T(8,128)(2,1)}, bf16[4,48,1664]{2,1,0:T(8,128)(2,1)S(1)}, u32[]{:S(2)}, u32[]{:S(2)}) collective-permute-start(bf16[4,48,1664]{2,1,0:T(8,128)(2,1)} %get-tuple-element.258), channel_id=1, source_target_pairs={{0,2},{1,3},{2,0},{3,1},{4,6},{5,7},{6,4},{7,5},{8,10},{9,11},{10,... | collective-permute-start | bytes 1916936 | tf_op jit(solution)/shard_map/ppermute | solution.py:637
  327.4 28.5 %collective-permute-start.54 = (bf16[4,48,1664]{2,1,0:T(8,128)(2,1)S(1)}, bf16[4,48,1664]{2,1,0:T(8,128)(2,1)}, u32[]{:S(2)}, u32[]{:S(2)}) collective-permute-start(bf16[4,48,1664]{2,1,0:T(8,128)(2,1)S(1)} %get-tuple-element.257), channel_id=1, source_target_pairs={{0,6},{1,7},{2,4},{3,5},{4,2},{5,3},{6,0},{7,1},{8,14},{9,15},{10,... | collective-permute-start | bytes 1916936 | tf_op jit(solution)/shard_map/ppermute | solution.py:637
  359.3 9.7 %collective-permute-start.58 = (bf16[48,1664]{1,0:T(8,128)(2,1)S(1)}, bf16[48,1664]{1,0:T(8,128)(2,1)}, u32[]{:S(2)}, u32[]{:S(2)}) collective-permute-start(bf16[48,1664]{1,0:T(8,128)(2,1)S(1)} %get-tuple-element.274), channel_id=1, source_target_pairs={{0,8},{1,9},{2,10},{3,11},{4,12},{5,13},{6,14},{7,15},{8,0},{9,1},... | collective-permute-start | bytes 479240 | tf_op jit(solution)/shard_map/ppermute | solution.py:637
  359.3 14.9 %collective-permute-start.59 = (bf16[48,1664]{1,0:T(8,128)(2,1)S(1)}, bf16[48,1664]{1,0:T(8,128)(2,1)}, u32[]{:S(2)}, u32[]{:S(2)}) collective-permute-start(bf16[48,1664]{1,0:T(8,128)(2,1)S(1)} %get-tuple-element.273), channel_id=1, source_target_pairs={{0,16},{1,17},{2,18},{3,19},{4,20},{5,21},{6,22},{7,23},{8,24},{9,... | collective-permute-start | bytes 479240 | tf_op jit(solution)/shard_map/ppermute | solution.py:637
  362.4 11.9 %collective-permute-start.60 = (bf16[48,1664]{1,0:T(8,128)(2,1)S(1)}, bf16[48,1664]{1,0:T(8,128)(2,1)}, u32[]{:S(2)}, u32[]{:S(2)}) collective-permute-start(bf16[48,1664]{1,0:T(8,128)(2,1)S(1)} %get-tuple-element.272), channel_id=1, source_target_pairs={{0,24},{1,25},{2,26},{3,27},{4,28},{5,29},{6,30},{7,31},{8,16},{9,... | collective-permute-start | bytes 479240 | tf_op jit(solution)/shard_map/ppermute | solution.py:637
  365.7 15.6 %collective-permute-start.63 = (bf16[4,48,768]{2,1,0:T(8,128)(2,1)S(1)}, bf16[4,48,768]{2,1,0:T(8,128)(2,1)S(1)}, u32[]{:S(2)}, u32[]{:S(2)}) collective-permute-start(bf16[4,48,768]{2,1,0:T(8,128)(2,1)S(1)} %get-tuple-element.262), channel_id=1, source_target_pairs={{0,4},{1,5},{2,6},{3,7},{4,0},{5,1},{6,2},{7,3},{8,12},{9,13},{10,... | collective-permute-start | bytes 884744 | tf_op jit(solution)/shard_map/ppermute | solution.py:637
  366.3 15.0 %collective-permute-start.64 = (bf16[4,48,768]{2,1,0:T(8,128)(2,1)S(1)}, bf16[4,48,768]{2,1,0:T(8,128)(2,1)S(1)}, u32[]{:S(2)}, u32[]{:S(2)}) collective-permute-start(bf16[4,48,768]{2,1,0:T(8,128)(2,1)S(1)} %get-tuple-element.261), channel_id=1, source_target_pairs={{0,2},{1,3},{2,0},{3,1},{4,6},{5,7},{6,4},{7,5},{8,10},{9,11},{10,... | collective-permute-start | bytes 884744 | tf_op jit(solution)/shard_map/ppermute | solution.py:637
  369.0 12.6 %collective-permute-start.65 = (bf16[4,48,768]{2,1,0:T(8,128)(2,1)S(1)}, bf16[4,48,768]{2,1,0:T(8,128)(2,1)S(1)}, u32[]{:S(2)}, u32[]{:S(2)}) collective-permute-start(bf16[4,48,768]{2,1,0:T(8,128)(2,1)S(1)} %get-tuple-element.260), channel_id=1, source_target_pairs={{0,6},{1,7},{2,4},{3,5},{4,2},{5,3},{6,0},{7,1},{8,14},{9,15},{10,... | collective-permute-start | bytes 884744 | tf_op jit(solution)/shard_map/ppermute | solution.py:637
  (81 other events, 583.8 us)
